TPU v7x, 128 devices: a whole 4x4x4 slice. The times are simulated.
128 devices in a mesh: expert: 16 (over y, z), fsdp: 8 (over x, core).
Axes of the slice: x: 4, y: 4, z: 4, core: 2. Of those that a mesh axis runs over, the one named last changes fastest.
Arguments:
- layer_input: bfloat16 [16, 1024, 1024], P('expert', 'fsdp'), may hold values from -6 to 6
- segment_ids: int32 [16, 1024], P('expert'), may hold values from 0 to 3, as said below
- routes: int32 [16, 1024, 8], P('expert', 'fsdp'), may hold values from 0 to 31, all different within a row; in each aligned block of 128 rows (0 to 127, 128 to 255, ..., all dimensions but the last counted through in order) at most 64 rows name the same one
- attn_gain: bfloat16 [1024], P('fsdp'), may hold values from 0.099609375 to 1.8984375
- w_query: bfloat16 [1024, 1024], P('fsdp'), may hold values from -0.25 to 0.25
- w_key: bfloat16 [1024, 512], P('fsdp'), may hold values from -0.25 to 0.25
- w_value: bfloat16 [1024, 512], P('fsdp'), may hold values from -0.1875 to 0.1875
- w_output: bfloat16 [1024, 1024], P('fsdp'), may hold values from -1.5 to 1.5
- w_router: bfloat16 [1024, 32], P('fsdp'), may hold values from -0.09375 to 0.09375
- ffn_gain: bfloat16 [1024], P('fsdp'), may hold values from 0.099609375 to 1.8984375
- w_gate: bfloat16 [32, 1024, 512], P('expert', 'fsdp'), may hold values from -0.1875 to 0.1875
- w_up: bfloat16 [32, 1024, 512], P('expert', 'fsdp'), may hold values from -0.1875 to 0.1875
- w_down: bfloat16 [32, 512, 1024], P('expert', None, 'fsdp'), may hold values from -0.75 to 0.75
- cotangent: bfloat16 [16, 1024, 1024], P('expert', 'fsdp'), may hold values from -6 to 6
Outputs:
- layer_output: bfloat16 [16, 1024, 1024], P('expert', 'fsdp')
- grad_input: bfloat16 [16, 1024, 1024], P('expert', 'fsdp')
- grad_attn_gain: float32 [1024], P('fsdp')
- grad_query: float32 [1024, 1024], P('fsdp')
- grad_key: float32 [1024, 512], P('fsdp')
- grad_value: float32 [1024, 512], P('fsdp')
- grad_output_proj: float32 [1024, 1024], P('fsdp')
- grad_router: float32 [1024, 32], P('fsdp')
- grad_ffn_gain: float32 [1024], P('fsdp')
- grad_gate: float32 [32, 1024, 512], P('expert', 'fsdp')
- grad_up: float32 [32, 1024, 512], P('expert', 'fsdp')
- grad_down: float32 [32, 512, 1024], P('expert', None, 'fsdp')
Inputs may be any that keep to these rules, and one draw needn't show every extreme that they name: `routes`: A token's 8 experts differ. In each aligned block of 128 tokens (one device's piece of one sequence) no expert is chosen by more than 64 tokens, and in some blocks one expert is chosen by exactly 64. `segment_ids`: never fall along a sequence and start at 0. On each index of expert, one of its 1 sequence has a document that begins in the first 128 tokens and ends in the last 128.
All inputs are finite; a program needn't handle non-finite values.
Results may differ from a plain program's by a relative error of at most 0.025.
Values may be sent and summed in bfloat16 or wider, within the bound.
No kernel may reach another device: no remote copies, remote signals or barrier semaphores. Data moves between devices by JAX's collectives and lax.ppermute only.
A program may use at most 192 MiB of HBM per device.

v0:
```python
import jax
import jax.numpy as jnp
from jax import lax
from jax.sharding import PartitionSpec as P

HEADS = 16
KV_HEADS = 8
HEAD_DIM = 64
TOP = 8
EXP_DEV = 2


epsilon = 1e-06
rope_base = 10000.0
highest = lax.Precision.HIGHEST


def rms_scale(values, gain_vec):
    return (
        values * lax.rsqrt(jnp.mean(values * values, axis=-1, keepdims=True) + epsilon) * gain_vec
    )


def rope_tables(positions, head_width):
    half_width = head_width // 2
    exponent = jnp.arange(half_width).astype(jnp.float32) * (2.0 / head_width)
    inverse = rope_base ** (-exponent)
    angles = positions.astype(jnp.float32)[:, None] * inverse[None, :]
    return (jnp.cos(angles), jnp.sin(angles))


def rotate(vectors, cosine_tab, sine_tab):
    half_width = vectors.shape[-1] // 2
    first_half = vectors[..., :half_width]
    second_half = vectors[..., half_width:]
    cosine_b = cosine_tab[:, None, :]
    sine_b = sine_tab[:, None, :]
    return jnp.concatenate(
        [
            first_half * cosine_b - second_half * sine_b,
            second_half * cosine_b + first_half * sine_b,
        ],
        axis=-1,
    )


def unrotate(grads_in, cosine_tab, sine_tab):
    half_width = grads_in.shape[-1] // 2
    first_half = grads_in[..., :half_width]
    second_half = grads_in[..., half_width:]
    cosine_b = cosine_tab[:, None, :]
    sine_b = sine_tab[:, None, :]
    return jnp.concatenate(
        [
            first_half * cosine_b + second_half * sine_b,
            second_half * cosine_b - first_half * sine_b,
        ],
        axis=-1,
    )


def local(
    layer_input,
    segment_ids,
    routes,
    attn_gain,
    w_query,
    w_key,
    w_value,
    w_output,
    w_router,
    ffn_gain,
    w_gate,
    w_up,
    w_down,
    cotangent,
):
    seq_count, piece_len, model_dim = layer_input.shape
    tok_rows = seq_count * piece_len
    owners = lax.axis_size("expert")
    experts = EXP_DEV * owners
    per_piece = 2 * piece_len * TOP // experts
    slot_count = seq_count * per_piece
    seq_length = piece_len * lax.axis_size("fsdp")
    groups = HEADS // KV_HEADS
    score_scale = HEAD_DIM ** (-0.5)
    key_width = KV_HEADS * HEAD_DIM
    query_width = HEADS * HEAD_DIM
    assign_count = tok_rows * TOP
    gain_one, query_mat, key_mat, value_mat, output_mat, router_mat, gain_two = (
        lax.all_gather(attn_gain, "fsdp", axis=0, tiled=True),
        lax.all_gather(w_query, "fsdp", axis=0, tiled=True),
        lax.all_gather(w_key, "fsdp", axis=0, tiled=True),
        lax.all_gather(w_value, "fsdp", axis=0, tiled=True),
        lax.all_gather(w_output, "fsdp", axis=0, tiled=True),
        lax.all_gather(w_router, "fsdp", axis=0, tiled=True),
        lax.all_gather(ffn_gain, "fsdp", axis=0, tiled=True),
    )
    gain_first = gain_one.astype(jnp.float32)
    gain_second = gain_two.astype(jnp.float32)
    input_full = layer_input.astype(jnp.float32)
    normed_full, norm_pull_one = jax.vjp(rms_scale, input_full, gain_first)
    normed = normed_full.astype(jnp.bfloat16)
    q_raw = jnp.dot(normed, query_mat, preferred_element_type=jnp.float32)
    k_raw = jnp.dot(normed, key_mat, preferred_element_type=jnp.float32)
    v_raw = jnp.dot(normed, value_mat, preferred_element_type=jnp.float32)
    first_row = lax.axis_index("fsdp") * piece_len
    query_pos = first_row + jnp.arange(piece_len)
    key_pos = jnp.arange(seq_length)
    cosine_tab, sine_tab = rope_tables(query_pos, HEAD_DIM)
    query_rot = (
        rotate(q_raw.reshape(seq_count, piece_len, HEADS, HEAD_DIM), cosine_tab, sine_tab)
        .reshape(seq_count, piece_len, query_width)
        .astype(jnp.bfloat16)
    )
    key_rot = (
        rotate(k_raw.reshape(seq_count, piece_len, KV_HEADS, HEAD_DIM), cosine_tab, sine_tab)
        .reshape(seq_count, piece_len, key_width)
        .astype(jnp.bfloat16)
    )
    value_low = v_raw.astype(jnp.bfloat16)
    keys_all, values_all = (
        lax.all_gather(key_rot, "fsdp", axis=1, tiled=True),
        lax.all_gather(value_low, "fsdp", axis=1, tiled=True),
    )

    def scores_of(query_seq, keys_seq, seg_row):
        query_h = query_seq.reshape(piece_len, KV_HEADS, groups, HEAD_DIM)
        keys_h = keys_seq.reshape(seq_length, KV_HEADS, HEAD_DIM)
        raw_scores = (
            jnp.einsum("qhgd,khd->hgqk", query_h, keys_h, preferred_element_type=jnp.float32)
            * score_scale
        )
        seg_here = lax.dynamic_slice_in_dim(seg_row, first_row, piece_len, 0)
        allowed = (seg_here[:, None] == seg_row[None, :]) & (key_pos[None, :] <= query_pos[:, None])
        return jnp.where(allowed, raw_scores, -1e30)

    def attend(items_in):
        query_seq, keys_seq, values_seq, seg_row = items_in
        scores = scores_of(query_seq, keys_seq, seg_row)
        row_top = jnp.max(scores, axis=-1, keepdims=True)
        expo_vals = jnp.exp(scores - row_top)
        totals = jnp.sum(expo_vals, axis=-1, keepdims=True)
        probs_low = (expo_vals / totals).astype(jnp.bfloat16)
        values_h = values_seq.reshape(seq_length, KV_HEADS, HEAD_DIM)
        mixed_heads = jnp.einsum(
            "hgqk,khd->qhgd", probs_low, values_h, preferred_element_type=jnp.float32
        )
        log_total = row_top[..., 0] + jnp.log(totals[..., 0])
        return (mixed_heads.reshape(piece_len, query_width).astype(jnp.bfloat16), log_total)

    attended, log_totals = lax.map(attend, (query_rot, keys_all, values_all, segment_ids))
    after_attn = input_full + jnp.dot(attended, output_mat, preferred_element_type=jnp.float32)
    normed_two_full, norm_pull_two = jax.vjp(rms_scale, after_attn, gain_second)
    normed_two = normed_two_full.astype(jnp.bfloat16)
    logits = jnp.dot(normed_two, router_mat, preferred_element_type=jnp.float32)
    expert_ids = jnp.arange(experts, dtype=jnp.int32)
    choose_table = (routes[..., None] == expert_ids).astype(jnp.float32)
    chosen = jnp.einsum("spke,spe->spk", choose_table, logits, precision=highest)
    gate_soft = jax.nn.softmax(chosen, axis=-1)
    flat_routes = routes.reshape(seq_count, piece_len * TOP)
    hit_table = (flat_routes[..., None] == expert_ids).astype(jnp.int32)
    before_count = jnp.cumsum(hit_table, axis=1) - hit_table
    rank_own = jnp.sum(before_count * hit_table, axis=-1)
    seq_offset = (jnp.arange(seq_count, dtype=jnp.int32) * per_piece)[:, None]
    slot_index = (flat_routes * slot_count + seq_offset + rank_own).reshape(-1)
    owner_of_slot = (
        jnp.full((experts * slot_count,), assign_count, jnp.int32)
        .at[slot_index]
        .set(jnp.arange(assign_count, dtype=jnp.int32))
    )
    token_of_slot = owner_of_slot // TOP
    padded_rows = jnp.concatenate(
        [normed_two.reshape(tok_rows, model_dim), jnp.zeros((1, model_dim), jnp.bfloat16)], axis=0
    )
    send_rows = padded_rows[token_of_slot].reshape(owners, EXP_DEV, slot_count, model_dim)
    received = lax.all_to_all(send_rows, "expert", split_axis=0, concat_axis=0, tiled=True)
    gate_all, up_all, down_all = (
        lax.all_gather(w_gate, "fsdp", axis=1, tiled=True),
        lax.all_gather(w_up, "fsdp", axis=1, tiled=True),
        lax.all_gather(w_down, "fsdp", axis=2, tiled=True),
    )
    gate_val = jnp.einsum("oecd,edf->oecf", received, gate_all, preferred_element_type=jnp.float32)
    up_val = jnp.einsum("oecd,edf->oecf", received, up_all, preferred_element_type=jnp.float32)
    sigmoid_g = jax.nn.sigmoid(gate_val)
    activated = gate_val * sigmoid_g
    hidden = (activated * up_val).astype(jnp.bfloat16)
    result = jnp.einsum(
        "oecf,efd->oecd", hidden, down_all, preferred_element_type=jnp.float32
    ).astype(jnp.bfloat16)
    returned = lax.all_to_all(result, "expert", split_axis=0, concat_axis=0, tiled=True)
    picked = returned.reshape(experts * slot_count, model_dim)[slot_index].reshape(
        seq_count, piece_len, TOP, model_dim
    )
    mixed_out = after_attn
    for choice_k in range(TOP):
        mixed_out = mixed_out + gate_soft[:, :, choice_k, None] * picked[:, :, choice_k].astype(
            jnp.float32
        )
    layer_output = mixed_out.astype(jnp.bfloat16)
    grad_out = cotangent.astype(jnp.float32)
    dgate = jnp.stack(
        [
            jnp.sum(grad_out * picked[:, :, choice_k].astype(jnp.float32), axis=-1)
            for choice_k in range(TOP)
        ],
        axis=-1,
    )
    dchosen = gate_soft * (dgate - jnp.sum(gate_soft * dgate, axis=-1, keepdims=True))
    dlogits = jnp.einsum("spk,spke->spe", dchosen, choose_table, precision=highest)
    dresult = (
        (gate_soft[..., None] * grad_out[:, :, None, :])
        .astype(jnp.bfloat16)
        .reshape(assign_count, model_dim)
    )
    padded_grads = jnp.concatenate([dresult, jnp.zeros((1, model_dim), jnp.bfloat16)], axis=0)
    dresult_send = padded_grads[owner_of_slot].reshape(owners, EXP_DEV, slot_count, model_dim)
    dresult_recv = lax.all_to_all(dresult_send, "expert", split_axis=0, concat_axis=0, tiled=True)
    gate_back, up_back, down_back = (
        lax.all_gather(w_gate, "fsdp", axis=1, tiled=True),
        lax.all_gather(w_up, "fsdp", axis=1, tiled=True),
        lax.all_gather(w_down, "fsdp", axis=2, tiled=True),
    )
    dhidden = jnp.einsum(
        "oecd,efd->oecf", dresult_recv, down_back, preferred_element_type=jnp.float32
    )
    grad_down_part = jnp.einsum(
        "oecf,oecd->efd", hidden, dresult_recv, preferred_element_type=jnp.float32
    )
    dgate_val = (dhidden * up_val * sigmoid_g * (1.0 + gate_val * (1.0 - sigmoid_g))).astype(
        jnp.bfloat16
    )
    dup_val = (dhidden * activated).astype(jnp.bfloat16)
    grad_gate_part = jnp.einsum(
        "oecd,oecf->edf", received, dgate_val, preferred_element_type=jnp.float32
    )
    grad_up_part = jnp.einsum(
        "oecd,oecf->edf", received, dup_val, preferred_element_type=jnp.float32
    )
    dassign = (
        jnp.einsum("oecf,edf->oecd", dgate_val, gate_back, preferred_element_type=jnp.float32)
        + jnp.einsum("oecf,edf->oecd", dup_val, up_back, preferred_element_type=jnp.float32)
    ).astype(jnp.bfloat16)
    dassign_back = lax.all_to_all(dassign, "expert", split_axis=0, concat_axis=0, tiled=True)
    grad_gate, grad_up, grad_down = (
        lax.psum_scatter(
            grad_gate_part.astype(jnp.bfloat16), "fsdp", scatter_dimension=1, tiled=True
        ).astype(jnp.float32),
        lax.psum_scatter(
            grad_up_part.astype(jnp.bfloat16), "fsdp", scatter_dimension=1, tiled=True
        ).astype(jnp.float32),
        lax.psum_scatter(
            grad_down_part.astype(jnp.bfloat16), "fsdp", scatter_dimension=2, tiled=True
        ).astype(jnp.float32),
    )
    dassign_rows = dassign_back.reshape(experts * slot_count, model_dim)[slot_index].reshape(
        seq_count, piece_len, TOP, model_dim
    )
    dnormed_two = jnp.einsum(
        "spe,de->spd", dlogits, router_mat.astype(jnp.float32), precision=highest
    )
    for choice_k in range(TOP):
        dnormed_two = dnormed_two + dassign_rows[:, :, choice_k].astype(jnp.float32)
    dafter_norm, grad_gain_two = norm_pull_two(dnormed_two)
    dafter = grad_out + dafter_norm
    dbranch = dafter.astype(jnp.bfloat16)
    dattended = jnp.einsum(
        "spd,id->spi", dbranch, output_mat, preferred_element_type=jnp.float32
    ).astype(jnp.bfloat16)

    def attend_back(items_in):
        query_seq, keys_seq, values_seq, seg_row, log_total, dmixed = items_in
        scores = scores_of(query_seq, keys_seq, seg_row)
        probs_full = jnp.exp(scores - log_total[..., None])
        probs_low = probs_full.astype(jnp.bfloat16)
        dmixed_h = dmixed.reshape(piece_len, KV_HEADS, groups, HEAD_DIM)
        values_h = values_seq.reshape(seq_length, KV_HEADS, HEAD_DIM)
        keys_h = keys_seq.reshape(seq_length, KV_HEADS, HEAD_DIM)
        query_h = query_seq.reshape(piece_len, KV_HEADS, groups, HEAD_DIM)
        dvalues = jnp.einsum(
            "hgqk,qhgd->khd", probs_low, dmixed_h, preferred_element_type=jnp.float32
        )
        dprobs = jnp.einsum(
            "qhgd,khd->hgqk", dmixed_h, values_h, preferred_element_type=jnp.float32
        )
        delta_row = jnp.sum(probs_full * dprobs, axis=-1, keepdims=True)
        dscores = (probs_full * (dprobs - delta_row)).astype(jnp.bfloat16)
        dquery = (
            jnp.einsum("hgqk,khd->qhgd", dscores, keys_h, preferred_element_type=jnp.float32)
            * score_scale
        )
        dkeys_part = (
            jnp.einsum("hgqk,qhgd->khd", dscores, query_h, preferred_element_type=jnp.float32)
            * score_scale
        )
        return (
            dquery.reshape(piece_len, HEADS, HEAD_DIM),
            dkeys_part.reshape(seq_length, key_width),
            dvalues.reshape(seq_length, key_width),
        )

    dquery_rot, dkeys_full, dvalues_full = lax.map(
        attend_back, (query_rot, keys_all, values_all, segment_ids, log_totals, dattended)
    )
    dkey_rot, dvalue = (
        lax.psum_scatter(
            dkeys_full.astype(jnp.bfloat16), "fsdp", scatter_dimension=1, tiled=True
        ).astype(jnp.float32),
        lax.psum_scatter(
            dvalues_full.astype(jnp.bfloat16), "fsdp", scatter_dimension=1, tiled=True
        ).astype(jnp.float32),
    )
    dq_low = (
        unrotate(dquery_rot, cosine_tab, sine_tab)
        .reshape(seq_count, piece_len, query_width)
        .astype(jnp.bfloat16)
    )
    dk_low = (
        unrotate(dkey_rot.reshape(seq_count, piece_len, KV_HEADS, HEAD_DIM), cosine_tab, sine_tab)
        .reshape(seq_count, piece_len, key_width)
        .astype(jnp.bfloat16)
    )
    dv_low = dvalue.astype(jnp.bfloat16)
    dnormed = jnp.einsum("spi,di->spd", dq_low, query_mat, preferred_element_type=jnp.float32)
    dnormed = dnormed + jnp.einsum(
        "spi,di->spd", dk_low, key_mat, preferred_element_type=jnp.float32
    )
    dnormed = dnormed + jnp.einsum(
        "spi,di->spd", dv_low, value_mat, preferred_element_type=jnp.float32
    )
    dinput_norm, grad_gain_one = norm_pull_one(dnormed)
    grad_input = (dafter + dinput_norm).astype(jnp.bfloat16)
    grad_router_full = jnp.einsum(
        "spd,spe->de", normed_two.astype(jnp.float32), dlogits, precision=highest
    )
    grad_output_full = jnp.einsum(
        "spi,spd->id", attended, dbranch, preferred_element_type=jnp.float32
    )
    grad_query_full = jnp.einsum("spd,spi->di", normed, dq_low, preferred_element_type=jnp.float32)
    grad_key_full = jnp.einsum("spd,spi->di", normed, dk_low, preferred_element_type=jnp.float32)
    grad_value_full = jnp.einsum("spd,spi->di", normed, dv_low, preferred_element_type=jnp.float32)
    part_gain_one, part_query, part_key, part_value, part_output, part_router, part_gain_two = (
        lax.psum_scatter(
            grad_gain_one.astype(jnp.bfloat16), "fsdp", scatter_dimension=0, tiled=True
        ).astype(jnp.float32),
        lax.psum_scatter(
            grad_query_full.astype(jnp.bfloat16), "fsdp", scatter_dimension=0, tiled=True
        ).astype(jnp.float32),
        lax.psum_scatter(
            grad_key_full.astype(jnp.bfloat16), "fsdp", scatter_dimension=0, tiled=True
        ).astype(jnp.float32),
        lax.psum_scatter(
            grad_value_full.astype(jnp.bfloat16), "fsdp", scatter_dimension=0, tiled=True
        ).astype(jnp.float32),
        lax.psum_scatter(
            grad_output_full.astype(jnp.bfloat16), "fsdp", scatter_dimension=0, tiled=True
        ).astype(jnp.float32),
        lax.psum_scatter(
            grad_router_full.astype(jnp.bfloat16), "fsdp", scatter_dimension=0, tiled=True
        ).astype(jnp.float32),
        lax.psum_scatter(
            grad_gain_two.astype(jnp.bfloat16), "fsdp", scatter_dimension=0, tiled=True
        ).astype(jnp.float32),
    )
    sum_gain_one, sum_query, sum_key, sum_value, sum_output, sum_router, sum_gain_two = (
        lax.psum(part_gain_one.astype(jnp.bfloat16), "expert").astype(jnp.float32),
        lax.psum(part_query.astype(jnp.bfloat16), "expert").astype(jnp.float32),
        lax.psum(part_key.astype(jnp.bfloat16), "expert").astype(jnp.float32),
        lax.psum(part_value.astype(jnp.bfloat16), "expert").astype(jnp.float32),
        lax.psum(part_output.astype(jnp.bfloat16), "expert").astype(jnp.float32),
        lax.psum(part_router.astype(jnp.bfloat16), "expert").astype(jnp.float32),
        lax.psum(part_gain_two.astype(jnp.bfloat16), "expert").astype(jnp.float32),
    )
    return (
        layer_output,
        grad_input,
        sum_gain_one,
        sum_query,
        sum_key,
        sum_value,
        sum_output,
        sum_router,
        sum_gain_two,
        grad_gate,
        grad_up,
        grad_down,
    )


def solution(mesh):
    placed = (
        P("expert", "fsdp", None),
        P("expert", None),
        P("expert", "fsdp", None),
        P("fsdp"),
        P("fsdp", None),
        P("fsdp", None),
        P("fsdp", None),
        P("fsdp", None),
        P("fsdp", None),
        P("fsdp"),
        P("expert", "fsdp", None),
        P("expert", "fsdp", None),
        P("expert", None, "fsdp"),
        P("expert", "fsdp", None),
    )
    return jax.shard_map(
        local,
        mesh=mesh,
        in_specs=placed,
        out_specs=(
            P("expert", "fsdp", None),
            P("expert", "fsdp", None),
            P("fsdp"),
            P("fsdp", None),
            P("fsdp", None),
            P("fsdp", None),
            P("fsdp", None),
            P("fsdp", None),
            P("fsdp"),
            P("expert", "fsdp", None),
            P("expert", "fsdp", None),
            P("expert", None, "fsdp"),
        ),
        check_vma=False,
    )
```

profile of v0, /device:TPU:0, one launch (start us, length us, event | category | flops | bytes accessed | tf_op | source)
XLA Modules:
  0.0 969.9 jit_solution(15732642532546843857)
XLA Ops:
  9.5 10.8 %all-gather.1 = bf16[8,1,128]{2,1,0:T(2,128)(2,1)S(1)} all-gather(bf16[1,1,128]{2,1,0:T(2,128)(2,1)} %bitcast.472), channel_id=1, replica_groups=mesh['expert'=16,'fsdp'=8] {'fsdp'}, dimensions={0}, use_global_device_ids=true | all-gather | bytes 2304 | tf_op jit(solution)/shard_map/all_gather | solution.py:91
  21.5 14.0 %all-gather.15.cloned.1.call-done = bf16[1024,512]{1,0:T(8,128)(2,1)} async-done(((bf16[128,512]{1,0:T(8,128)(2,1)}), bf16[1024,512]{1,0:T(8,128)(2,1)}) %all-gather.15.cloned.1.call-update) | async-done | bytes 1048592 | tf_op jit(solution)/shard_map/all_gather | solution.py:93
  39.3 21.2 %all-gather.13.cloned.1.call-done = bf16[1024,512]{1,0:T(8,128)(2,1)} async-done(((bf16[128,512]{1,0:T(8,128)(2,1)}), bf16[1024,512]{1,0:T(8,128)(2,1)}) %all-gather.13.cloned.1.call-update) | async-done | bytes 1048592 | tf_op jit(solution)/shard_map/all_gather | solution.py:94
  60.5 2.2 convolution_convert_fusion.5
  65.1 9.0 reduce-window.6
  74.3 8.8 all-gather.2
  83.7 4.3 scatter_custom_fusion
  88.9 2.9 copy.73
  92.7 20.4 %all-gather.17.cloned.1.call-done = bf16[1,1024,512]{1,2,0:T(8,128)(2,1)} async-done(((bf16[1,128,512]{1,2,0:T(8,128)(2,1)}), bf16[1,1024,512]{1,2,0:T(8,128)(2,1)}) %all-gather.17.cloned.1.call-update) | async-done | bytes 1048592 | tf_op jit(solution)/shard_map/all_gather | solution.py:123
  113.1 2.7 fusion.117
  115.8 3.3 copy-done
  120.2 19.4 %all-gather.29.cloned.1.call-done = bf16[1024,512]{1,0:T(8,128)(2,1)} async-done(((bf16[128,512]{1,0:T(8,128)(2,1)}), bf16[1024,512]{1,0:T(8,128)(2,1)}) %all-gather.29.cloned.1.call-update) | async-done | bytes 1048592 | tf_op jit(solution)/shard_map/all_gather | solution.py:124
  141.1 5.2 fusion.50
  146.4 19.8 %all-gather.21.cloned.1.call-done = bf16[1024,1024]{1,0:T(8,128)(2,1)} async-done(((bf16[128,1024]{1,0:T(8,128)(2,1)}), bf16[1024,1024]{1,0:T(8,128)(2,1)}) %all-gather.21.cloned.1.call-update) | async-done | bytes 2097168 | tf_op jit(solution)/shard_map/all_gather | solution.py:95
  166.2 2.1 multiply_reduce_fusion
  168.6 9.7 gather_fusion
  178.2 7.0 all-to-all-start
  186.0 7.4 all-gather.23.cloned.1.call-done
  193.4 48.2 %all-to-all-done = bf16[16,2,64,1024]{3,2,1,0:T(8,128)(2,1)} async-done(((bf16[16,2,64,1024]{3,2,1,0:T(8,128)(2,1)}), bf16[16,2,64,1024]{3,2,1,0:T(8,128)(2,1)}, u32[]{:S(2)}, u32[]{:S(2)}) %all-to-all-start) | async-done | bytes 4194336 | tf_op jit(solution)/shard_map/all_to_all | solution.py:177
  241.6 7.1 fusion.26
  248.7 9.4 fusion.13
  258.2 4.6 convert_bitcast_fusion
  262.7 2.5 copy.82
  265.3 13.9 %all-to-all-start.1 = ((bf16[16,2,64,1024]{3,2,1,0:T(8,128)(2,1)}), bf16[16,2,64,1024]{3,2,1,0:T(8,128)(2,1)}, u32[]{:S(2)}, u32[]{:S(2)}) async-start(bf16[16,2,64,1024]{3,2,1,0:T(8,128)(2,1)} %copy.82), calls=%async_computation.1 | async-start | bytes 8388608 | tf_op jit(solution)/shard_map/all_to_all | solution.py:191
  279.3 11.2 %all_gather.47 = bf16[1024,32]{0,1:T(8,128)(2,1)S(1)} all-gather(bf16[128,32]{0,1:T(8,128)(2,1)S(1)} %copy-done.62), channel_id=1, replica_groups=mesh['expert'=16,'fsdp'=8] {'fsdp'}, dimensions={0}, use_global_device_ids=true | all-gather | bytes 73728 | tf_op jit(solution)/shard_map/all_gather | solution.py:96
  292.6 41.0 %all-to-all-done.1 = bf16[16,2,64,1024]{3,2,1,0:T(8,128)(2,1)} async-done(((bf16[16,2,64,1024]{3,2,1,0:T(8,128)(2,1)}), bf16[16,2,64,1024]{3,2,1,0:T(8,128)(2,1)}, u32[]{:S(2)}, u32[]{:S(2)}) %all-to-all-start.1) | async-done | bytes 4194336 | tf_op jit(solution)/shard_map/all_to_all | solution.py:191
  333.6 7.7 gather_fusion.1
  341.3 3.5 fusion.116
  348.1 10.3 %gather_fusion.2 = bf16[2048,1024]{1,0:T(8,128)(2,1)} fusion(bf16[1025,1024]{1,0:T(8,128)(2,1)S(1)} %concatenate.37, s32[2048]{0:T(1024)} %get-tuple-element.130), kind=kCustom, calls=%fused_computation.2 | custom fusion | bytes 8396800 | tf_op jit(solution)/shard_map/gather | solution.py:217
  358.4 68.1 %all_to_all.20 = bf16[16,2,64,1024]{3,2,1,0:T(8,128)(2,1)S(1)} all-to-all(bf16[16,2,64,1024]{3,2,1,0:T(8,128)(2,1)} %bitcast.407), channel_id=1, replica_groups=mesh['expert'=16,'fsdp'=8] {'expert'}, dimensions={0} | all-to-all | bytes 8388608 | tf_op jit(solution)/shard_map/all_to_all | solution.py:218
  426.5 7.1 fusion.11
  433.7 2.4 fusion.31
  436.8 2.4 fusion.7
  439.2 2.5 copy.93
  441.7 4.7 all-to-all-start.3
  447.9 47.1 %all-to-all-done.3 = bf16[16,2,64,1024]{3,2,1,0:T(8,128)(2,1)} async-done(((bf16[16,2,64,1024]{3,2,1,0:T(8,128)(2,1)}), bf16[16,2,64,1024]{3,2,1,0:T(8,128)(2,1)}, u32[]{:S(2)}, u32[]{:S(2)}) %all-to-all-start.3) | async-done | bytes 4194336 | tf_op jit(solution)/shard_map/all_to_all | solution.py:244
  495.0 7.7 gather_fusion.3
  502.8 3.5 fusion.115
  509.3 5.5 fusion
  518.8 2.4 fusion.28
  521.2 4.6 copy.132
  527.2 5.9 bitcast_convert_fusion.3
  533.1 4.6 copy.134
  541.4 6.6 bitcast_convert_fusion
  548.0 4.8 copy.138
  554.8 6.7 bitcast_convert_fusion.2
  561.6 5.9 bitcast_convert_fusion.1
  569.1 2.2 convolution_convert_fusion.3
  571.4 21.6 %reduce-scatter.33.cloned.1.call-done = bf16[128,512]{1,0:T(8,128)(2,1)} async-done(((bf16[1024,512]{1,0:T(8,128)(2,1)}), bf16[128,512]{1,0:T(8,128)(2,1)}) %reduce-scatter.33.cloned.1.call-update) | async-done | bytes 131088
  596.0 3.0 convolution_multiply_fusion
  599.8 2.2 convolution_convert_fusion.1
  602.1 2.0 convolution_convert_fusion
  605.7 3.5 fusion.63
  609.2 15.9 %reduce-scatter.35.cloned.1.call-done = bf16[128,32]{1,0:T(8,128)(2,1)} async-done(((bf16[1024,32]{1,0:T(8,128)(2,1)}), bf16[128,32]{1,0:T(8,128)(2,1)}) %reduce-scatter.35.cloned.1.call-update) | async-done | bytes 8208
  627.8 32.3 %reduce-scatter.37.cloned.1.call-done = bf16[128,1024]{1,0:T(8,128)(2,1)} async-done(((bf16[1024,1024]{1,0:T(8,128)(2,1)}), bf16[128,1024]{1,0:T(8,128)(2,1)}) %reduce-scatter.37.cloned.1.call-update) | async-done | bytes 262160
  665.6 29.5 %reduce-scatter.27.cloned.1.call-done = bf16[2,128,512]{2,1,0:T(8,128)(2,1)} async-done(((bf16[2,1024,512]{2,1,0:T(8,128)(2,1)}), bf16[2,128,512]{2,1,0:T(8,128)(2,1)}) %reduce-scatter.27.cloned.1.call-update) | async-done | bytes 262160 | tf_op jit(solution)/shard_map/reduce_scatter | solution.py:246
  696.8 33.1 %reduce-scatter.29.cloned.1.call-done = bf16[2,128,512]{2,1,0:T(8,128)(2,1)} async-done(((bf16[2,1024,512]{2,1,0:T(8,128)(2,1)}), bf16[2,128,512]{2,1,0:T(8,128)(2,1)}) %reduce-scatter.29.cloned.1.call-update) | async-done | bytes 262160 | tf_op jit(solution)/shard_map/reduce_scatter | solution.py:249
  731.7 31.4 %reduce-scatter.21.cloned.1.call-done = bf16[128,512]{1,0:T(8,128)(2,1)} async-done(((bf16[1024,512]{1,0:T(8,128)(2,1)}), bf16[128,512]{1,0:T(8,128)(2,1)}) %reduce-scatter.21.cloned.1.call-update) | async-done | bytes 131088 | tf_op jit(solution)/shard_map/reduce_scatter | solution.py:349
  763.1 33.1 %reduce-scatter.23.cloned.1.call-done = bf16[128,512]{1,0:T(8,128)(2,1)} async-done(((bf16[1024,512]{1,0:T(8,128)(2,1)}), bf16[128,512]{1,0:T(8,128)(2,1)}) %reduce-scatter.23.cloned.1.call-update) | async-done | bytes 131088 | tf_op jit(solution)/shard_map/reduce_scatter | solution.py:352
  796.2 34.9 %reduce-scatter.19.cloned.1.call-done = bf16[128,1024]{1,0:T(8,128)(2,1)} async-done(((bf16[1024,1024]{1,0:T(8,128)(2,1)}), bf16[128,1024]{1,0:T(8,128)(2,1)}) %reduce-scatter.19.cloned.1.call-update) | async-done | bytes 262160 | tf_op jit(solution)/shard_map/reduce_scatter | solution.py:346
  831.1 35.1 %reduce-scatter.25.cloned.1.call-done = bf16[128,1024]{1,0:T(8,128)(2,1)} async-done(((bf16[1024,1024]{1,0:T(8,128)(2,1)}), bf16[128,1024]{1,0:T(8,128)(2,1)}) %reduce-scatter.25.cloned.1.call-update) | async-done | bytes 262160 | tf_op jit(solution)/shard_map/reduce_scatter | solution.py:355
  868.2 12.7 %all-reduce.6 = (bf16[1024]{0:T(1024)(128)(2,1)S(1)}, bf16[1024]{0:T(1024)(128)(2,1)S(1)}) all-reduce(bf16[1024]{0:T(1024)(128)(2,1)S(1)} %get-tuple-element.70, bf16[1024]{0:T(1024)(128)(2,1)} %get-tuple-element.68), channel_id=5, replica_groups=mesh['expert'=16,'fsdp'=8] {'fsdp'}, use_global_device_ids=true, to_apply=%region_25.26.clone | all-reduce | flops 2048 | bytes 8192
  881.1 41.8 %all-reduce.4 = (bf16[128]{0:T(256)(128)(2,1)S(1)}, bf16[128,32]{0,1:T(8,128)(2,1)S(1)}, bf16[128]{0:T(256)(128)(2,1)S(1)}) all-reduce(bf16[128]{0:T(256)(128)(2,1)S(1)} %dynamic-slice.3, bf16[128,32]{0,1:T(8,128)(2,1)S(1)} %copy.137, bf16[128]{0:T(256)(128)(2,1)S(1)} %dynamic-slice.5), channel_id=1, replica_groups=mesh['expert'=16,'fsdp'=8] {'expert'}, use_global_device_ids=true, to_apply=%region_26.27 | all-reduce | flops 4352 | bytes 17408 | tf_op jit(solution)/shard_map/psum | solution.py:366
  926.0 29.8 %all-reduce.9.cloned.1.call-done = (bf16[128,1024]{1,0:T(8,128)(2,1)}, bf16[128,512]{1,0:T(8,128)(2,1)}, bf16[128,512]{1,0:T(8,128)(2,1)}, bf16[128,1024]{1,0:T(8,128)(2,1)}) async-done(((bf16[128,1024]{1,0:T(8,128)(2,1)}, bf16[128,512]{1,0:T(8,128)(2,1)}, bf16[128,512]{1,0:T(8,128)(2,1)}, bf16[128,1024]{1,0:T(8,128)(2,1)}), (bf16[128,1024]{1,0:T(8,128)(2,1)}, bf16[128,512]{1,0:T(8,128)(2,1)}, ...) | async-done | bytes 786448 | tf_op jit(solution)/shard_map/psum | solution.py:367
  (305 shorter events, 66.8 us)
Async XLA Ops:
  7.2 53.3 %copy-start.2 = (bf16[1,128,1024]{2,1,0:T(8,128)(2,1)S(1)}, bf16[1,128,1024]{2,1,0:T(8,128)(2,1)}, u32[]{:S(2)}) copy-start(bf16[1,128,1024]{2,1,0:T(8,128)(2,1)} %param.14) | copy-start | bytes 786436
  7.2 57.7 %copy-start.53 = (s32[1,128,8]{1,2,0:T(8,128)S(1)}, s32[1,128,8]{1,2,0:T(8,128)}, u32[]{:S(2)}) copy-start(s32[1,128,8]{1,2,0:T(8,128)} %param.16) | copy-start | bytes 12292
  7.2 28.4 %all-gather.15.cloned.1.call-start = ((), (), s32[]{:S(2)}) async-start(), calls=%async_computation.15 | async-start | bytes 1179648 | tf_op jit(solution)/shard_map/all_gather | solution.py:93
  7.9 52.6 %all-gather.13.cloned.1.call-start = ((), (), s32[]{:S(2)}) async-start(), calls=%async_computation.14 | async-start | bytes 1179648 | tf_op jit(solution)/shard_map/all_gather | solution.py:94
  8.7 80.2 %all-gather.19.cloned.1.call-start = ((), (), s32[]{:S(2)}) async-start(), calls=%async_computation.17 | async-start | bytes 2359296 | tf_op jit(solution)/shard_map/all_gather | solution.py:92
  9.4 103.7 %all-gather.17.cloned.1.call-start = ((), (), s32[]{:S(2)}) async-start(), calls=%async_computation.16 | async-start | bytes 1179648 | tf_op jit(solution)/shard_map/all_gather | solution.py:123
  20.2 71.5 %copy-start.41 = (f32[8,1,128]{2,1,0:T(1,128)}, f32[8,1,128]{2,1,0:T(1,128)S(1)}, u32[]{:S(2)}) copy-start(f32[8,1,128]{2,1,0:T(1,128)S(1)} %convert_element_type.612) | copy-start | bytes 12292
  21.3 14.2 %copy-start.70 = (f32[128]{0:T(128)}, f32[128]{0:T(128)S(1)}, u32[]{:S(2)}) copy-start(f32[128]{0:T(128)S(1)} %fusion.66) | copy-start | bytes 1540
  21.3 52.9 %copy-start.71 = (bf16[128]{0:T(256)(128)(2,1)S(1)}, bf16[128]{0:T(256)(128)(2,1)}, u32[]{:S(2)}) copy-start(bf16[128]{0:T(256)(128)(2,1)} %param.23) | copy-start | bytes 772
  21.4 70.4 %copy-start.58 = (f32[128]{0:T(128)}, f32[128]{0:T(128)S(1)}, u32[]{:S(2)}) copy-start(f32[128]{0:T(128)S(1)} %fusion.105) | copy-start | bytes 1540
  21.5 71.1 %copy-start.36 = (f32[128,32]{0,1:T(8,128)}, f32[128,32]{0,1:T(8,128)S(1)}, u32[]{:S(2)}) copy-start(f32[128,32]{0,1:T(8,128)S(1)} %get-tuple-element.140) | copy-start | bytes 49156
  21.5 71.1 %copy-start.38 = (f32[128,32]{0,1:T(8,128)}, f32[128,32]{0,1:T(8,128)S(1)}, u32[]{:S(2)}) copy-start(f32[128,32]{0,1:T(8,128)S(1)} %get-tuple-element.141) | copy-start | bytes 49156
  35.6 53.1 %copy-start.65 = (s32[1,1024]{1,0:T(1,128)S(1)}, s32[1,1024]{1,0:T(1,128)}, u32[]{:S(2)}) copy-start(s32[1,1024]{1,0:T(1,128)} %param.15) | copy-start | bytes 12292
  39.3 100.3 %all-gather.29.cloned.1.call-start = ((), (), s32[]{:S(2)}) async-start(), calls=%async_computation.28 | async-start | bytes 1179648 | tf_op jit(solution)/shard_map/all_gather | solution.py:124
  62.8 103.4 %all-gather.21.cloned.1.call-start = ((), (), s32[]{:S(2)}) async-start(), calls=%async_computation.18 | async-start | bytes 2359296 | tf_op jit(solution)/shard_map/all_gather | solution.py:95
  63.4 130.0 %all-gather.23.cloned.1.call-start = ((), (), s32[]{:S(2)}) async-start(), calls=%async_computation.19 | async-start | bytes 2359296 | tf_op jit(solution)/shard_map/all_gather | solution.py:179
  64.1 184.6 %all-gather.25.cloned.1.call-start = ((), (), s32[]{:S(2)}) async-start(), calls=%async_computation.20 | async-start | bytes 2359296 | tf_op jit(solution)/shard_map/all_gather | solution.py:180
  83.1 85.3 %copy-start.49 = (f32[8,1,128]{2,1,0:T(1,128)}, f32[8,1,128]{2,1,0:T(1,128)S(1)}, u32[]{:S(2)}) copy-start(f32[8,1,128]{2,1,0:T(1,128)S(1)} %convert_element_type.613) | copy-start | bytes 12292
  92.7 23.1 %copy-start.25 = (bf16[1,128,16,64]{1,3,2,0:T(8,128)(2,1)}, bf16[1,128,16,64]{1,3,2,0:T(8,128)(2,1)S(1)}, u32[]{:S(2)}) copy-start(bf16[1,128,16,64]{1,3,2,0:T(8,128)(2,1)S(1)} %pad_maximum_fusion) | copy-start | bytes 786436
  120.2 26.1 %copy-start.56 = (f32[8,2,128]{2,1,0:T(2,128)}, f32[8,2,128]{2,1,0:T(2,128)S(1)}, u32[]{:S(2)}) copy-start(f32[8,2,128]{2,1,0:T(2,128)S(1)} %fusion.3) | copy-start | bytes 24580
  141.1 5.3 copy-start.14
  146.4 31.8 %copy-start.34 = (bf16[8,64,2,128]{3,1,2,0:T(8,128)(2,1)}, bf16[8,64,2,128]{3,1,2,0:T(8,128)(2,1)S(1)}, u32[]{:S(2)}) copy-start(bf16[8,64,2,128]{3,1,2,0:T(8,128)(2,1)S(1)} %fusion.50) | copy-start | bytes 786436
  168.4 9.9 %copy-start.72 = (f32[128]{0:T(128)}, f32[128]{0:T(128)S(1)}, u32[]{:S(2)}) copy-start(f32[128]{0:T(128)S(1)} %get-tuple-element.144) | copy-start | bytes 1540
  168.4 9.8 %copy-start.68 = (f32[128]{0:T(128)}, f32[128]{0:T(128)S(1)}, u32[]{:S(2)}) copy-start(f32[128]{0:T(128)S(1)} %fusion.106) | copy-start | bytes 1540
  168.5 122.8 %copy-start.19 = (bf16[128,1024]{1,0:T(8,128)(2,1)}, bf16[128,1024]{1,0:T(8,128)(2,1)S(1)}, u32[]{:S(2)}) copy-start(bf16[128,1024]{1,0:T(8,128)(2,1)S(1)} %fusion.81) | copy-start | bytes 786436
  178.2 63.4 %all-to-all-start = ((bf16[16,2,64,1024]{3,2,1,0:T(8,128)(2,1)}), bf16[16,2,64,1024]{3,2,1,0:T(8,128)(2,1)}, u32[]{:S(2)}, u32[]{:S(2)}) async-start(bf16[16,2,64,1024]{3,2,1,0:T(8,128)(2,1)} %bitcast.406), calls=%async_computation | async-start | bytes 8388608 | tf_op jit(solution)/shard_map/all_to_all | solution.py:177
  185.3 72.9 %all-gather.27.cloned.1.call-start = ((), (), s32[]{:S(2)}) async-start(), calls=%async_computation.21 | async-start | bytes 2359296 | tf_op jit(solution)/shard_map/all_gather | solution.py:181
  265.3 14.0 %copy-start.62 = (bf16[128,32]{0,1:T(8,128)(2,1)S(1)}, bf16[128,32]{0,1:T(8,128)(2,1)}, u32[]{:S(2)}) copy-start(bf16[128,32]{0,1:T(8,128)(2,1)} %param.22) | copy-start | bytes 24580
  265.3 25.2 %copy-start.21 = (bf16[1,128,1024]{2,1,0:T(8,128)(2,1)S(1)}, bf16[1,128,1024]{2,1,0:T(8,128)(2,1)}, u32[]{:S(2)}) copy-start(bf16[1,128,1024]{2,1,0:T(8,128)(2,1)} %param.27) | copy-start | bytes 786436
  265.3 68.4 %all-to-all-start.1 = ((bf16[16,2,64,1024]{3,2,1,0:T(8,128)(2,1)}), bf16[16,2,64,1024]{3,2,1,0:T(8,128)(2,1)}, u32[]{:S(2)}, u32[]{:S(2)}) async-start(bf16[16,2,64,1024]{3,2,1,0:T(8,128)(2,1)} %copy.82), calls=%async_computation.1 | async-start | bytes 8388608 | tf_op jit(solution)/shard_map/all_to_all | solution.py:191
  290.5 50.8 %copy-start.51 = (s32[1024]{0:T(1024)}, s32[1024]{0:T(1024)S(1)}, u32[]{:S(2)}) copy-start(s32[1024]{0:T(1024)S(1)} %broadcast_clamp_fusion) | copy-start | bytes 12292
  292.1 41.5 %copy-start.63 = (f32[128]{0:T(128)}, f32[128]{0:T(128)S(1)}, u32[]{:S(2)}) copy-start(f32[128]{0:T(128)S(1)} %reduce_max.20) | copy-start | bytes 1540
  347.4 11.1 %copy-start.45 = (f32[128,8]{0,1:T(8,128)}, f32[128,8]{0,1:T(8,128)S(1)}, u32[]{:S(2)}) copy-start(f32[128,8]{0,1:T(8,128)S(1)} %get-tuple-element.103) | copy-start | bytes 12292
  358.4 68.1 %copy-start.74 = (bf16[2,512,1024]{2,1,0:T(8,128)(2,1)S(1)}, bf16[2,512,1024]{2,1,0:T(8,128)(2,1)}, u32[]{:S(2)}) copy-start(bf16[2,512,1024]{2,1,0:T(8,128)(2,1)} %all-gather.27.cloned.1.call-done) | copy-start | bytes 6291460
  358.4 68.1 %copy-start.76 = (f32[2,16,64,512]{3,2,1,0:T(8,128)S(1)}, f32[2,16,64,512]{3,2,1,0:T(8,128)}, u32[]{:S(2)}) copy-start(f32[2,16,64,512]{3,2,1,0:T(8,128)} %fusion.26) | copy-start | bytes 12582916
  426.5 7.1 copy-start.16
  426.5 7.2 copy-start.28
  441.7 53.3 %copy-start.52 = (s32[1024]{0:T(1024)S(1)}, s32[1024]{0:T(1024)}, u32[]{:S(2)}) copy-start(s32[1024]{0:T(1024)} %copy-done.51) | copy-start | bytes 12292
  441.7 53.3 %all-to-all-start.3 = ((bf16[16,2,64,1024]{3,2,1,0:T(8,128)(2,1)}), bf16[16,2,64,1024]{3,2,1,0:T(8,128)(2,1)}, u32[]{:S(2)}, u32[]{:S(2)}) async-start(bf16[16,2,64,1024]{3,2,1,0:T(8,128)(2,1)} %copy.93), calls=%async_computation.3 | async-start | bytes 8388608 | tf_op jit(solution)/shard_map/all_to_all | solution.py:244
  446.4 121.3 %reduce-scatter.31.cloned.1.call-start = ((), (), s32[]{:S(2)}) async-start(), calls=%async_computation.29 | async-start | bytes 1179648
  509.2 5.6 copy-start.20
  509.2 5.6 slice-start
  509.3 5.9 slice-start.1
  527.1 65.9 %reduce-scatter.33.cloned.1.call-start = ((), (), s32[]{:S(2)}) async-start(), calls=%async_computation.30 | async-start | bytes 1179648
  539.0 86.2 %reduce-scatter.35.cloned.1.call-start = ((), (), s32[]{:S(2)}) async-start(), calls=%async_computation.31 | async-start | bytes 294912
  541.1 119.0 %reduce-scatter.37.cloned.1.call-start = ((), (), s32[]{:S(2)}) async-start(), calls=%async_computation.32 | async-start | bytes 2359296
  554.7 6.9 copy-start.32
  554.7 140.3 %reduce-scatter.27.cloned.1.call-start = ((), (), s32[]{:S(2)}) async-start(), calls=%async_computation.26 | async-start | bytes 2359296 | tf_op jit(solution)/shard_map/reduce_scatter | solution.py:246
  561.6 7.5 copy-start.37
  561.6 7.5 copy-start.39
  561.6 168.4 %reduce-scatter.29.cloned.1.call-start = ((), (), s32[]{:S(2)}) async-start(), calls=%async_computation.27 | async-start | bytes 2359296 | tf_op jit(solution)/shard_map/reduce_scatter | solution.py:249
  567.6 26.7 %copy-start.42 = (f32[8,1,128]{2,1,0:T(1,128)S(1)}, f32[8,1,128]{2,1,0:T(1,128)}, u32[]{:S(2)}) copy-start(f32[8,1,128]{2,1,0:T(1,128)} %copy-done.41) | copy-start | bytes 12292
  567.6 26.7 %copy-start.59 = (f32[128]{0:T(128)S(1)}, f32[128]{0:T(128)}, u32[]{:S(2)}) copy-start(f32[128]{0:T(128)} %copy-done.58) | copy-start | bytes 1540
  567.6 28.3 %copy-start.5 = (bf16[1,1024,512]{1,2,0:T(8,128)(2,1)S(1)}, bf16[1,1024,512]{1,2,0:T(8,128)(2,1)}, u32[]{:S(2)}) copy-start(bf16[1,1024,512]{1,2,0:T(8,128)(2,1)} %all-gather.17.cloned.1.call-done) | copy-start | bytes 3145732
  567.6 195.5 %reduce-scatter.21.cloned.1.call-start = ((), (), s32[]{:S(2)}) async-start(), calls=%async_computation.23 | async-start | bytes 1179648 | tf_op jit(solution)/shard_map/reduce_scatter | solution.py:349
  571.3 224.9 %reduce-scatter.23.cloned.1.call-start = ((), (), s32[]{:S(2)}) async-start(), calls=%async_computation.24 | async-start | bytes 1179648 | tf_op jit(solution)/shard_map/reduce_scatter | solution.py:352
  595.9 235.2 %reduce-scatter.19.cloned.1.call-start = ((), (), s32[]{:S(2)}) async-start(), calls=%async_computation.22 | async-start | bytes 2359296 | tf_op jit(solution)/shard_map/reduce_scatter | solution.py:346
  602.0 264.1 %reduce-scatter.25.cloned.1.call-start = ((), (), s32[]{:S(2)}) async-start(), calls=%async_computation.25 | async-start | bytes 2359296 | tf_op jit(solution)/shard_map/reduce_scatter | solution.py:355
  604.1 21.8 %copy-start.3 = (bf16[1024,1024]{1,0:T(8,128)(2,1)S(1)}, bf16[1024,1024]{1,0:T(8,128)(2,1)}, u32[]{:S(2)}) copy-start(bf16[1024,1024]{1,0:T(8,128)(2,1)} %all-gather.19.cloned.1.call-done) | copy-start | bytes 6291460
  604.1 351.6 %all-reduce.9.cloned.1.call-start = ((), (), s32[]{:S(2)}) async-start(), calls=%async_computation.33 | async-start | bytes 1572864 | tf_op jit(solution)/shard_map/psum | solution.py:367
  625.9 240.7 %copy-start.44 = (f32[8,1,128]{2,1,0:T(1,128)S(1)}, f32[8,1,128]{2,1,0:T(1,128)}, u32[]{:S(2)}) copy-start(f32[8,1,128]{2,1,0:T(1,128)} %copy-done.41) | copy-start | bytes 12292
  626.0 240.7 %copy-start.61 = (f32[128]{0:T(128)S(1)}, f32[128]{0:T(128)}, u32[]{:S(2)}) copy-start(f32[128]{0:T(128)} %copy-done.58) | copy-start | bytes 1540
  627.8 238.4 %copy-start.17 = (bf16[1024,512]{1,0:T(8,128)(2,1)S(1)}, bf16[1024,512]{1,0:T(8,128)(2,1)}, u32[]{:S(2)}) copy-start(bf16[1024,512]{1,0:T(8,128)(2,1)} %all-gather.15.cloned.1.call-done) | copy-start | bytes 3145732
  627.8 238.9 %copy-start.18 = (bf16[1024,512]{1,0:T(8,128)(2,1)S(1)}, bf16[1024,512]{1,0:T(8,128)(2,1)}, u32[]{:S(2)}) copy-start(bf16[1024,512]{1,0:T(8,128)(2,1)} %all-gather.13.cloned.1.call-done) | copy-start | bytes 3145732
  (38 other events, 108.6 us)
Sparse Core Ops, SparseCore 0:
  9.7 25.7 all-gather.14
  37.3 23.1 all-gather.12
  62.2 24.9 all-gather.18
  89.4 23.6 all-gather.16
  115.3 24.3 all-gather.28
  141.2 24.9 all-gather.20
  167.9 25.4 all-gather.22
  195.1 25.4 all-gather.24
  222.2 27.5 all-gather.26
  527.3 32.5 reduce-scatter.30
  562.2 30.7 reduce-scatter.32
  595.8 29.3 reduce-scatter.34
  627.7 32.4 reduce-scatter.36
  662.5 32.4 reduce-scatter.26
  697.4 32.4 reduce-scatter.28
  732.3 30.7 reduce-scatter.20
  765.5 30.6 reduce-scatter.22
  798.6 32.4 reduce-scatter.18
  833.6 32.4 reduce-scatter.24
  870.0 85.6 all-reduce.8
where the time goes:
time: 979 us; the launch traced here: 970 us
  waiting for transfers between devices  540 us (55%)
  blocking collectives  153 us (16%)
  matrix products  100 us (10%)
  local copies, waits for them, and re-layouts  94.8 us (10%)
  other arithmetic  37.6 us (4%)
  starting transfers between devices  27.2 us (3%)
  between operations  16.9 us (2%)
    unnamed x24, waiting for transfers between devices  74.5 us
    all_to_all x1, blocking collectives, local(): lax.all_to_all(dresult_send, 'expert', split_axis=0, concat_axis=0, tiled...  68.1 us
    all_to_all x1, waiting for transfers between devices, local(): lax.all_to_all(send_rows, 'expert', split_axis=0, concat_axis=0, tiled=True)  48.2 us
    all_to_all x1, waiting for transfers between devices, local(): lax.all_to_all(dassign, 'expert', split_axis=0, concat_axis=0, tiled=True)  47.1 us
    psum x1, blocking collectives, local(): lax.psum(part_gain_one.astype(jnp.bfloat16), 'expert').astype(jnp.float32)  41.8 us
    all_to_all x1, waiting for transfers between devices, local(): lax.all_to_all(result, 'expert', split_axis=0, concat_axis=0, tiled=True)  41 us
    unnamed x177, local copies, waits for them, and re-layouts  35.5 us
    reduce_scatter x1, waiting for transfers between devices, local(): lax.psum_scatter(grad_output_full.astype(jnp.bfloat16), 'fsdp', scatter_d...  35.1 us
  transfers between devices with their start and end apart: 23, of which 19 were waited for; matrix products, arithmetic and copies ran while one was open for 15% of the time, Pallas kernels for 0%

commit v1 on v0

v1 whole, which is shorter than its diff:
```python
import jax
import jax.numpy as jnp
from jax import lax
from jax.sharding import PartitionSpec as P

HEAD_DIM = 64
EXPERTS = 32
SLOTS = 64
NF = 8
NE = 16
LP = 128
LENGTH = 1024
D = 1024
FF = 512

epsilon = 1e-06
rope_base = 10000.0
highest = lax.Precision.HIGHEST
bf16 = jnp.bfloat16
f32 = jnp.float32


def shift_x(v, k):
    return lax.ppermute(v, "fsdp", [(i, (i + 2 * k) % NF) for i in range(NF)])


def swap_core(v):
    return lax.ppermute(v, "fsdp", [(i, i ^ 1) for i in range(NF)])


def shift_z(v, k):
    return lax.ppermute(v, "expert", [(i, (i // 4) * 4 + (i + k) % 4) for i in range(NE)])


def shift_y(v, k):
    return lax.ppermute(v, "expert", [(i, (i + 4 * k) % NE) for i in range(NE)])


def put(buffer, piece, place):
    return lax.dynamic_update_index_in_dim(buffer, piece, place, 0)


def ring_gather(shift, v, place):
    got = [(v, place)] + [(shift(v, k), (place - k) % 4) for k in (1, 3, 2)]
    out = jnp.zeros((4,) + v.shape, v.dtype)
    for piece, where in got:
        out = put(out, piece, where)
    return out


def gather_fsdp(v):
    f = lax.axis_index("fsdp")
    x, c = f // 2, f % 2
    mine = ring_gather(shift_x, v, x)
    other = swap_core(mine)
    first = jnp.where(c == 0, mine, other)
    second = jnp.where(c == 0, other, mine)
    return jnp.stack([first, second], axis=1).reshape((NF,) + v.shape)


def gather_expert(v):
    e = lax.axis_index("expert")
    y, z = e // 4, e % 4
    n = v.shape[0] // 2
    a = ring_gather(shift_z, v[:n], z)
    b = ring_gather(shift_y, v[n:], y)
    a = ring_gather(shift_y, a, y)
    b = ring_gather(shift_z, b, z)
    return jnp.concatenate([a, jnp.swapaxes(b, 0, 1)], axis=2).reshape((NE,) + v.shape)


def ring_sum(shift, p, place):
    total = lax.dynamic_index_in_dim(p, place, 0, keepdims=False).astype(f32)
    for k in (1, 3, 2):
        piece = lax.dynamic_index_in_dim(p, (place + k) % 4, 0, keepdims=False)
        total = total + shift(piece, k).astype(f32)
    return total


def scatter_expert(p):
    e = lax.axis_index("expert")
    y, z = e // 4, e % 4
    n = p.shape[1] // 2
    p = p.reshape((4, 4) + p.shape[1:])
    a = p[:, :, :n]
    b = jnp.swapaxes(p[:, :, n:], 0, 1)
    a = ring_sum(shift_y, a, y).astype(bf16)
    b = ring_sum(shift_z, b, z).astype(bf16)
    a = ring_sum(shift_z, a, z)
    b = ring_sum(shift_y, b, y)
    return jnp.concatenate([a, b], axis=0)


def swap_fsdp(v):
    return lax.all_to_all(v, "fsdp", split_axis=0, concat_axis=0, tiled=True)


def rope_tables(positions):
    half_width = HEAD_DIM // 2
    exponent = jnp.arange(half_width).astype(f32) * (2.0 / HEAD_DIM)
    inverse = rope_base ** (-exponent)
    angles = positions.astype(f32)[:, None] * inverse[None, :]
    return (jnp.cos(angles), jnp.sin(angles))


def rotate(vectors, cosine_tab, sine_tab):
    a, b = vectors[..., : HEAD_DIM // 2], vectors[..., HEAD_DIM // 2 :]
    cos, sin = cosine_tab[:, None, :], sine_tab[:, None, :]
    return jnp.concatenate([a * cos - b * sin, b * cos + a * sin], axis=-1)


def masked_gates(logits, member):
    low = jnp.where(member, logits, -1e30)
    top = jnp.max(low, axis=-1, keepdims=True)
    expo = jnp.where(member, jnp.exp(low - top), 0.0)
    return expo / jnp.sum(expo, axis=-1, keepdims=True)


def norm_back(u, v, gain):
    r = lax.rsqrt(jnp.mean(v * v, axis=-1, keepdims=True) + epsilon)
    inner = jnp.mean(gain * u * v, axis=-1, keepdims=True)
    return r * gain * u - v * (r * r * r) * inner, jnp.sum(u * v * r, axis=0)


def local(
    layer_input,
    segment_ids,
    routes,
    attn_gain,
    w_query,
    w_key,
    w_value,
    w_output,
    w_router,
    ffn_gain,
    w_gate,
    w_up,
    w_down,
    cotangent,
):
    e = lax.axis_index("expert")
    x_own = layer_input[0]
    cot_own = cotangent[0]
    columns = jnp.concatenate(
        [
            w_query.reshape(LP, NF, 128),
            w_key.reshape(LP, NF, 64),
            w_value.reshape(LP, NF, 64),
        ],
        axis=-1,
    ).swapaxes(0, 1)
    extra = jnp.concatenate(
        [
            jnp.concatenate([attn_gain, ffn_gain])[None],
            w_router.reshape(16, 256),
            jnp.zeros((15, 256), bf16),
        ],
        axis=0,
    )
    payload = jnp.concatenate([columns, jnp.broadcast_to(extra[None], (NF, 32, 256))], axis=1)
    got = swap_fsdp(payload)
    x_all = gather_fsdp(x_own).reshape(LENGTH, D)
    w_qkv = got[:, :LP].reshape(D, 256)
    gain_one = got[:, LP, :128].reshape(D).astype(f32)
    gain_two = got[:, LP, 128:].reshape(D).astype(f32)
    router = got[:, LP + 1 : LP + 17].reshape(D, EXPERTS)
    w_out = lax.all_gather(w_output, "fsdp", axis=0, tiled=True)
    w_gu = lax.all_gather(jnp.concatenate([w_gate, w_up], axis=-1), "fsdp", axis=0)
    w_gu = w_gu.swapaxes(0, 1).reshape(2, D, 2 * FF)
    w_dn = lax.all_gather(w_down, "fsdp", axis=0)
    w_dn = w_dn.transpose(1, 2, 0, 3).reshape(2, FF, D)
    cot_all = gather_expert(cot_own)
    routes_all = lax.all_gather(routes[0], "expert", axis=0)

    own_ids = 2 * e + jnp.arange(2, dtype=jnp.int32)
    chosen_own = jnp.any(routes_all[:, :, :, None] == own_ids, axis=2)
    before = (jnp.arange(LP)[:, None] > jnp.arange(LP)[None, :]).astype(bf16)
    rank = jnp.einsum(
        "ts,bsj->jbt", before, chosen_own.astype(bf16), preferred_element_type=f32
    )
    member_t = chosen_own.transpose(2, 0, 1)
    pick = (
        (rank[:, :, None, :] == jnp.arange(SLOTS, dtype=f32)[:, None]) & member_t[:, :, None, :]
    ).astype(bf16)
    member_all = jnp.any(
        routes_all[:, :, :, None] == jnp.arange(EXPERTS, dtype=jnp.int32), axis=2
    )
    member_own = jnp.any(
        routes[0][:, :, None] == jnp.arange(EXPERTS, dtype=jnp.int32), axis=1
    )
    cot_slots = jnp.einsum("jbst,btd->jbsd", pick, cot_all, preferred_element_type=bf16).reshape(
        2, NE * SLOTS, D
    )

    x_full = x_all.astype(f32)
    r_one = lax.rsqrt(jnp.mean(x_full * x_full, axis=-1, keepdims=True) + epsilon)
    normed = (x_full * r_one * gain_one).astype(bf16)
    qkv = jnp.dot(normed, w_qkv, preferred_element_type=f32)
    cosine_tab, sine_tab = rope_tables(jnp.arange(LENGTH))
    rotated = rotate(qkv[:, :192].reshape(LENGTH, 3, HEAD_DIM), cosine_tab, sine_tab).astype(bf16)
    query, key = rotated[:, :2], rotated[:, 2]
    value = qkv[:, 192:].astype(bf16)
    seg = segment_ids[0]
    places = jnp.arange(LENGTH)
    allowed = (seg[:, None] == seg[None, :]) & (places[None, :] <= places[:, None])
    scale = HEAD_DIM**-0.5
    scores = jnp.einsum("qhd,kd->hqk", query, key, preferred_element_type=f32) * scale
    scores = jnp.where(allowed, scores, -1e30)
    row_top = jnp.max(scores, axis=-1, keepdims=True)
    expo = jnp.exp(scores - row_top)
    total = jnp.sum(expo, axis=-1, keepdims=True)
    probs = expo / total
    probs_low = probs.astype(bf16)
    attended = jnp.einsum("hqk,kd->qhd", probs_low, value, preferred_element_type=f32)
    attended = attended.reshape(LENGTH, 128).astype(bf16)
    attended_own = swap_fsdp(attended.reshape(NF, LP, 128)).swapaxes(0, 1).reshape(LP, D)
    after_attn = x_own.astype(f32) + jnp.dot(attended_own, w_out, preferred_element_type=f32)
    r_two = lax.rsqrt(jnp.mean(after_attn * after_attn, axis=-1, keepdims=True) + epsilon)
    normed_two = (after_attn * r_two * gain_two).astype(bf16)

    rows_all = gather_expert(normed_two)
    logits_all = jnp.einsum("btd,de->bte", rows_all, router, preferred_element_type=f32)
    gates_all = masked_gates(logits_all, member_all)
    gates_pair = lax.dynamic_slice_in_dim(gates_all, 2 * e, 2, axis=2).transpose(2, 0, 1)
    pick_f = pick.astype(f32)
    gate_slots = jnp.sum(pick_f * gates_pair[:, :, None, :], axis=-1).reshape(2, NE * SLOTS, 1)
    inputs = jnp.einsum("jbst,btd->jbsd", pick, rows_all, preferred_element_type=bf16).reshape(
        2, NE * SLOTS, D
    )
    both = jnp.einsum("jrd,jdf->jrf", inputs, w_gu, preferred_element_type=f32)
    gate_val, up_val = both[..., :FF], both[..., FF:]
    sig = jax.nn.sigmoid(gate_val)
    activated = gate_val * sig
    hidden = (activated * up_val).astype(bf16)
    result = jnp.einsum("jrf,jfd->jrd", hidden, w_dn, preferred_element_type=f32).astype(bf16)
    cot_f = cot_slots.astype(f32)
    result_f = result.astype(f32)
    dgate_slots = jnp.sum(result_f * cot_f, axis=-1).reshape(2, NE, SLOTS)
    weighted = (gate_slots * result_f).astype(bf16).reshape(2, NE, SLOTS, D)
    mix_part = jnp.einsum("jbst,jbsd->btd", pick, weighted, preferred_element_type=f32).astype(
        bf16
    )
    dresult = (gate_slots * cot_f).astype(bf16)
    dhidden = jnp.einsum("jrd,jfd->jrf", dresult, w_dn, preferred_element_type=f32)
    dgate_val = (dhidden * up_val * sig * (1.0 + gate_val * (1.0 - sig))).astype(bf16)
    dup_val = (dhidden * activated).astype(bf16)
    dboth = jnp.concatenate([dgate_val, dup_val], axis=-1)
    dassign = jnp.einsum("jrf,jdf->jrd", dboth, w_gu, preferred_element_type=f32).astype(bf16)
    dassign = dassign.reshape(2, NE, SLOTS, D)
    drows_part = jnp.einsum("jbst,jbsd->btd", pick, dassign, preferred_element_type=f32)
    dgate_tok = jnp.sum(pick_f * dgate_slots[..., None], axis=2)
    dgate_high = dgate_tok.astype(bf16).astype(f32)
    dgate_low = dgate_tok - dgate_high
    lanes = jnp.arange(128)
    extra_cols = jnp.zeros((NE, LP, 128), f32)
    for j in range(2):
        extra_cols = extra_cols + jnp.where(lanes == 2 * e + j, dgate_high[j][..., None], 0.0)
        extra_cols = extra_cols + jnp.where(
            lanes == EXPERTS + 2 * e + j, dgate_low[j][..., None], 0.0
        )
    drows_send = jnp.concatenate([drows_part, extra_cols], axis=-1).astype(bf16)
    drows = scatter_expert(drows_send)

    grad_gu_part = jnp.einsum("jrd,jrf->jdf", inputs, dboth, preferred_element_type=f32)
    grad_dn_part = jnp.einsum("jrf,jrd->jfd", hidden, dresult, preferred_element_type=f32)
    grad_gu = lax.psum_scatter(
        grad_gu_part.astype(bf16).reshape(2, NF, LP, 2 * FF).swapaxes(0, 1),
        "fsdp",
        scatter_dimension=0,
    ).astype(f32)
    grad_gate, grad_up = grad_gu[..., :FF], grad_gu[..., FF:]
    grad_down = lax.psum_scatter(
        grad_dn_part.astype(bf16).reshape(2, FF, NF, LP).transpose(2, 0, 1, 3),
        "fsdp",
        scatter_dimension=0,
    ).astype(f32)
    mix = scatter_expert(mix_part)
    layer_output = (after_attn + mix).astype(bf16)

    logits = jnp.dot(normed_two, router, preferred_element_type=f32)
    gates = masked_gates(logits, member_own)
    dgate_own = drows[:, D : D + EXPERTS] + drows[:, D + EXPERTS : D + 2 * EXPERTS]
    dlogits = gates * (dgate_own - jnp.sum(gates * dgate_own, axis=-1, keepdims=True))
    dnormed_two = drows[:, :D] + jnp.einsum(
        "te,de->td", dlogits, router.astype(f32), precision=highest
    )
    dafter_norm, part_gain_two = norm_back(dnormed_two, after_attn, gain_two)
    dafter = cot_own.astype(f32) + dafter_norm
    dbranch = dafter.astype(bf16)
    dattended_own = jnp.einsum("td,id->ti", dbranch, w_out, preferred_element_type=f32).astype(
        bf16
    )
    dattended = swap_fsdp(dattended_own.reshape(LP, NF, 128).swapaxes(0, 1)).reshape(
        LENGTH, 2, HEAD_DIM
    )
    dbranch_all = gather_fsdp(dbranch).reshape(LENGTH, D)
    part_router = jnp.einsum(
        "td,te->de", normed_two.astype(f32), dlogits, precision=highest
    )

    dvalue = jnp.einsum("hqk,qhd->kd", probs_low, dattended, preferred_element_type=f32)
    dprobs = jnp.einsum("qhd,kd->hqk", dattended, value, preferred_element_type=f32)
    delta = jnp.sum(probs * dprobs, axis=-1, keepdims=True)
    dscores = (probs * (dprobs - delta)).astype(bf16)
    dquery = jnp.einsum("hqk,kd->qhd", dscores, key, preferred_element_type=f32) * scale
    dkey = jnp.einsum("hqk,qhd->kd", dscores, query, preferred_element_type=f32) * scale
    unrotated = rotate(
        jnp.concatenate([dquery, dkey[:, None]], axis=1), cosine_tab, -sine_tab
    ).reshape(LENGTH, 192)
    dqkv = jnp.concatenate([unrotated, dvalue], axis=-1).astype(bf16)
    part_qkv = jnp.einsum("td,ti->di", normed, dqkv, preferred_element_type=f32)
    dnormed_part = jnp.einsum("ti,di->td", dqkv, w_qkv, preferred_element_type=f32)
    part_gain_one = jnp.sum(dnormed_part * (x_full * r_one), axis=0)
    dnormed = lax.psum_scatter(
        dnormed_part.astype(bf16).reshape(NF, LP, D), "fsdp", scatter_dimension=0
    ).astype(f32)
    dinput_norm, _ = norm_back(dnormed, x_own.astype(f32), gain_one)
    grad_input = (dafter + dinput_norm).astype(bf16)

    part_output = jnp.einsum("ti,td->id", attended, dbranch_all, preferred_element_type=f32)
    grad_output = lax.psum(part_output.astype(bf16), "expert").astype(f32)
    small = jnp.concatenate(
        [
            part_qkv,
            part_router,
            part_gain_one[:, None],
            part_gain_two[:, None],
            jnp.zeros((D, 94), f32),
        ],
        axis=-1,
    ).astype(bf16)
    traded = swap_fsdp(small.reshape(NF, LP, 384))
    heads_part = traded[:, :, :256].swapaxes(0, 1)
    rest_part = jnp.sum(traded[:, :, 256:].astype(f32), axis=0).astype(bf16)
    total_part = jnp.concatenate([heads_part.reshape(LP, 2048), rest_part], axis=-1)
    chunk = lax.all_to_all(
        total_part.reshape(NE, LP // NE, 2176), "expert", split_axis=0, concat_axis=0, tiled=True
    )
    chunk = jnp.sum(chunk.astype(f32), axis=0).astype(bf16)
    total_sum = lax.all_gather(chunk, "expert", axis=0, tiled=True).astype(f32)
    heads_sum = total_sum[:, :2048].reshape(LP, NF, 256)
    grad_query = heads_sum[:, :, :128].reshape(LP, 1024)
    grad_key = heads_sum[:, :, 128:192].reshape(LP, 512)
    grad_value = heads_sum[:, :, 192:].reshape(LP, 512)
    grad_router = total_sum[:, 2048:2080]
    grad_gain_one = total_sum[:, 2080]
    grad_gain_two = total_sum[:, 2081]
    return (
        layer_output[None],
        grad_input[None],
        grad_gain_one,
        grad_query,
        grad_key,
        grad_value,
        grad_output,
        grad_router,
        grad_gain_two,
        grad_gate,
        grad_up,
        grad_down,
    )


def solution(mesh):
    placed = (
        P("expert", "fsdp", None),
        P("expert", None),
        P("expert", "fsdp", None),
        P("fsdp"),
        P("fsdp", None),
        P("fsdp", None),
        P("fsdp", None),
        P("fsdp", None),
        P("fsdp", None),
        P("fsdp"),
        P("expert", "fsdp", None),
        P("expert", "fsdp", None),
        P("expert", None, "fsdp"),
        P("expert", "fsdp", None),
    )
    return jax.shard_map(
        local,
        mesh=mesh,
        in_specs=placed,
        out_specs=(
            P("expert", "fsdp", None),
            P("expert", "fsdp", None),
            P("fsdp"),
            P("fsdp", None),
            P("fsdp", None),
            P("fsdp", None),
            P("fsdp", None),
            P("fsdp", None),
            P("fsdp"),
            P("expert", "fsdp", None),
            P("expert", "fsdp", None),
            P("expert", None, "fsdp"),
        ),
        check_vma=False,
    )
```

time: 979 us -> 621 us (0.63)
  waiting for transfers between devices: 540 us -> 134 us
  starting transfers between devices: 27.2 us -> 107 us
  blocking collectives: 153 us -> 78.9 us
  local copies, waits for them, and re-layouts: 94.8 us -> 123 us
  other arithmetic: 37.6 us -> 54.5 us
    all_to_all x3, waiting for transfers between devices: 136 us -> 0.01 us  [swap_fsdp(): return lax.all_to_all(v, 'fsdp', split_axis=0, concat_axis=0, tiled=True)]
    reduce_scatter x6 -> x3, waiting for transfers between devices: 197 us -> 70.4 us  [the longest x1 36.3 us: local(): lax.psum_scatter(grad_gu_part.astype(bf16).reshape(2, NF, LP, 2 * FF).swa...]
    all_gather x9 -> x3, waiting for transfers between devices: 102 us -> 0.01 us  [the longest x1 0.01 us: local(): w_out = lax.all_gather(w_output, 'fsdp', axis=0, tiled=True)]
    ppermute x0 -> x56, starting transfers between devices: none -> 94 us  [the longest x24 38.1 us: shift_z(): lax.ppermute(v, 'expert', [(i, i // 4 * 4 + (i + k) % 4) for i in range(N...]
    unnamed x24 -> x7, waiting for transfers between devices: 74.5 us -> 1.46 us
    ppermute x0 -> x56, waiting for transfers between devices: none -> 61.9 us  [the longest x24 40.9 us: shift_z(): lax.ppermute(v, 'expert', [(i, i // 4 * 4 + (i + k) % 4) for i in range(N...]
    psum x1 -> x0, blocking collectives: 41.8 us -> none  [local(): lax.psum(part_gain_one.astype(jnp.bfloat16), 'expert').astype(jnp.float32)]
    gather x4 -> x0, local copies, waits for them, and re-layouts: 35.4 us -> none  [the longest x1 10.3 us: local(): padded_grads[owner_of_slot].reshape(owners, EXP_DEV, slot_count, model_dim)]
  transfers between devices with their start and end apart: 23 -> 66, of which waited for: 19 -> 21; matrix products, arithmetic and copies ran while one was open for 15% -> 33% of each run, Pallas kernels for 0% -> 0%
where the time goes in v1:
time: 621 us; the launch traced here: 611 us
  waiting for transfers between devices  134 us (22%)
  local copies, waits for them, and re-layouts  123 us (20%)
  starting transfers between devices  107 us (17%)
  matrix products  97.9 us (16%)
  blocking collectives  78.9 us (13%)
  other arithmetic  54.5 us (9%)
  between operations  16.2 us (3%)
    ppermute x24, waiting for transfers between devices, shift_z(): lax.ppermute(v, 'expert', [(i, i // 4 * 4 + (i + k) % 4) for i in range(N...  40.9 us
    ppermute x24, starting transfers between devices, shift_z(): lax.ppermute(v, 'expert', [(i, i // 4 * 4 + (i + k) % 4) for i in range(N...  38.1 us
    reduce_scatter x1, waiting for transfers between devices, local(): lax.psum_scatter(grad_gu_part.astype(bf16).reshape(2, NF, LP, 2 * FF).swa...  36.3 us
    dynamic_update_slice x38, local copies, waits for them, and re-layouts, put(): return lax.dynamic_update_index_in_dim(buffer, piece, place, 0)  32.9 us
    reduce_scatter x1, waiting for transfers between devices, local(): lax.psum_scatter(dnormed_part.astype(bf16).reshape(NF, LP, D), 'fsdp', sc...  32.7 us
    ppermute x24, starting transfers between devices, shift_y(): return lax.ppermute(v, 'expert', [(i, (i + 4 * k) % NE) for i in range(NE)])  32.3 us
    all_gather x1, blocking collectives, local(): routes_all = lax.all_gather(routes[0], 'expert', axis=0)  23.6 us
    all_gather x1, blocking collectives, local(): total_sum = lax.all_gather(chunk, 'expert', axis=0, tiled=True).astype(f32)  22.6 us
  transfers between devices with their start and end apart: 66, of which 21 were waited for; matrix products, arithmetic and copies ran while one was open for 33% of the time, Pallas kernels for 0%

profile of v1, /device:TPU:0, one launch (start us, length us, event | category | flops | bytes accessed | tf_op | source)
XLA Modules:
  0.0 611.3 jit_solution(3367001275345111408)
XLA Ops:
  27.3 4.2 all-to-all-start
  34.4 23.6 %all_gather.22 = s32[16,128,8]{1,2,0:T(8,128)S(1)} all-gather(s32[1,128,8]{1,2,0:T(8,128)S(1)} %copy-done.43), channel_id=1, replica_groups=mesh['expert'=16,'fsdp'=8] {'expert'}, dimensions={0}, use_global_device_ids=true | all-gather | bytes 69632 | tf_op jit(solution)/shard_map/all_gather | solution.py:173
  67.8 3.1 collective-permute-done.30
  77.5 4.8 collective-permute-done.36
  87.2 2.2 collective-permute-start.33
  92.3 2.5 collective-permute-start.38
  102.8 11.5 %collective-permute-start.3 = (bf16[4,128,1024]{2,1,0:T(8,128)(2,1)S(1)}, bf16[4,128,1024]{2,1,0:T(8,128)(2,1)S(1)}, u32[]{:S(2)}, u32[]{:S(2)}) collective-permute-start(bf16[4,128,1024]{2,1,0:T(8,128)(2,1)S(1)} %bitcast_dynamic-update-slice_fusion.20), channel_id=1, source_target_pairs={{0,1},{1,0},{2,3},{3,2},{4,5},{5,4},{6,7},{7,6},{8,9},{9,8},{10,11... | collective-permute-start | bytes 3145736 | tf_op jit(solution)/shard_map/ppermute | solution.py:28
  121.2 4.3 pad_maximum_fusion.1
  129.4 8.6 %fusion.144 = (f32[2,1024]{1,0:T(2,128)}, f32[2,1024,1024]{1,2,0:T(8,128)}) fusion(pred[1024,1024]{0,1:T(8,128)(4,1)} %fusion.16, bf16[1024,64,1]{0,1,2:T(8,128)(2,1)} %maximum_bitcast_fusion.1, bf16[1024,3,32]{0,2,1:T(8,128)(2,1)} %copy-done.17, bf16[1024,3,32]{0,2,1:T(8,128)(2,1)} %copy-done.15), kind=kOutput, calls=%fused_computation.320 | convolution fusion | flops 277349376 | bytes 9969664 | tf_op jit(solution)/shard_map/sub | solution.py:210
  138.0 4.2 fusion.34
  143.7 4.8 all-to-all-start.1
  148.5 3.4 convert_bitcast_fusion
  151.9 4.2 copy.418
  156.1 2.1 multiply_reduce_fusion.4
  166.1 3.2 collective-permute-start.11
  170.8 2.1 fusion.146
  174.5 4.3 copy.510
  178.8 4.2 reshape.418
  190.1 2.6 collective-permute-start.8
  192.7 2.1 collective-permute-start.9
  198.6 3.2 collective-permute-start.14
  207.3 6.9 %collective-permute-done.8 = bf16[4,64,1024]{2,1,0:T(8,128)(2,1)S(1)} collective-permute-done((bf16[4,64,1024]{2,1,0:T(8,128)(2,1)}, bf16[4,64,1024]{2,1,0:T(8,128)(2,1)S(1)}, u32[]{:S(2)}, u32[]{:S(2)}) %collective-permute-start.8) | collective-permute-done | bytes 524320 | tf_op jit(solution)/shard_map/ppermute | solution.py:36
  215.2 7.9 %collective-permute-done.13 = bf16[4,64,1024]{2,1,0:T(8,128)(2,1)S(1)} collective-permute-done((bf16[4,64,1024]{2,1,0:T(8,128)(2,1)}, bf16[4,64,1024]{2,1,0:T(8,128)(2,1)S(1)}, u32[]{:S(2)}, u32[]{:S(2)}) %collective-permute-start.13) | collective-permute-done | bytes 524320 | tf_op jit(solution)/shard_map/ppermute | solution.py:32
  225.8 2.7 copy.407
  228.5 4.9 fusion.145
  234.8 6.8 %copy.408 = bf16[8,2,128,1024]{2,0,3,1:T(8,128)(2,1)} copy(bf16[8,2,128,1024]{3,2,1,0:T(8,128)(2,1)} %bitcast.444) | data formatting | bytes 8388608 | tf_op jit(solution)/shard_map/all_gather | solution.py:168
  241.6 7.3 %reshape.417 = bf16[2,1024,1024]{1,2,0:T(8,128)(2,1)} reshape(bf16[2,8,128,1024]{2,1,3,0:T(8,128)(2,1)} %bitcast.437) | data formatting | bytes 8388608 | tf_op jit(solution)/shard_map/reshape | solution.py:169
  248.9 7.6 %fusion.150 = f32[2,1024,1024]{1,2,0:T(8,128)S(1)} fusion(bf16[2,1024,1024]{2,1,0:T(8,128)(2,1)} %bitcast.445, bf16[2,1024,1024]{1,2,0:T(8,128)(2,1)} %reshape.417), kind=kOutput, calls=%fused_computation.325 | convolution fusion | flops 4294967296 | bytes 16777216 | tf_op jit(solution)/shard_map/jrd,jdf->jrf/dot_general | solution.py:230
  256.5 3.3 copy-done.1
  261.4 9.3 %fusion.3 = (f32[2,1024]{1,0:T(2,128)}, bf16[2,1024,1024]{2,1,0:T(8,128)(2,1)}) fusion(f32[2,16,64,1024]{3,2,1,0:T(8,128)} %copy.418, bf16[2,1024,512]{1,2,0:T(8,128)(2,1)S(1)} %multiply_convert_fusion.3, bf16[2,512,1024]{2,1,0:T(8,128)(2,1)S(1)} %copy-done.5), kind=kOutput, calls=%fused_computation.5 | convolution fusion | flops 2155870208 | bytes 16785408 | tf_op jit(solution)/shard_map/jrf,jfd->jrd/dot_general | solution.py:235
  276.9 7.3 %fusion.7 = (bf16[2,1024,1024]{2,1,0:T(8,128)(2,1)}, bf16[2,1024,1024]{2,1,0:T(8,128)(2,1)S(1)}) fusion(f32[2,16,64,1024]{3,2,1,0:T(8,128)} %copy.418, f32[2,1024]{1,0:T(2,128)} %mul.473, bf16[2,1024,1024]{2,1,0:T(8,128)(2,1)} %get-tuple-element.168), kind=kLoop, calls=%fused_computation.13 | loop fusion | flops 10485760 | bytes 20979712 | tf_op jit(solution)/shard_map/convert_element_type | solution.py:243
  286.0 7.6 %multiply_convert_fusion.2 = (bf16[2,1024,512]{1,2,0:T(8,128)(2,1)}, bf16[2,1024,512]{1,2,0:T(8,128)(2,1)}) fusion(f32[2,1024,1024]{1,2,0:T(8,128)S(1)} %copy-done.2, bf16[2,1024,1024]{2,1,0:T(8,128)(2,1)} %get-tuple-element.154, bf16[2,512,1024]{2,1,0:T(8,128)(2,1)S(1)} %copy-done.6), kind=kOutput, calls=%fused_computation.37 | convolution fusion | flops 2161115136 | bytes 18874368 | tf_op jit(solution)/shard_map/jrd,jfd->jrf/dot_general | solution.py:244
  296.5 2.5 collective-permute-start.16
  299.8 3.7 collective-permute-start.18
  304.4 3.2 collective-permute-start.23
  307.7 7.1 %fusion.20 = bf16[2,1024,1024]{2,1,0:T(8,128)(2,1)S(1)} fusion(bf16[2,1024,1024]{1,2,0:T(8,128)(2,1)S(1)} %copy-done.7, bf16[2,1024,512]{1,2,0:T(8,128)(2,1)} %get-tuple-element.98, bf16[2,1024,512]{1,2,0:T(8,128)(2,1)} %get-tuple-element.97), kind=kOutput, calls=%fused_computation.51 | convolution fusion | flops 4305453056 | bytes 12582912 | tf_op jit(solution)/shard_map/jrf,jdf->jrd/dot_general | solution.py:248
  327.5 8.2 %collective-permute-done.24 = bf16[4,64,1024]{2,1,0:T(8,128)(2,1)S(1)} collective-permute-done((bf16[4,64,1024]{2,1,0:T(8,128)(2,1)S(1)}, bf16[4,64,1024]{2,1,0:T(8,128)(2,1)S(1)}, u32[]{:S(2)}, u32[]{:S(2)}) %collective-permute-start.24) | collective-permute-done | bytes 524320 | tf_op jit(solution)/shard_map/ppermute | solution.py:32
  337.3 11.6 %collective-permute-done.46 = bf16[4,64,1152]{2,1,0:T(8,128)(2,1)S(1)} collective-permute-done((bf16[4,64,1152]{2,1,0:T(8,128)(2,1)S(1)}, bf16[4,64,1152]{2,1,0:T(8,128)(2,1)S(1)}, u32[]{:S(2)}, u32[]{:S(2)}) %collective-permute-start.46) | collective-permute-done | bytes 589856 | tf_op jit(solution)/shard_map/ppermute | solution.py:32
  348.9 4.2 collective-permute-done.47
  353.7 3.3 collective-permute-start.20
  360.4 3.8 collective-permute-start.26
  365.5 2.5 collective-permute-start.50
  368.0 2.3 collective-permute-start.51
  371.2 2.4 collective-permute-start.44
  376.7 3.7 collective-permute-done.45
  384.8 3.3 collective-permute-start.52
  389.3 2.4 collective-permute-start.54
  395.3 2.6 collective-permute-done.54
  400.2 3.5 all-to-all-start.2
  408.1 5.2 convert_bitcast_fusion.1
  415.5 4.9 fusion.4
  420.4 4.7 fusion.6
  428.6 5.5 fusion.51
  435.2 4.6 multiply_reduce_fusion
  440.1 8.6 %fusion.21 = bf16[2,1024,1024]{2,1,0:T(8,128)(2,1)S(1)} fusion(bf16[2,1024,1024]{2,1,0:T(8,128)(2,1)} %bitcast.446, bf16[2,1024,512]{1,2,0:T(8,128)(2,1)} %get-tuple-element.98, bf16[2,1024,512]{1,2,0:T(8,128)(2,1)} %get-tuple-element.97), kind=kOutput, calls=%fused_computation.52 | convolution fusion | flops 4305453056 | bytes 12582912 | tf_op jit(solution)/shard_map/jrd,jrf->jdf/dot_general | solution.py:264
  448.7 2.6 copy.508
  453.7 2.6 copy.469
  457.1 2.5 convolution_convert_fusion.1
  459.6 2.6 concatenate.90
  462.3 17.8 %all_to_all.25 = bf16[8,128,384]{2,1,0:T(8,128)(2,1)S(1)} all-to-all(bf16[8,128,384]{2,1,0:T(8,128)(2,1)S(1)} %concatenate.90), channel_id=1, replica_groups=mesh['expert'=16,'fsdp'=8] {'fsdp'}, dimensions={0} | all-to-all | bytes 1572864 | tf_op jit(solution)/shard_map/all_to_all | solution.py:95
  480.8 14.9 %all_to_all.26 = bf16[16,8,2176]{2,1,0:T(8,128)(2,1)S(1)} all-to-all(bf16[16,8,2176]{2,1,0:T(8,128)(2,1)S(1)} %pad_maximum_fusion.12), channel_id=1, replica_groups=mesh['expert'=16,'fsdp'=8] {'expert'}, dimensions={0} | all-to-all | bytes 1114112 | tf_op jit(solution)/shard_map/all_to_all | solution.py:336
  495.8 22.6 %all_gather.27 = bf16[128,2176]{1,0:T(8,128)(2,1)S(1)} all-gather(bf16[8,2176]{1,0:T(8,128)(2,1)S(1)} %reduce_sum.179), channel_id=1, replica_groups=mesh['expert'=16,'fsdp'=8] {'expert'}, dimensions={0}, use_global_device_ids=true | all-gather | bytes 591872 | tf_op jit(solution)/shard_map/all_gather | solution.py:340
  530.1 32.7 %reduce-scatter.4.cloned.1.call-done = bf16[1,128,1024]{2,1,0:T(8,128)(2,1)} async-done(((bf16[8,128,1024]{2,1,0:T(8,128)(2,1)}), bf16[1,128,1024]{2,1,0:T(8,128)(2,1)}) %reduce-scatter.4.cloned.1.call-update) | async-done | bytes 262160 | tf_op jit(solution)/shard_map/reduce_scatter | solution.py:314
  565.8 36.3 %reduce-scatter.6.cloned.1.call-done = bf16[1,2,128,1024]{3,2,1,0:T(8,128)(2,1)} async-done(((bf16[8,2,128,1024]{3,2,1,0:T(8,128)(2,1)}), bf16[1,2,128,1024]{3,2,1,0:T(8,128)(2,1)}) %reduce-scatter.6.cloned.1.call-update) | async-done | bytes 524304 | tf_op jit(solution)/shard_map/reduce_scatter | solution.py:266
  (412 shorter events, 179.9 us)
Async XLA Ops:
  7.2 148.9 %all-gather.6.cloned.1.call-start = ((), (), s32[]{:S(2)}) async-start(), calls=%async_computation.8 | async-start | bytes 2359296 | tf_op jit(solution)/shard_map/all_gather | solution.py:167
  7.9 166.6 %all-gather.10.cloned.1.call-start = ((), (), s32[]{:S(2)}) async-start(), calls=%async_computation.14 | async-start | bytes 2359296 | tf_op jit(solution)/shard_map/all_gather | solution.py:170
  8.7 78.5 %collective-permute-start = (bf16[128,1024]{1,0:T(8,128)(2,1)}, bf16[128,1024]{1,0:T(8,128)(2,1)}, u32[]{:S(2)}, u32[]{:S(2)}) collective-permute-start(bf16[128,1024]{1,0:T(8,128)(2,1)} %bitcast.450), channel_id=1, source_target_pairs={{0,2},{1,3},{2,4},{3,5},{4,6},{5,7},{6,0},{7,1},{8,10},{9,11},{10,... | collective-permute-start | bytes 786440 | tf_op jit(solution)/shard_map/ppermute | solution.py:24
  10.3 80.1 %collective-permute-start.1 = (bf16[128,1024]{1,0:T(8,128)(2,1)}, bf16[128,1024]{1,0:T(8,128)(2,1)}, u32[]{:S(2)}, u32[]{:S(2)}) collective-permute-start(bf16[128,1024]{1,0:T(8,128)(2,1)} %bitcast.451), channel_id=1, source_target_pairs={{0,6},{1,7},{2,0},{3,1},{4,2},{5,3},{6,4},{7,5},{8,14},{9,15},{10,... | collective-permute-start | bytes 786440 | tf_op jit(solution)/shard_map/ppermute | solution.py:24
  12.0 80.3 %collective-permute-start.2 = (bf16[128,1024]{1,0:T(8,128)(2,1)}, bf16[128,1024]{1,0:T(8,128)(2,1)}, u32[]{:S(2)}, u32[]{:S(2)}) collective-permute-start(bf16[128,1024]{1,0:T(8,128)(2,1)} %bitcast.452), channel_id=1, source_target_pairs={{0,4},{1,5},{2,6},{3,7},{4,0},{5,1},{6,2},{7,3},{8,12},{9,13},{10,... | collective-permute-start | bytes 786440 | tf_op jit(solution)/shard_map/ppermute | solution.py:24
  16.5 47.7 %collective-permute-start.28 = (bf16[64,1024]{1,0:T(8,128)(2,1)}, bf16[64,1024]{1,0:T(8,128)(2,1)S(1)}, u32[]{:S(2)}, u32[]{:S(2)}) collective-permute-start(bf16[64,1024]{1,0:T(8,128)(2,1)} %get-tuple-element.143), channel_id=1, source_target_pairs={{0,8},{8,16},{16,24},{24,0},{32,40},{40,48},{48,56},{56,32},{64,72... | collective-permute-start | bytes 393224 | tf_op jit(solution)/shard_map/ppermute | solution.py:32
  18.4 47.9 %collective-permute-start.29 = (bf16[64,1024]{1,0:T(8,128)(2,1)}, bf16[64,1024]{1,0:T(8,128)(2,1)S(1)}, u32[]{:S(2)}, u32[]{:S(2)}) collective-permute-start(bf16[64,1024]{1,0:T(8,128)(2,1)} %get-tuple-element.143), channel_id=1, source_target_pairs={{0,24},{8,0},{16,8},{24,16},{32,56},{40,32},{48,40},{56,48},{64,88... | collective-permute-start | bytes 393224 | tf_op jit(solution)/shard_map/ppermute | solution.py:32
  27.3 68.4 %all-to-all-start = ((bf16[8,160,256]{2,1,0:T(8,128)(2,1)}), bf16[8,160,256]{2,1,0:T(8,128)(2,1)}, u32[]{:S(2)}, u32[]{:S(2)}) async-start(bf16[8,160,256]{2,1,0:T(8,128)(2,1)} %copy.393), calls=%async_computation | async-start | bytes 1310720 | tf_op jit(solution)/shard_map/all_to_all | solution.py:95
  31.5 203.3 %all-gather.8.cloned.1.call-start = ((), (), s32[]{:S(2)}) async-start(), calls=%async_computation.13 | async-start | bytes 4718592 | tf_op jit(solution)/shard_map/all_gather | solution.py:168
  64.2 6.7 %collective-permute-start.30 = (bf16[64,1024]{1,0:T(8,128)(2,1)}, bf16[64,1024]{1,0:T(8,128)(2,1)S(1)}, u32[]{:S(2)}, u32[]{:S(2)}) collective-permute-start(bf16[64,1024]{1,0:T(8,128)(2,1)} %get-tuple-element.143), channel_id=1, source_target_pairs={{0,16},{8,24},{16,0},{24,8},{32,48},{40,56},{48,32},{56,40},{64,80... | collective-permute-start | bytes 393224 | tf_op jit(solution)/shard_map/ppermute | solution.py:32
  66.3 8.6 %collective-permute-start.34 = (bf16[64,1024]{1,0:T(8,128)(2,1)}, bf16[64,1024]{1,0:T(8,128)(2,1)S(1)}, u32[]{:S(2)}, u32[]{:S(2)}) collective-permute-start(bf16[64,1024]{1,0:T(8,128)(2,1)} %get-tuple-element.144), channel_id=1, source_target_pairs={{0,32},{8,40},{16,48},{24,56},{32,64},{40,72},{48,80},{56,88},{64,... | collective-permute-start | bytes 393224 | tf_op jit(solution)/shard_map/ppermute | solution.py:36
  70.9 5.7 collective-permute-start.35
  74.9 7.4 %collective-permute-start.36 = (bf16[64,1024]{1,0:T(8,128)(2,1)}, bf16[64,1024]{1,0:T(8,128)(2,1)S(1)}, u32[]{:S(2)}, u32[]{:S(2)}) collective-permute-start(bf16[64,1024]{1,0:T(8,128)(2,1)} %get-tuple-element.144), channel_id=1, source_target_pairs={{0,64},{8,72},{16,80},{24,88},{32,96},{40,104},{48,112},{56,120},{... | collective-permute-start | bytes 393224 | tf_op jit(solution)/shard_map/ppermute | solution.py:36
  76.5 24.8 %collective-permute-start.31 = (bf16[4,64,1024]{2,1,0:T(8,128)(2,1)}, bf16[4,64,1024]{2,1,0:T(8,128)(2,1)}, u32[]{:S(2)}, u32[]{:S(2)}) collective-permute-start(bf16[4,64,1024]{2,1,0:T(8,128)(2,1)} %bitcast_dynamic-update-slice_fusion.26), channel_id=1, source_target_pairs={{0,32},{8,40},{16,48},{24,56},{32,64},{40,72},{48,80},{56,88},{64,... | collective-permute-start | bytes 1572872 | tf_op jit(solution)/shard_map/ppermute | solution.py:36
  82.4 20.4 %collective-permute-start.32 = (bf16[4,64,1024]{2,1,0:T(8,128)(2,1)}, bf16[4,64,1024]{2,1,0:T(8,128)(2,1)}, u32[]{:S(2)}, u32[]{:S(2)}) collective-permute-start(bf16[4,64,1024]{2,1,0:T(8,128)(2,1)} %bitcast_dynamic-update-slice_fusion.26), channel_id=1, source_target_pairs={{0,96},{8,104},{16,112},{24,120},{32,0},{40,8},{48,16},{56,24},{64... | collective-permute-start | bytes 1572872 | tf_op jit(solution)/shard_map/ppermute | solution.py:36
  87.2 28.3 %collective-permute-start.33 = (bf16[4,64,1024]{2,1,0:T(8,128)(2,1)}, bf16[4,64,1024]{2,1,0:T(8,128)(2,1)}, u32[]{:S(2)}, u32[]{:S(2)}) collective-permute-start(bf16[4,64,1024]{2,1,0:T(8,128)(2,1)} %bitcast_dynamic-update-slice_fusion.26), channel_id=1, source_target_pairs={{0,64},{8,72},{16,80},{24,88},{32,96},{40,104},{48,112},{56,120},{... | collective-permute-start | bytes 1572872 | tf_op jit(solution)/shard_map/ppermute | solution.py:36
  90.4 26.2 %collective-permute-start.37 = (bf16[4,64,1024]{2,1,0:T(8,128)(2,1)}, bf16[4,64,1024]{2,1,0:T(8,128)(2,1)}, u32[]{:S(2)}, u32[]{:S(2)}) collective-permute-start(bf16[4,64,1024]{2,1,0:T(8,128)(2,1)} %bitcast_dynamic-update-slice_fusion.23), channel_id=1, source_target_pairs={{0,8},{8,16},{16,24},{24,0},{32,40},{40,48},{48,56},{56,32},{64,72... | collective-permute-start | bytes 1572872 | tf_op jit(solution)/shard_map/ppermute | solution.py:32
  92.3 26.2 %collective-permute-start.38 = (bf16[4,64,1024]{2,1,0:T(8,128)(2,1)}, bf16[4,64,1024]{2,1,0:T(8,128)(2,1)}, u32[]{:S(2)}, u32[]{:S(2)}) collective-permute-start(bf16[4,64,1024]{2,1,0:T(8,128)(2,1)} %bitcast_dynamic-update-slice_fusion.23), channel_id=1, source_target_pairs={{0,24},{8,0},{16,8},{24,16},{32,56},{40,32},{48,40},{56,48},{64,88... | collective-permute-start | bytes 1572872 | tf_op jit(solution)/shard_map/ppermute | solution.py:32
  101.4 19.0 %collective-permute-start.39 = (bf16[4,64,1024]{2,1,0:T(8,128)(2,1)}, bf16[4,64,1024]{2,1,0:T(8,128)(2,1)S(1)}, u32[]{:S(2)}, u32[]{:S(2)}) collective-permute-start(bf16[4,64,1024]{2,1,0:T(8,128)(2,1)} %bitcast_dynamic-update-slice_fusion.23), channel_id=1, source_target_pairs={{0,16},{8,24},{16,0},{24,8},{32,48},{40,56},{48,32},{56,40},{64,80... | collective-permute-start | bytes 1572872 | tf_op jit(solution)/shard_map/ppermute | solution.py:32
  102.8 22.8 %collective-permute-start.3 = (bf16[4,128,1024]{2,1,0:T(8,128)(2,1)S(1)}, bf16[4,128,1024]{2,1,0:T(8,128)(2,1)S(1)}, u32[]{:S(2)}, u32[]{:S(2)}) collective-permute-start(bf16[4,128,1024]{2,1,0:T(8,128)(2,1)S(1)} %bitcast_dynamic-update-slice_fusion.20), channel_id=1, source_target_pairs={{0,1},{1,0},{2,3},{3,2},{4,5},{5,4},{6,7},{7,6},{8,9},{9,8},{10,11... | collective-permute-start | bytes 3145736 | tf_op jit(solution)/shard_map/ppermute | solution.py:28
  143.7 12.4 %all-to-all-start.1 = ((bf16[8,128,128]{1,2,0:T(8,128)(2,1)}), bf16[8,128,128]{1,2,0:T(8,128)(2,1)S(1)}, u32[]{:S(2)}, u32[]{:S(2)}) async-start(bf16[8,128,128]{1,2,0:T(8,128)(2,1)} %copy.396), calls=%async_computation.1 | async-start | bytes 524288 | tf_op jit(solution)/shard_map/all_to_all | solution.py:95
  160.8 23.7 %collective-permute-start.4 = (bf16[64,1024]{1,0:T(8,128)(2,1)}, bf16[64,1024]{1,0:T(8,128)(2,1)}, u32[]{:S(2)}, u32[]{:S(2)}) collective-permute-start(bf16[64,1024]{1,0:T(8,128)(2,1)} %get-tuple-element.146), channel_id=1, source_target_pairs={{0,8},{8,16},{16,24},{24,0},{32,40},{40,48},{48,56},{56,32},{64,72... | collective-permute-start | bytes 393224 | tf_op jit(solution)/shard_map/ppermute | solution.py:32
  162.2 24.1 %collective-permute-start.5 = (bf16[64,1024]{1,0:T(8,128)(2,1)}, bf16[64,1024]{1,0:T(8,128)(2,1)}, u32[]{:S(2)}, u32[]{:S(2)}) collective-permute-start(bf16[64,1024]{1,0:T(8,128)(2,1)} %get-tuple-element.146), channel_id=1, source_target_pairs={{0,24},{8,0},{16,8},{24,16},{32,56},{40,32},{48,40},{56,48},{64,88... | collective-permute-start | bytes 393224 | tf_op jit(solution)/shard_map/ppermute | solution.py:32
  164.1 23.8 %collective-permute-start.6 = (bf16[64,1024]{1,0:T(8,128)(2,1)}, bf16[64,1024]{1,0:T(8,128)(2,1)}, u32[]{:S(2)}, u32[]{:S(2)}) collective-permute-start(bf16[64,1024]{1,0:T(8,128)(2,1)} %get-tuple-element.146), channel_id=1, source_target_pairs={{0,16},{8,24},{16,0},{24,8},{32,48},{40,56},{48,32},{56,40},{64,80... | collective-permute-start | bytes 393224 | tf_op jit(solution)/shard_map/ppermute | solution.py:32
  166.1 26.6 %collective-permute-start.10 = (bf16[64,1024]{1,0:T(8,128)(2,1)}, bf16[64,1024]{1,0:T(8,128)(2,1)}, u32[]{:S(2)}, u32[]{:S(2)}) collective-permute-start(bf16[64,1024]{1,0:T(8,128)(2,1)} %get-tuple-element.147), channel_id=1, source_target_pairs={{0,32},{8,40},{16,48},{24,56},{32,64},{40,72},{48,80},{56,88},{64,... | collective-permute-start | bytes 393224 | tf_op jit(solution)/shard_map/ppermute | solution.py:36
  166.1 30.3 %collective-permute-start.11 = (bf16[64,1024]{1,0:T(8,128)(2,1)}, bf16[64,1024]{1,0:T(8,128)(2,1)}, u32[]{:S(2)}, u32[]{:S(2)}) collective-permute-start(bf16[64,1024]{1,0:T(8,128)(2,1)} %get-tuple-element.147), channel_id=1, source_target_pairs={{0,96},{8,104},{16,112},{24,120},{32,0},{40,8},{48,16},{56,24},{64... | collective-permute-start | bytes 393224 | tf_op jit(solution)/shard_map/ppermute | solution.py:36
  184.5 13.4 %collective-permute-start.12 = (bf16[64,1024]{1,0:T(8,128)(2,1)}, bf16[64,1024]{1,0:T(8,128)(2,1)S(1)}, u32[]{:S(2)}, u32[]{:S(2)}) collective-permute-start(bf16[64,1024]{1,0:T(8,128)(2,1)} %get-tuple-element.147), channel_id=1, source_target_pairs={{0,64},{8,72},{16,80},{24,88},{32,96},{40,104},{48,112},{56,120},{... | collective-permute-start | bytes 393224 | tf_op jit(solution)/shard_map/ppermute | solution.py:36
  189.4 15.8 %collective-permute-start.7 = (bf16[4,64,1024]{2,1,0:T(8,128)(2,1)}, bf16[4,64,1024]{2,1,0:T(8,128)(2,1)S(1)}, u32[]{:S(2)}, u32[]{:S(2)}) collective-permute-start(bf16[4,64,1024]{2,1,0:T(8,128)(2,1)} %bitcast_dynamic-update-slice_fusion.33), channel_id=1, source_target_pairs={{0,32},{8,40},{16,48},{24,56},{32,64},{40,72},{48,80},{56,88},{64,... | collective-permute-start | bytes 1572872 | tf_op jit(solution)/shard_map/ppermute | solution.py:36
  190.1 24.1 %collective-permute-start.8 = (bf16[4,64,1024]{2,1,0:T(8,128)(2,1)}, bf16[4,64,1024]{2,1,0:T(8,128)(2,1)S(1)}, u32[]{:S(2)}, u32[]{:S(2)}) collective-permute-start(bf16[4,64,1024]{2,1,0:T(8,128)(2,1)} %bitcast_dynamic-update-slice_fusion.33), channel_id=1, source_target_pairs={{0,96},{8,104},{16,112},{24,120},{32,0},{40,8},{48,16},{56,24},{64... | collective-permute-start | bytes 1572872 | tf_op jit(solution)/shard_map/ppermute | solution.py:36
  192.7 22.5 %collective-permute-start.9 = (bf16[4,64,1024]{2,1,0:T(8,128)(2,1)}, bf16[4,64,1024]{2,1,0:T(8,128)(2,1)S(1)}, u32[]{:S(2)}, u32[]{:S(2)}) collective-permute-start(bf16[4,64,1024]{2,1,0:T(8,128)(2,1)} %bitcast_dynamic-update-slice_fusion.33), channel_id=1, source_target_pairs={{0,64},{8,72},{16,80},{24,88},{32,96},{40,104},{48,112},{56,120},{... | collective-permute-start | bytes 1572872 | tf_op jit(solution)/shard_map/ppermute | solution.py:36
  198.6 24.5 %collective-permute-start.13 = (bf16[4,64,1024]{2,1,0:T(8,128)(2,1)}, bf16[4,64,1024]{2,1,0:T(8,128)(2,1)S(1)}, u32[]{:S(2)}, u32[]{:S(2)}) collective-permute-start(bf16[4,64,1024]{2,1,0:T(8,128)(2,1)} %bitcast_dynamic-update-slice_fusion.29), channel_id=1, source_target_pairs={{0,8},{8,16},{16,24},{24,0},{32,40},{40,48},{48,56},{56,32},{64,72... | collective-permute-start | bytes 1572872 | tf_op jit(solution)/shard_map/ppermute | solution.py:32
  198.6 24.5 %collective-permute-start.14 = (bf16[4,64,1024]{2,1,0:T(8,128)(2,1)}, bf16[4,64,1024]{2,1,0:T(8,128)(2,1)S(1)}, u32[]{:S(2)}, u32[]{:S(2)}) collective-permute-start(bf16[4,64,1024]{2,1,0:T(8,128)(2,1)} %bitcast_dynamic-update-slice_fusion.29), channel_id=1, source_target_pairs={{0,24},{8,0},{16,8},{24,16},{32,56},{40,32},{48,40},{56,48},{64,88... | collective-permute-start | bytes 1572872 | tf_op jit(solution)/shard_map/ppermute | solution.py:32
  205.2 18.0 %collective-permute-start.15 = (bf16[4,64,1024]{2,1,0:T(8,128)(2,1)}, bf16[4,64,1024]{2,1,0:T(8,128)(2,1)S(1)}, u32[]{:S(2)}, u32[]{:S(2)}) collective-permute-start(bf16[4,64,1024]{2,1,0:T(8,128)(2,1)} %bitcast_dynamic-update-slice_fusion.29), channel_id=1, source_target_pairs={{0,16},{8,24},{16,0},{24,8},{32,48},{40,56},{48,32},{56,40},{64,80... | collective-permute-start | bytes 1572872 | tf_op jit(solution)/shard_map/ppermute | solution.py:32
  296.5 22.7 %collective-permute-start.16 = (bf16[4,64,1024]{2,1,0:T(8,128)(2,1)}, bf16[4,64,1024]{2,1,0:T(8,128)(2,1)}, u32[]{:S(2)}, u32[]{:S(2)}) collective-permute-start(bf16[4,64,1024]{2,1,0:T(8,128)(2,1)} %get-tuple-element.112), channel_id=1, source_target_pairs={{0,32},{8,40},{16,48},{24,56},{32,64},{40,72},{48,80},{56,88},{64,... | collective-permute-start | bytes 1572872 | tf_op jit(solution)/shard_map/ppermute | solution.py:36
  299.1 22.0 %collective-permute-start.17 = (bf16[4,64,1024]{2,1,0:T(8,128)(2,1)}, bf16[4,64,1024]{2,1,0:T(8,128)(2,1)}, u32[]{:S(2)}, u32[]{:S(2)}) collective-permute-start(bf16[4,64,1024]{2,1,0:T(8,128)(2,1)} %get-tuple-element.114), channel_id=1, source_target_pairs={{0,96},{8,104},{16,112},{24,120},{32,0},{40,8},{48,16},{56,24},{64... | collective-permute-start | bytes 1572872 | tf_op jit(solution)/shard_map/ppermute | solution.py:36
  299.8 22.9 %collective-permute-start.18 = (bf16[4,64,1024]{2,1,0:T(8,128)(2,1)S(1)}, bf16[4,64,1024]{2,1,0:T(8,128)(2,1)}, u32[]{:S(2)}, u32[]{:S(2)}) collective-permute-start(bf16[4,64,1024]{2,1,0:T(8,128)(2,1)S(1)} %get-tuple-element.113), channel_id=1, source_target_pairs={{0,64},{8,72},{16,80},{24,88},{32,96},{40,104},{48,112},{56,120},{... | collective-permute-start | bytes 1572872 | tf_op jit(solution)/shard_map/ppermute | solution.py:36
  304.4 20.0 %collective-permute-start.22 = (bf16[4,64,1024]{2,1,0:T(8,128)(2,1)}, bf16[4,64,1024]{2,1,0:T(8,128)(2,1)}, u32[]{:S(2)}, u32[]{:S(2)}) collective-permute-start(bf16[4,64,1024]{2,1,0:T(8,128)(2,1)} %get-tuple-element.115), channel_id=1, source_target_pairs={{0,8},{8,16},{16,24},{24,0},{32,40},{40,48},{48,56},{56,32},{64,72... | collective-permute-start | bytes 1572872 | tf_op jit(solution)/shard_map/ppermute | solution.py:32
  304.4 23.0 %collective-permute-start.23 = (bf16[4,64,1024]{2,1,0:T(8,128)(2,1)S(1)}, bf16[4,64,1024]{2,1,0:T(8,128)(2,1)}, u32[]{:S(2)}, u32[]{:S(2)}) collective-permute-start(bf16[4,64,1024]{2,1,0:T(8,128)(2,1)S(1)} %get-tuple-element.116), channel_id=1, source_target_pairs={{0,24},{8,0},{16,8},{24,16},{32,56},{40,32},{48,40},{56,48},{64,88... | collective-permute-start | bytes 1572872 | tf_op jit(solution)/shard_map/ppermute | solution.py:32
  319.2 16.5 %collective-permute-start.24 = (bf16[4,64,1024]{2,1,0:T(8,128)(2,1)S(1)}, bf16[4,64,1024]{2,1,0:T(8,128)(2,1)S(1)}, u32[]{:S(2)}, u32[]{:S(2)}) collective-permute-start(bf16[4,64,1024]{2,1,0:T(8,128)(2,1)S(1)} %get-tuple-element.117), channel_id=1, source_target_pairs={{0,16},{8,24},{16,0},{24,8},{32,48},{40,56},{48,32},{56,40},{64,80... | collective-permute-start | bytes 1572872 | tf_op jit(solution)/shard_map/ppermute | solution.py:32
  321.1 27.8 %collective-permute-start.46 = (bf16[4,64,1152]{2,1,0:T(8,128)(2,1)S(1)}, bf16[4,64,1152]{2,1,0:T(8,128)(2,1)S(1)}, u32[]{:S(2)}, u32[]{:S(2)}) collective-permute-start(bf16[4,64,1152]{2,1,0:T(8,128)(2,1)S(1)} %get-tuple-element.103), channel_id=1, source_target_pairs={{0,8},{8,16},{16,24},{24,0},{32,40},{40,48},{48,56},{56,32},{64,72... | collective-permute-start | bytes 1769480 | tf_op jit(solution)/shard_map/ppermute | solution.py:32
  322.7 30.4 %collective-permute-start.47 = (bf16[4,64,1152]{2,1,0:T(8,128)(2,1)S(1)}, bf16[4,64,1152]{2,1,0:T(8,128)(2,1)S(1)}, u32[]{:S(2)}, u32[]{:S(2)}) collective-permute-start(bf16[4,64,1152]{2,1,0:T(8,128)(2,1)S(1)} %get-tuple-element.104), channel_id=1, source_target_pairs={{0,24},{8,0},{16,8},{24,16},{32,56},{40,32},{48,40},{56,48},{64,88... | collective-permute-start | bytes 1769480 | tf_op jit(solution)/shard_map/ppermute | solution.py:32
  324.4 29.3 %collective-permute-start.48 = (bf16[4,64,1152]{2,1,0:T(8,128)(2,1)S(1)}, bf16[4,64,1152]{2,1,0:T(8,128)(2,1)S(1)}, u32[]{:S(2)}, u32[]{:S(2)}) collective-permute-start(bf16[4,64,1152]{2,1,0:T(8,128)(2,1)S(1)} %get-tuple-element.105), channel_id=1, source_target_pairs={{0,16},{8,24},{16,0},{24,8},{32,48},{40,56},{48,32},{56,40},{64,80... | collective-permute-start | bytes 1769480 | tf_op jit(solution)/shard_map/ppermute | solution.py:32
  327.4 29.9 %collective-permute-start.40 = (bf16[4,64,1152]{2,1,0:T(8,128)(2,1)S(1)}, bf16[4,64,1152]{2,1,0:T(8,128)(2,1)S(1)}, u32[]{:S(2)}, u32[]{:S(2)}) collective-permute-start(bf16[4,64,1152]{2,1,0:T(8,128)(2,1)S(1)} %get-tuple-element.106), channel_id=1, source_target_pairs={{0,32},{8,40},{16,48},{24,56},{32,64},{40,72},{48,80},{56,88},{64,... | collective-permute-start | bytes 1769480 | tf_op jit(solution)/shard_map/ppermute | solution.py:36
  335.7 23.2 %collective-permute-start.41 = (bf16[4,64,1152]{2,1,0:T(8,128)(2,1)S(1)}, bf16[4,64,1152]{2,1,0:T(8,128)(2,1)S(1)}, u32[]{:S(2)}, u32[]{:S(2)}) collective-permute-start(bf16[4,64,1152]{2,1,0:T(8,128)(2,1)S(1)} %get-tuple-element.108), channel_id=1, source_target_pairs={{0,96},{8,104},{16,112},{24,120},{32,0},{40,8},{48,16},{56,24},{64... | collective-permute-start | bytes 1769480 | tf_op jit(solution)/shard_map/ppermute | solution.py:36
  348.9 11.5 %collective-permute-start.42 = (bf16[4,64,1152]{2,1,0:T(8,128)(2,1)S(1)}, bf16[4,64,1152]{2,1,0:T(8,128)(2,1)S(1)}, u32[]{:S(2)}, u32[]{:S(2)}) collective-permute-start(bf16[4,64,1152]{2,1,0:T(8,128)(2,1)S(1)} %get-tuple-element.107), channel_id=1, source_target_pairs={{0,64},{8,72},{16,80},{24,88},{32,96},{40,104},{48,112},{56,120},{... | collective-permute-start | bytes 1769480 | tf_op jit(solution)/shard_map/ppermute | solution.py:36
  353.1 11.4 %collective-permute-start.19 = (bf16[64,1024]{1,0:T(8,128)(2,1)S(1)}, bf16[64,1024]{1,0:T(8,128)(2,1)S(1)}, u32[]{:S(2)}, u32[]{:S(2)}) collective-permute-start(bf16[64,1024]{1,0:T(8,128)(2,1)S(1)} %get-tuple-element.137), channel_id=1, source_target_pairs={{0,8},{8,16},{16,24},{24,0},{32,40},{40,48},{48,56},{56,32},{64,72... | collective-permute-start | bytes 393224 | tf_op jit(solution)/shard_map/ppermute | solution.py:32
  353.7 10.9 %collective-permute-start.20 = (bf16[64,1024]{1,0:T(8,128)(2,1)S(1)}, bf16[64,1024]{1,0:T(8,128)(2,1)S(1)}, u32[]{:S(2)}, u32[]{:S(2)}) collective-permute-start(bf16[64,1024]{1,0:T(8,128)(2,1)S(1)} %get-tuple-element.139), channel_id=1, source_target_pairs={{0,24},{8,0},{16,8},{24,16},{32,56},{40,32},{48,40},{56,48},{64,88... | collective-permute-start | bytes 393224 | tf_op jit(solution)/shard_map/ppermute | solution.py:32
  357.3 8.1 %collective-permute-start.21 = (bf16[64,1024]{1,0:T(8,128)(2,1)S(1)}, bf16[64,1024]{1,0:T(8,128)(2,1)S(1)}, u32[]{:S(2)}, u32[]{:S(2)}) collective-permute-start(bf16[64,1024]{1,0:T(8,128)(2,1)S(1)} %get-tuple-element.138), channel_id=1, source_target_pairs={{0,16},{8,24},{16,0},{24,8},{32,48},{40,56},{48,32},{56,40},{64,80... | collective-permute-start | bytes 393224 | tf_op jit(solution)/shard_map/ppermute | solution.py:32
  358.9 9.1 %collective-permute-start.25 = (bf16[64,1024]{1,0:T(8,128)(2,1)S(1)}, bf16[64,1024]{1,0:T(8,128)(2,1)S(1)}, u32[]{:S(2)}, u32[]{:S(2)}) collective-permute-start(bf16[64,1024]{1,0:T(8,128)(2,1)S(1)} %get-tuple-element.140), channel_id=1, source_target_pairs={{0,32},{8,40},{16,48},{24,56},{32,64},{40,72},{48,80},{56,88},{64,... | collective-permute-start | bytes 393224 | tf_op jit(solution)/shard_map/ppermute | solution.py:36
  360.4 10.0 %collective-permute-start.26 = (bf16[64,1024]{1,0:T(8,128)(2,1)S(1)}, bf16[64,1024]{1,0:T(8,128)(2,1)S(1)}, u32[]{:S(2)}, u32[]{:S(2)}) collective-permute-start(bf16[64,1024]{1,0:T(8,128)(2,1)S(1)} %get-tuple-element.142), channel_id=1, source_target_pairs={{0,96},{8,104},{16,112},{24,120},{32,0},{40,8},{48,16},{56,24},{64... | collective-permute-start | bytes 393224 | tf_op jit(solution)/shard_map/ppermute | solution.py:36
  364.5 6.7 %collective-permute-start.27 = (bf16[64,1024]{1,0:T(8,128)(2,1)S(1)}, bf16[64,1024]{1,0:T(8,128)(2,1)S(1)}, u32[]{:S(2)}, u32[]{:S(2)}) collective-permute-start(bf16[64,1024]{1,0:T(8,128)(2,1)S(1)} %get-tuple-element.141), channel_id=1, source_target_pairs={{0,64},{8,72},{16,80},{24,88},{32,96},{40,104},{48,112},{56,120},{... | collective-permute-start | bytes 393224 | tf_op jit(solution)/shard_map/ppermute | solution.py:36
  364.6 9.0 %collective-permute-start.49 = (bf16[64,1152]{1,0:T(8,128)(2,1)S(1)}, bf16[64,1152]{1,0:T(8,128)(2,1)S(1)}, u32[]{:S(2)}, u32[]{:S(2)}) collective-permute-start(bf16[64,1152]{1,0:T(8,128)(2,1)S(1)} %get-tuple-element.130), channel_id=1, source_target_pairs={{0,32},{8,40},{16,48},{24,56},{32,64},{40,72},{48,80},{56,88},{64,... | collective-permute-start | bytes 442376 | tf_op jit(solution)/shard_map/ppermute | solution.py:36
  365.5 9.5 %collective-permute-start.50 = (bf16[64,1152]{1,0:T(8,128)(2,1)S(1)}, bf16[64,1152]{1,0:T(8,128)(2,1)S(1)}, u32[]{:S(2)}, u32[]{:S(2)}) collective-permute-start(bf16[64,1152]{1,0:T(8,128)(2,1)S(1)} %get-tuple-element.132), channel_id=1, source_target_pairs={{0,96},{8,104},{16,112},{24,120},{32,0},{40,8},{48,16},{56,24},{64... | collective-permute-start | bytes 442376 | tf_op jit(solution)/shard_map/ppermute | solution.py:36
  368.0 7.0 %collective-permute-start.51 = (bf16[64,1152]{1,0:T(8,128)(2,1)S(1)}, bf16[64,1152]{1,0:T(8,128)(2,1)S(1)}, u32[]{:S(2)}, u32[]{:S(2)}) collective-permute-start(bf16[64,1152]{1,0:T(8,128)(2,1)S(1)} %get-tuple-element.131), channel_id=1, source_target_pairs={{0,64},{8,72},{16,80},{24,88},{32,96},{40,104},{48,112},{56,120},{... | collective-permute-start | bytes 442376 | tf_op jit(solution)/shard_map/ppermute | solution.py:36
  370.3 6.4 %collective-permute-start.43 = (bf16[64,1152]{1,0:T(8,128)(2,1)S(1)}, bf16[64,1152]{1,0:T(8,128)(2,1)S(1)}, u32[]{:S(2)}, u32[]{:S(2)}) collective-permute-start(bf16[64,1152]{1,0:T(8,128)(2,1)S(1)} %get-tuple-element.133), channel_id=1, source_target_pairs={{0,8},{8,16},{16,24},{24,0},{32,40},{40,48},{48,56},{56,32},{64,72... | collective-permute-start | bytes 442376 | tf_op jit(solution)/shard_map/ppermute | solution.py:32
  373.6 6.7 %collective-permute-start.45 = (bf16[64,1152]{1,0:T(8,128)(2,1)S(1)}, bf16[64,1152]{1,0:T(8,128)(2,1)S(1)}, u32[]{:S(2)}, u32[]{:S(2)}) collective-permute-start(bf16[64,1152]{1,0:T(8,128)(2,1)S(1)} %get-tuple-element.134), channel_id=1, source_target_pairs={{0,16},{8,24},{16,0},{24,8},{32,48},{40,56},{48,32},{56,40},{64,80... | collective-permute-start | bytes 442376 | tf_op jit(solution)/shard_map/ppermute | solution.py:32
  384.8 8.8 %collective-permute-start.52 = (bf16[128,1024]{1,0:T(8,128)(2,1)S(1)}, bf16[128,1024]{1,0:T(8,128)(2,1)S(1)}, u32[]{:S(2)}, u32[]{:S(2)}) collective-permute-start(bf16[128,1024]{1,0:T(8,128)(2,1)S(1)} %get-tuple-element.93), channel_id=1, source_target_pairs={{0,2},{1,3},{2,4},{3,5},{4,6},{5,7},{6,0},{7,1},{8,10},{9,11},{10,... | collective-permute-start | bytes 786440 | tf_op jit(solution)/shard_map/ppermute | solution.py:24
  388.2 6.4 %collective-permute-start.53 = (bf16[128,1024]{1,0:T(8,128)(2,1)S(1)}, bf16[128,1024]{1,0:T(8,128)(2,1)S(1)}, u32[]{:S(2)}, u32[]{:S(2)}) collective-permute-start(bf16[128,1024]{1,0:T(8,128)(2,1)S(1)} %get-tuple-element.93), channel_id=1, source_target_pairs={{0,6},{1,7},{2,0},{3,1},{4,2},{5,3},{6,4},{7,5},{8,14},{9,15},{10,... | collective-permute-start | bytes 786440 | tf_op jit(solution)/shard_map/ppermute | solution.py:24
  389.3 8.6 %collective-permute-start.54 = (bf16[128,1024]{1,0:T(8,128)(2,1)S(1)}, bf16[128,1024]{1,0:T(8,128)(2,1)S(1)}, u32[]{:S(2)}, u32[]{:S(2)}) collective-permute-start(bf16[128,1024]{1,0:T(8,128)(2,1)S(1)} %get-tuple-element.93), channel_id=1, source_target_pairs={{0,4},{1,5},{2,6},{3,7},{4,0},{5,1},{6,2},{7,3},{8,12},{9,13},{10,... | collective-permute-start | bytes 786440 | tf_op jit(solution)/shard_map/ppermute | solution.py:24
  400.2 15.0 %all-to-all-start.2 = ((bf16[8,128,128]{2,1,0:T(8,128)(2,1)}), bf16[8,128,128]{2,1,0:T(8,128)(2,1)S(1)}, u32[]{:S(2)}, u32[]{:S(2)}) async-start(bf16[8,128,128]{2,1,0:T(8,128)(2,1)} %bitcast.428), calls=%async_computation.2 | async-start | bytes 524288 | tf_op jit(solution)/shard_map/all_to_all | solution.py:95
  403.7 121.3 %all-reduce.2.cloned.1.call-start = ((), (), s32[]{:S(2)}) async-start(), calls=%async_computation.10 | async-start | bytes 524288 | tf_op jit(solution)/shard_map/psum | solution.py:321
  407.6 120.7 %reduce-scatter.8.cloned.1.call-start = ((), (), s32[]{:S(2)}) async-start(), calls=%async_computation.12 | async-start | bytes 2359296 | tf_op jit(solution)/shard_map/reduce_scatter | solution.py:272
  415.1 147.6 %reduce-scatter.4.cloned.1.call-start = ((), (), s32[]{:S(2)}) async-start(), calls=%async_computation.9 | async-start | bytes 2359296 | tf_op jit(solution)/shard_map/reduce_scatter | solution.py:314
  439.9 162.2 %reduce-scatter.6.cloned.1.call-start = ((), (), s32[]{:S(2)}) async-start(), calls=%async_computation.11 | async-start | bytes 4718592 | tf_op jit(solution)/shard_map/reduce_scatter | solution.py:266
  (62 other events, 579.4 us)
Sparse Core Ops, SparseCore 0:
  9.7 27.6 all-gather.5
  39.1 28.5 all-gather.9
  70.0 32.3 all-gather.7
  408.0 83.1 all-reduce.1
  493.6 34.6 reduce-scatter.7
  530.7 32.0 reduce-scatter.3
  565.2 36.8 reduce-scatter.5

commit v2 on v1

--- a/solution.py
+++ b/solution.py
@@ -1,6 +1,8 @@
 import jax
 import jax.numpy as jnp
 from jax import lax
+from jax.experimental import pallas as pl
+from jax.experimental.pallas import tpu as pltpu
 from jax.sharding import PartitionSpec as P
 
 HEAD_DIM = 64
@@ -77,7 +79,7 @@
     return total
 
 
-def scatter_expert(p):
+def scatter_expert(p, beside=None):
     e = lax.axis_index("expert")
     y, z = e // 4, e % 4
     n = p.shape[1] // 2
@@ -86,9 +88,159 @@
     b = jnp.swapaxes(p[:, :, n:], 0, 1)
     a = ring_sum(shift_y, a, y).astype(bf16)
     b = ring_sum(shift_z, b, z).astype(bf16)
+    if beside is not None:
+        a, b, beside = lax.optimization_barrier((a, b, beside))
     a = ring_sum(shift_z, a, z)
     b = ring_sum(shift_y, b, y)
-    return jnp.concatenate([a, b], axis=0)
+    return jnp.concatenate([a, b], axis=0), beside
+
+
+def after(v, first):
+    return lax.optimization_barrier((v, first))[0]
+
+
+def dot(a, b, dims=((1,), (0,))):
+    return lax.dot_general(a, b, (dims, ((), ())), preferred_element_type=f32)
+
+
+NT = ((1,), (1,))
+TN = ((0,), (0,))
+
+
+def expert_kernel(
+    e_ref, rows, cot, member, pick, pick_t, router, w, inputs, hidden, dboth, dres, mix, drows
+):
+    e = e_ref[0]
+    lane = lax.broadcasted_iota(jnp.int32, (1, 128), 1)
+    gates = []
+    for b in range(4):
+        has = member[b] > 0
+        low = jnp.where(has, dot(rows[b], router[...]), -1e30)
+        top = jnp.max(low, axis=-1, keepdims=True)
+        expo = jnp.where(has, jnp.exp(low - top), 0.0)
+        soft = expo / jnp.sum(expo, axis=-1, keepdims=True)
+        high = soft.astype(bf16)
+        rest = soft - high.astype(f32)
+        mid = rest.astype(bf16)
+        last = (rest - mid.astype(f32)).astype(bf16)
+        gates.append(dot(pick[b], high) + dot(pick[b], mid) + dot(pick[b], last))
+    x_slots = [dot(pick[b], rows[b]).astype(bf16) for b in range(4)]
+    c_slots = [dot(pick[b], cot[b, :LP]) for b in range(4)]
+    weighted, dassign, extra = [], [], []
+    for j in range(2):
+        part = slice(j * SLOTS, (j + 1) * SLOTS)
+        x_in = jnp.concatenate([v[part] for v in x_slots], axis=0)
+        c_in = jnp.concatenate([v[part] for v in c_slots], axis=0)
+        gate_rows = jnp.concatenate([v[part] for v in gates], axis=0)
+        gate_in = jnp.sum(jnp.where(lane == 2 * e + j, gate_rows, 0.0), axis=-1, keepdims=True)
+        w_g = w[:, j * 1024 : j * 1024 + FF]
+        w_u = w[:, j * 1024 + FF : (j + 1) * 1024]
+        w_d = w[:, 2048 + j * FF : 2048 + (j + 1) * FF]
+        gate_val = dot(x_in, w_g)
+        up_val = dot(x_in, w_u)
+        sig = 1.0 / (1.0 + jnp.exp(-gate_val))
+        activated = gate_val * sig
+        hid = (activated * up_val).astype(bf16)
+        result = dot(hid, w_d, NT).astype(bf16).astype(f32)
+        dgate = jnp.sum(result * c_in, axis=-1, keepdims=True)
+        dresult = (gate_in * c_in).astype(bf16)
+        dhidden = dot(dresult, w_d)
+        dgate_val = (dhidden * up_val * sig * (1.0 + gate_val * (1.0 - sig))).astype(bf16)
+        dup_val = (dhidden * activated).astype(bf16)
+        da = (dot(dgate_val, w_g, NT) + dot(dup_val, w_u, NT)).astype(bf16)
+        weighted.append((gate_in * result).astype(bf16))
+        dassign.append(da)
+        dg_high = dgate.astype(bf16).astype(f32)
+        dg_low = dgate - dg_high
+        extra.append(
+            (
+                jnp.where(lane == 2 * e + j, dg_high, 0.0)
+                + jnp.where(lane == EXPERTS + 2 * e + j, dg_low, 0.0)
+            ).astype(bf16)
+        )
+        inputs[j] = x_in
+        hidden[j] = hid
+        dboth[j, :, :FF] = dgate_val
+        dboth[j, :, FF:] = dup_val
+        dres[j] = dresult
+    for b in range(4):
+        part = slice(b * SLOTS, (b + 1) * SLOTS)
+        mix[b] = dot(
+            pick_t[b], jnp.concatenate([weighted[0][part], weighted[1][part]], axis=0)
+        ).astype(bf16)
+        drows[b, :, :D] = dot(
+            pick_t[b], jnp.concatenate([dassign[0][part], dassign[1][part]], axis=0)
+        ).astype(bf16)
+        drows[b, :, D:] = dot(
+            pick_t[b], jnp.concatenate([extra[0][part], extra[1][part]], axis=0)
+        ).astype(bf16)
+
+
+def experts(e, rows_all, cot_all, member, pick, pick_t, router, w):
+    rows = NE * SLOTS
+    step = rows // 4
+    return pl.pallas_call(
+        expert_kernel,
+        grid=(4,),
+        in_specs=[
+            pl.BlockSpec(memory_space=pltpu.SMEM),
+            pl.BlockSpec((4, LP, D), lambda i: (i, 0, 0)),
+            pl.BlockSpec((4, cot_all.shape[1], D), lambda i: (i, 0, 0)),
+            pl.BlockSpec((4, LP, 128), lambda i: (i, 0, 0)),
+            pl.BlockSpec((4, 128, LP), lambda i: (i, 0, 0)),
+            pl.BlockSpec((4, LP, 128), lambda i: (i, 0, 0)),
+            pl.BlockSpec((D, 128), lambda i: (0, 0)),
+            pl.BlockSpec((D, 3072), lambda i: (0, 0), pipeline_mode=pl.Buffered(1)),
+        ],
+        out_specs=[
+            pl.BlockSpec((2, step, D), lambda i: (0, i, 0)),
+            pl.BlockSpec((2, step, FF), lambda i: (0, i, 0)),
+            pl.BlockSpec((2, step, 2 * FF), lambda i: (0, i, 0)),
+            pl.BlockSpec((2, step, D), lambda i: (0, i, 0)),
+            pl.BlockSpec((4, LP, D), lambda i: (i, 0, 0)),
+            pl.BlockSpec((4, LP, D + 128), lambda i: (i, 0, 0)),
+        ],
+        out_shape=[
+            jax.ShapeDtypeStruct((2, rows, D), bf16),
+            jax.ShapeDtypeStruct((2, rows, FF), bf16),
+            jax.ShapeDtypeStruct((2, rows, 2 * FF), bf16),
+            jax.ShapeDtypeStruct((2, rows, D), bf16),
+            jax.ShapeDtypeStruct((NE, LP, D), bf16),
+            jax.ShapeDtypeStruct((NE, LP, D + 128), bf16),
+        ],
+        compiler_params=pltpu.CompilerParams(vmem_limit_bytes=56 * 2**20),
+        cost_estimate=pl.CostEstimate(
+            flops=14 * 10**9, bytes_accessed=30 * 2**20, transcendentals=10**6
+        ),
+        name="experts",
+    )(e, rows_all, cot_all, member, pick, pick_t, router, w)
+
+
+def weight_kernel(inputs, dres, dboth, hidden, out):
+    for j in range(2):
+        out[:, j * 1024 : (j + 1) * 1024] = dot(inputs[j], dboth[j], TN).astype(bf16)
+        out[:, 2048 + j * FF : 2048 + (j + 1) * FF] = dot(dres[j], hidden[j], TN).astype(bf16)
+
+
+def expert_weights(inputs, dres, dboth, hidden):
+    rows = NE * SLOTS
+    return pl.pallas_call(
+        weight_kernel,
+        grid=(4,),
+        in_specs=[
+            pl.BlockSpec((2, rows, 256), lambda i: (0, 0, i)),
+            pl.BlockSpec((2, rows, 256), lambda i: (0, 0, i)),
+            pl.BlockSpec((2, rows, 2 * FF), lambda i: (0, 0, 0)),
+            pl.BlockSpec((2, rows, FF), lambda i: (0, 0, 0)),
+        ],
+        out_specs=pl.BlockSpec((256, 3072), lambda i: (i, 0)),
+        out_shape=jax.ShapeDtypeStruct((D, 3072), bf16),
+        compiler_params=pltpu.CompilerParams(vmem_limit_bytes=56 * 2**20),
+        cost_estimate=pl.CostEstimate(
+            flops=7 * 10**9, bytes_accessed=20 * 2**20, transcendentals=0
+        ),
+        name="expert_weights",
+    )(inputs, dres, dboth, hidden)
 
 
 def swap_fsdp(v):
@@ -158,39 +310,45 @@
         axis=0,
     )
     payload = jnp.concatenate([columns, jnp.broadcast_to(extra[None], (NF, 32, 256))], axis=1)
+    x_all = lax.all_gather(x_own, "fsdp", axis=0, tiled=True)
     got = swap_fsdp(payload)
-    x_all = gather_fsdp(x_own).reshape(LENGTH, D)
     w_qkv = got[:, :LP].reshape(D, 256)
     gain_one = got[:, LP, :128].reshape(D).astype(f32)
     gain_two = got[:, LP, 128:].reshape(D).astype(f32)
     router = got[:, LP + 1 : LP + 17].reshape(D, EXPERTS)
-    w_out = lax.all_gather(w_output, "fsdp", axis=0, tiled=True)
-    w_gu = lax.all_gather(jnp.concatenate([w_gate, w_up], axis=-1), "fsdp", axis=0)
-    w_gu = w_gu.swapaxes(0, 1).reshape(2, D, 2 * FF)
-    w_dn = lax.all_gather(w_down, "fsdp", axis=0)
-    w_dn = w_dn.transpose(1, 2, 0, 3).reshape(2, FF, D)
-    cot_all = gather_expert(cot_own)
-    routes_all = lax.all_gather(routes[0], "expert", axis=0)
+    w_out = lax.all_gather(after(w_output, x_all), "fsdp", axis=0, tiled=True)
+    w_own = jnp.concatenate(
+        [w_gate[0], w_up[0], w_gate[1], w_up[1], w_down[0].T, w_down[1].T], axis=1
+    )
+    w_exp = lax.all_gather(after(w_own, w_out), "fsdp", axis=0, tiled=True)
+    cot_all = gather_expert(
+        jnp.concatenate(
+            [cot_own, routes[0].astype(bf16).reshape(1, D), jnp.zeros((15, D), bf16)], axis=0
+        )
+    )
+    routes_all = cot_all[:, LP].reshape(NE, LP, 8).astype(jnp.int32)
 
     own_ids = 2 * e + jnp.arange(2, dtype=jnp.int32)
     chosen_own = jnp.any(routes_all[:, :, :, None] == own_ids, axis=2)
     before = (jnp.arange(LP)[:, None] > jnp.arange(LP)[None, :]).astype(bf16)
     rank = jnp.einsum(
-        "ts,bsj->jbt", before, chosen_own.astype(bf16), preferred_element_type=f32
-    )
-    member_t = chosen_own.transpose(2, 0, 1)
+        "ts,bsj->bjt", before, chosen_own.astype(bf16), preferred_element_type=f32
+    )
+    slot_ids = jnp.arange(SLOTS, dtype=f32)
+    member_t = chosen_own.swapaxes(1, 2)
     pick = (
-        (rank[:, :, None, :] == jnp.arange(SLOTS, dtype=f32)[:, None]) & member_t[:, :, None, :]
+        ((rank[:, :, None, :] == slot_ids[:, None]) & member_t[:, :, None, :])
+        .astype(bf16)
+        .reshape(NE, 2 * SLOTS, LP)
+    )
+    pick_t = pick.swapaxes(1, 2)
+    member_all = jnp.any(
+        routes_all[:, :, :, None] == jnp.arange(128, dtype=jnp.int32), axis=2
     ).astype(bf16)
-    member_all = jnp.any(
-        routes_all[:, :, :, None] == jnp.arange(EXPERTS, dtype=jnp.int32), axis=2
-    )
     member_own = jnp.any(
         routes[0][:, :, None] == jnp.arange(EXPERTS, dtype=jnp.int32), axis=1
     )
-    cot_slots = jnp.einsum("jbst,btd->jbsd", pick, cot_all, preferred_element_type=bf16).reshape(
-        2, NE * SLOTS, D
-    )
+    router_wide = jnp.concatenate([router, jnp.zeros((D, 128 - EXPERTS), bf16)], axis=1)
 
     x_full = x_all.astype(f32)
     r_one = lax.rsqrt(jnp.mean(x_full * x_full, axis=-1, keepdims=True) + epsilon)
@@ -219,62 +377,18 @@
     normed_two = (after_attn * r_two * gain_two).astype(bf16)
 
     rows_all = gather_expert(normed_two)
-    logits_all = jnp.einsum("btd,de->bte", rows_all, router, preferred_element_type=f32)
-    gates_all = masked_gates(logits_all, member_all)
-    gates_pair = lax.dynamic_slice_in_dim(gates_all, 2 * e, 2, axis=2).transpose(2, 0, 1)
-    pick_f = pick.astype(f32)
-    gate_slots = jnp.sum(pick_f * gates_pair[:, :, None, :], axis=-1).reshape(2, NE * SLOTS, 1)
-    inputs = jnp.einsum("jbst,btd->jbsd", pick, rows_all, preferred_element_type=bf16).reshape(
-        2, NE * SLOTS, D
-    )
-    both = jnp.einsum("jrd,jdf->jrf", inputs, w_gu, preferred_element_type=f32)
-    gate_val, up_val = both[..., :FF], both[..., FF:]
-    sig = jax.nn.sigmoid(gate_val)
-    activated = gate_val * sig
-    hidden = (activated * up_val).astype(bf16)
-    result = jnp.einsum("jrf,jfd->jrd", hidden, w_dn, preferred_element_type=f32).astype(bf16)
-    cot_f = cot_slots.astype(f32)
-    result_f = result.astype(f32)
-    dgate_slots = jnp.sum(result_f * cot_f, axis=-1).reshape(2, NE, SLOTS)
-    weighted = (gate_slots * result_f).astype(bf16).reshape(2, NE, SLOTS, D)
-    mix_part = jnp.einsum("jbst,jbsd->btd", pick, weighted, preferred_element_type=f32).astype(
-        bf16
-    )
-    dresult = (gate_slots * cot_f).astype(bf16)
-    dhidden = jnp.einsum("jrd,jfd->jrf", dresult, w_dn, preferred_element_type=f32)
-    dgate_val = (dhidden * up_val * sig * (1.0 + gate_val * (1.0 - sig))).astype(bf16)
-    dup_val = (dhidden * activated).astype(bf16)
-    dboth = jnp.concatenate([dgate_val, dup_val], axis=-1)
-    dassign = jnp.einsum("jrf,jdf->jrd", dboth, w_gu, preferred_element_type=f32).astype(bf16)
-    dassign = dassign.reshape(2, NE, SLOTS, D)
-    drows_part = jnp.einsum("jbst,jbsd->btd", pick, dassign, preferred_element_type=f32)
-    dgate_tok = jnp.sum(pick_f * dgate_slots[..., None], axis=2)
-    dgate_high = dgate_tok.astype(bf16).astype(f32)
-    dgate_low = dgate_tok - dgate_high
-    lanes = jnp.arange(128)
-    extra_cols = jnp.zeros((NE, LP, 128), f32)
-    for j in range(2):
-        extra_cols = extra_cols + jnp.where(lanes == 2 * e + j, dgate_high[j][..., None], 0.0)
-        extra_cols = extra_cols + jnp.where(
-            lanes == EXPERTS + 2 * e + j, dgate_low[j][..., None], 0.0
-        )
-    drows_send = jnp.concatenate([drows_part, extra_cols], axis=-1).astype(bf16)
-    drows = scatter_expert(drows_send)
-
-    grad_gu_part = jnp.einsum("jrd,jrf->jdf", inputs, dboth, preferred_element_type=f32)
-    grad_dn_part = jnp.einsum("jrf,jrd->jfd", hidden, dresult, preferred_element_type=f32)
-    grad_gu = lax.psum_scatter(
-        grad_gu_part.astype(bf16).reshape(2, NF, LP, 2 * FF).swapaxes(0, 1),
-        "fsdp",
-        scatter_dimension=0,
+    inputs, hidden, dboth, dres, mix_part, drows_part = experts(
+        e[None], rows_all, cot_all, member_all, pick, pick_t, router_wide, w_exp
+    )
+    grad_exp = expert_weights(inputs, dres, dboth, hidden)
+    drows, grad_exp = scatter_expert(drows_part, grad_exp)
+    grad_exp = lax.psum_scatter(
+        grad_exp.reshape(NF, LP, 3072), "fsdp", scatter_dimension=0
     ).astype(f32)
-    grad_gate, grad_up = grad_gu[..., :FF], grad_gu[..., FF:]
-    grad_down = lax.psum_scatter(
-        grad_dn_part.astype(bf16).reshape(2, FF, NF, LP).transpose(2, 0, 1, 3),
-        "fsdp",
-        scatter_dimension=0,
-    ).astype(f32)
-    mix = scatter_expert(mix_part)
+    grad_gate = jnp.stack([grad_exp[:, :512], grad_exp[:, 1024:1536]])
+    grad_up = jnp.stack([grad_exp[:, 512:1024], grad_exp[:, 1536:2048]])
+    grad_down = jnp.stack([grad_exp[:, 2048:2560].T, grad_exp[:, 2560:].T])
+    mix, _ = scatter_expert(after(mix_part, drows))
     layer_output = (after_attn + mix).astype(bf16)
 
     logits = jnp.dot(normed_two, router, preferred_element_type=f32)
@@ -293,7 +407,7 @@
     dattended = swap_fsdp(dattended_own.reshape(LP, NF, 128).swapaxes(0, 1)).reshape(
         LENGTH, 2, HEAD_DIM
     )
-    dbranch_all = gather_fsdp(dbranch).reshape(LENGTH, D)
+    dbranch_all = lax.all_gather(dbranch, "fsdp", axis=0, tiled=True)
     part_router = jnp.einsum(
         "td,te->de", normed_two.astype(f32), dlogits, precision=highest
     )
@@ -318,7 +432,14 @@
     grad_input = (dafter + dinput_norm).astype(bf16)
 
     part_output = jnp.einsum("ti,td->id", attended, dbranch_all, preferred_element_type=f32)
-    grad_output = lax.psum(part_output.astype(bf16), "expert").astype(f32)
+    part_output = lax.all_to_all(
+        part_output.astype(bf16).reshape(NE, LP // NE, D),
+        "expert",
+        split_axis=0,
+        concat_axis=0,
+        tiled=True,
+    )
+    chunk_output = jnp.sum(part_output.astype(f32), axis=0)
     small = jnp.concatenate(
         [
             part_qkv,
@@ -329,16 +450,27 @@
         ],
         axis=-1,
     ).astype(bf16)
-    traded = swap_fsdp(small.reshape(NF, LP, 384))
-    heads_part = traded[:, :, :256].swapaxes(0, 1)
-    rest_part = jnp.sum(traded[:, :, 256:].astype(f32), axis=0).astype(bf16)
-    total_part = jnp.concatenate([heads_part.reshape(LP, 2048), rest_part], axis=-1)
-    chunk = lax.all_to_all(
-        total_part.reshape(NE, LP // NE, 2176), "expert", split_axis=0, concat_axis=0, tiled=True
-    )
-    chunk = jnp.sum(chunk.astype(f32), axis=0).astype(bf16)
-    total_sum = lax.all_gather(chunk, "expert", axis=0, tiled=True).astype(f32)
+    small = small.reshape(NF, NE, LP // NE, 384).swapaxes(0, 1).reshape(NF * NE, LP // NE, 384)
+    small = lax.all_to_all(small, ("expert", "fsdp"), split_axis=0, concat_axis=0, tiled=True)
+    small = jnp.sum(small.reshape(NE, NF, LP // NE, 384).astype(f32), axis=0)
+    chunk = jnp.concatenate(
+        [
+            small[:, :, :256].swapaxes(0, 1).reshape(LP // NE, 2048),
+            jnp.sum(small[:, :, 256:], axis=0),
+            chunk_output,
+        ],
+        axis=-1,
+    ).astype(bf16)
+    total_sum = lax.all_to_all(
+        jnp.broadcast_to(chunk[None], (NE,) + chunk.shape),
+        "expert",
+        split_axis=0,
+        concat_axis=0,
+        tiled=True,
+    ).reshape(LP, 3200)
+    total_sum = total_sum.astype(f32)
     heads_sum = total_sum[:, :2048].reshape(LP, NF, 256)
+    grad_output = total_sum[:, 2176:]
     grad_query = heads_sum[:, :, :128].reshape(LP, 1024)
     grad_key = heads_sum[:, :, 128:192].reshape(LP, 512)
     grad_value = heads_sum[:, :, 192:].reshape(LP, 512)

time: 621 us -> 437 us (0.70)
  blocking collectives: 78.9 us -> 0 us
  matrix products: 97.9 us -> 33.1 us
  local copies, waits for them, and re-layouts: 123 us -> 72.7 us
  Pallas kernels: 0 us -> 45.3 us
  waiting for transfers between devices: 134 us -> 114 us
  other arithmetic: 54.5 us -> 39.6 us
    dot_general x11 -> x1, matrix products: 52.7 us -> 0.14 us  [local(): jnp.einsum('ts,bsj->bjt', before, chosen_own.astype(bf16), preferred_elem...]
    all_gather x2 -> x0, blocking collectives: 46.2 us -> none  [the longest x1 23.6 us: local(): routes_all = lax.all_gather(routes[0], 'expert', axis=0)]
    pallas_call x0 -> x2, Pallas kernels: none -> 45.3 us  [the longest x1 32.9 us: experts(): pl.pallas_call(expert_kernel, grid=(4,), in_specs=[pl.BlockSpec(memory_sp...]
    all_to_all x0 -> x3, waiting for transfers between devices: none -> 35.9 us  [the longest x1 17.5 us: local(): lax.all_to_all(small, ('expert', 'fsdp'), split_axis=0, concat_axis=0, ti...]
    all_to_all x2 -> x0, blocking collectives: 32.8 us -> none  [the longest x1 17.8 us: swap_fsdp(): return lax.all_to_all(v, 'fsdp', split_axis=0, concat_axis=0, tiled=True)]
    reduce_scatter x1, waiting for transfers between devices: 32.7 us -> 0.02 us  [local(): lax.psum_scatter(dnormed_part.astype(bf16).reshape(NF, LP, D), 'fsdp', sc...]
    reduce_scatter x2 -> x1, waiting for transfers between devices: 37.8 us -> 5.94 us  [local(): lax.psum_scatter(grad_exp.reshape(NF, LP, 3072), 'fsdp', scatter_dimensio...]
    ppermute x8 -> x0, starting transfers between devices: 23.6 us -> none  [the longest x6 12 us: shift_x(): return lax.ppermute(v, 'fsdp', [(i, (i + 2 * k) % NF) for i in range(NF)])]
  transfers between devices with their start and end apart: 66 -> 60, of which waited for: 21 -> 23; matrix products, arithmetic and copies ran while one was open for 33% -> 29% of each run, Pallas kernels for 0% -> 3%
where the time goes in v2:
time: 437 us; the launch traced here: 429 us
  waiting for transfers between devices  114 us (26%)
  starting transfers between devices  107 us (24%)
  local copies, waits for them, and re-layouts  72.7 us (17%)
  Pallas kernels  45.3 us (10%)
  other arithmetic  39.6 us (9%)
  matrix products  33.1 us (8%)
  between operations  16.4 us (4%)
    ppermute x24, starting transfers between devices, shift_z(): lax.ppermute(v, 'expert', [(i, i // 4 * 4 + (i + k) % 4) for i in range(N...  40.2 us
    ppermute x24, starting transfers between devices, shift_y(): return lax.ppermute(v, 'expert', [(i, (i + 4 * k) % NE) for i in range(NE)])  37.8 us
    ppermute x24, waiting for transfers between devices, shift_y(): return lax.ppermute(v, 'expert', [(i, (i + 4 * k) % NE) for i in range(NE)])  34.4 us
    pallas_call x1, Pallas kernels, experts(): pl.pallas_call(expert_kernel, grid=(4,), in_specs=[pl.BlockSpec(memory_sp...  32.9 us
    ppermute x24, waiting for transfers between devices, shift_z(): lax.ppermute(v, 'expert', [(i, i // 4 * 4 + (i + k) % 4) for i in range(N...  27.9 us
    all_to_all x1, waiting for transfers between devices, local(): lax.all_to_all(small, ('expert', 'fsdp'), split_axis=0, concat_axis=0, ti...  17.5 us
    dynamic_update_slice x30, local copies, waits for them, and re-layouts, put(): return lax.dynamic_update_index_in_dim(buffer, piece, place, 0)  15.6 us
    unnamed x162, local copies, waits for them, and re-layouts  15.3 us
  transfers between devices with their start and end apart: 60, of which 23 were waited for; matrix products, arithmetic and copies ran while one was open for 29% of the time, Pallas kernels for 3%

profile of v2, /device:TPU:0, one launch (start us, length us, event | category | flops | bytes accessed | tf_op | source)
XLA Modules:
  0.0 428.6 jit_solution(14628964611273064695)
XLA Ops:
  10.5 2.0 collective-permute-start.12
  12.5 2.1 collective-permute-start.13
  25.5 4.4 %all-to-all-start = ((bf16[8,160,256]{2,1,0:T(8,128)(2,1)}), bf16[8,160,256]{2,1,0:T(8,128)(2,1)S(1)}, u32[]{:S(2)}, u32[]{:S(2)}) async-start(bf16[8,160,256]{2,1,0:T(8,128)(2,1)} %pad_maximum_fusion.3), calls=%async_computation | async-start | bytes 1310720 | tf_op jit(solution)/shard_map/all_to_all | solution.py:247
  35.1 2.1 collective-permute-start.20
  39.8 2.6 collective-permute-start.16
  45.8 2.2 collective-permute-start.22
  51.1 1.9 bitcast_dynamic-update-slice_fusion.2
  55.4 13.3 %collective-permute-done.15 = bf16[4,72,1024]{2,1,0:T(8,128)(2,1)} collective-permute-done((bf16[4,72,1024]{2,1,0:T(8,128)(2,1)}, bf16[4,72,1024]{2,1,0:T(8,128)(2,1)}, u32[]{:S(2)}, u32[]{:S(2)}) %collective-permute-start.15) | collective-permute-done | bytes 589856 | tf_op jit(solution)/shard_map/ppermute | solution.py:38
  68.8 2.2 collective-permute-start.23
  74.4 1.9 bitcast_dynamic-update-slice_fusion.1
  76.3 1.9 bitcast_dynamic-update-slice_fusion
  78.3 2.6 collective-permute-done.23
  81.7 2.4 pad_maximum_fusion
  84.2 2.1 copy-done.7
  91.8 3.9 fusion.4
  95.7 2.1 fusion.10
  97.9 2.6 fusion.48
  102.1 5.4 %fusion.104 = (f32[2,1024]{1,0:T(2,128)S(1)}, f32[2,1024,1024]{1,2,0:T(8,128)}) fusion(pred[1024,1024]{0,1:T(8,128)(4,1)S(1)} %copy-done.21, bf16[1024,64,1]{0,1,2:T(8,128)(2,1)S(1)} %maximum_bitcast_fusion.1, bf16[1024,3,32]{0,2,1:T(8,128)(2,1)S(1)} %get-tuple-element.149, bf16[1024,3,32]{0,2,1:T(8,128)(2,1)S(1)} %get-tuple-element.148), kind=kOutput, calls=%fused_computation.256 | convolution fusion | flops 277349376 | bytes 9969664 | tf_op jit(solution)/shard_map/sub | solution.py:368
  107.5 4.4 %fusion.20 = bf16[64,2,1024]{2,0,1:T(8,128)(2,1)S(1)} fusion(f32[1024,256]{0,1:T(8,128)} %copy-done.25, f32[2,1024,1024]{1,2,0:T(8,128)} %get-tuple-element.179, f32[2,1024]{1,0:T(2,128)S(1)} %get-tuple-element.178), kind=kOutput, calls=%fused_computation.35 | convolution fusion | flops 272760832 | bytes 8790016 | tf_op jit(solution)/shard_map/hqk,kd->qhd/dot_general | solution.py:372
  113.4 4.4 %all-to-all-start.1 = ((bf16[8,128,128]{1,2,0:T(8,128)(2,1)}), bf16[8,128,128]{1,2,0:T(8,128)(2,1)}, u32[]{:S(2)}, u32[]{:S(2)}) async-start(bf16[8,128,128]{1,2,0:T(8,128)(2,1)} %copy.302), calls=%async_computation.1 | async-start | bytes 524288 | tf_op jit(solution)/shard_map/all_to_all | solution.py:247
  117.8 2.0 and_convert_fusion
  119.8 2.0 copy.329.pick
  128.8 2.2 collective-permute-start.1
  131.4 3.2 collective-permute-start.7
  137.6 3.2 collective-permute-start.4
  141.9 2.0 collective-permute-done.8
  144.4 2.8 collective-permute-start.10
  147.8 7.3 %collective-permute-done.3 = bf16[4,64,1024]{2,1,0:T(8,128)(2,1)S(1)} collective-permute-done((bf16[4,64,1024]{2,1,0:T(8,128)(2,1)S(1)}, bf16[4,64,1024]{2,1,0:T(8,128)(2,1)S(1)}, u32[]{:S(2)}, u32[]{:S(2)}) %collective-permute-start.3) | collective-permute-done | bytes 524320 | tf_op jit(solution)/shard_map/ppermute | solution.py:38
  155.1 2.8 collective-permute-start.11
  157.9 4.0 collective-permute-done.4
  163.6 3.4 collective-permute-done.11
  167.0 2.2 pad_maximum_fusion.1
  169.2 32.9 %experts.1 = (bf16[2,1024,1024]{2,1,0:T(8,128)(2,1)}, bf16[2,1024,512]{2,1,0:T(8,128)(2,1)}, bf16[2,1024,1024]{2,1,0:T(8,128)(2,1)}, bf16[2,1024,1024]{2,1,0:T(8...) custom-call(s32[1]{0:T(128)} %bitcast.16.e_ref, bf16[16,128,1024]{2,1,0:T(8,128)(2,1)} %bitcast.393, ...), custom_call_target="tpu_custom_call" | custom-call | flops 14000000000 | bytes 31457280 | tf_op jit(solution)/shard_map/experts/pallas_call | solution.py:182
  202.2 3.0 fusion.99
  207.8 3.2 collective-permute-start.37
  211.0 6.4 %collective-permute-start.38 = (bf16[4,64,1024]{2,1,0:T(8,128)(2,1)}, bf16[4,64,1024]{2,1,0:T(8,128)(2,1)}, u32[]{:S(2)}, u32[]{:S(2)}) collective-permute-start(bf16[4,64,1024]{2,1,0:T(8,128)(2,1)} %get-tuple-element.133), channel_id=1, source_target_pairs={{0,64},{8,72},{16,80},{24,88},{32,96},{40,104},{48,112},{56,120},{... | collective-permute-start | bytes 1572872 | tf_op jit(solution)/shard_map/ppermute | solution.py:38
  222.0 12.4 %expert_weights.1 = bf16[1024,3072]{1,0:T(8,128)(2,1)} custom-call(bf16[2,1024,1024]{2,1,0:T(8,128)(2,1)} %get-tuple-element.28.inputs, bf16[2,1024,1024]{2,1,0:T(8,128)(2,1)} %get-tuple-element.29.dres, bf16[2,1024,1024]{2,1,0:T(8,128)(2,1)} %get-tuple-element.30.dboth, bf16[2,1024,512]{2,1,0:T(8,128)(2,1)} %get-tuple-element.31.hidden), custom_call_target="tpu_custom_call" | custom-call | flops 7000000000 | bytes 20971520 | tf_op jit(solution)/shard_map/expert_weights/pallas_call | solution.py:227
  237.6 3.2 collective-permute-start.28
  243.3 8.6 %collective-permute-done.44 = bf16[4,64,1024]{2,1,0:T(8,128)(2,1)S(1)} collective-permute-done((bf16[4,64,1024]{2,1,0:T(8,128)(2,1)S(1)}, bf16[4,64,1024]{2,1,0:T(8,128)(2,1)S(1)}, u32[]{:S(2)}, u32[]{:S(2)}) %collective-permute-start.44) | collective-permute-done | bytes 524320 | tf_op jit(solution)/shard_map/ppermute | solution.py:34
  254.2 6.9 %collective-permute-done.27 = bf16[4,64,1152]{2,1,0:T(8,128)(2,1)S(1)} collective-permute-done((bf16[4,64,1152]{2,1,0:T(8,128)(2,1)S(1)}, bf16[4,64,1152]{2,1,0:T(8,128)(2,1)S(1)}, u32[]{:S(2)}, u32[]{:S(2)}) %collective-permute-start.27) | collective-permute-done | bytes 589856 | tf_op jit(solution)/shard_map/ppermute | solution.py:34
  261.1 2.3 collective-permute-start.26
  265.0 4.0 collective-permute-done.29
  269.0 3.1 collective-permute-start.40
  280.1 2.4 collective-permute-start.31
  284.8 2.7 collective-permute-start.34
  287.6 2.1 collective-permute-start.35
  291.8 2.6 collective-permute-done.35
  298.6 5.3 %all-to-all-start.2 = ((bf16[8,128,128]{2,1,0:T(8,128)(2,1)}), bf16[8,128,128]{2,1,0:T(8,128)(2,1)S(1)}, u32[]{:S(2)}, u32[]{:S(2)}) async-start(bf16[8,128,128]{2,1,0:T(8,128)(2,1)} %bitcast.381), calls=%async_computation.2 | async-start | bytes 524288 | tf_op jit(solution)/shard_map/all_to_all | solution.py:247
  304.9 6.5 %all-to-all-done.2 = bf16[8,128,128]{2,1,0:T(8,128)(2,1)S(1)} async-done(((bf16[8,128,128]{2,1,0:T(8,128)(2,1)}), bf16[8,128,128]{2,1,0:T(8,128)(2,1)S(1)}, u32[]{:S(2)}, u32[]{:S(2)}) %all-to-all-start.2) | async-done | bytes 262176 | tf_op jit(solution)/shard_map/all_to_all | solution.py:247
  311.8 4.9 %fusion.1 = (f32[2,1024]{1,0:T(2,128)S(1)}, f32[1024,1024,2]{1,0,2:T(8,128)S(1)}) fusion(f32[2,1024,1024]{1,2,0:T(8,128)} %get-tuple-element.179, f32[2,1024]{1,0:T(2,128)S(1)} %copy-done.49, bf16[1024,2,64]{0,2,1:T(8,128)(2,1)S(1)} %reshape.370, f32[1024,256]{0,1:T(8,128)} %copy-done.25), kind=kOutput, calls=%fused_computation.3 | convolution fusion | flops 274724864 | bytes 17186816 | tf_op jit(solution)/shard_map/qhd,kd->hqk/dot_general | solution.py:416
  316.7 4.9 %fusion.3 = bf16[2,1024,1024]{1,2,0:T(8,128)(2,1)S(1)} fusion(f32[1024,1024,2]{1,0,2:T(8,128)S(1)} %get-tuple-element.186, f32[2,1024]{1,0:T(2,128)S(1)} %get-tuple-element.185, f32[2,1024,1024]{1,2,0:T(8,128)} %get-tuple-element.179, f32[2,1024]{1,0:T(2,128)S(1)} %copy-done.49), kind=kLoop, calls=%fused_computation.5 | loop fusion | flops 8388608 | bytes 20987904 | tf_op jit(solution)/shard_map/convert_element_type | solution.py:418
  325.9 3.2 fusion.9
  329.1 8.6 %copy.347 = bf16[8,128,3072]{1,2,0:T(8,128)(2,1)} copy(bf16[8,128,3072]{2,1,0:T(8,128)(2,1)} %bitcast.387) | data formatting | bytes 12582912 | tf_op jit(solution)/shard_map/reshape | solution.py:386
  340.2 2.0 convolution_convert_fusion
  343.3 2.8 concatenate.90
  346.0 7.0 %all-to-all-start.3 = ((bf16[128,8,384]{2,1,0:T(8,128)(2,1)}), bf16[128,8,384]{2,1,0:T(8,128)(2,1)S(1)}, u32[]{:S(2)}, u32[]{:S(2)}) async-start(bf16[128,8,384]{2,1,0:T(8,128)(2,1)} %bitcast.134), calls=%async_computation.4 | async-start | bytes 1572864 | tf_op jit(solution)/shard_map/all_to_all | solution.py:454
  353.1 2.7 fusion.30
  355.9 17.5 %all-to-all-done.3 = bf16[128,8,384]{2,1,0:T(8,128)(2,1)S(1)} async-done(((bf16[128,8,384]{2,1,0:T(8,128)(2,1)}), bf16[128,8,384]{2,1,0:T(8,128)(2,1)S(1)}, u32[]{:S(2)}, u32[]{:S(2)}) %all-to-all-start.3) | async-done | bytes 786464 | tf_op jit(solution)/shard_map/all_to_all | solution.py:454
  373.4 3.5 all-to-all-start.4
  377.1 8.3 %all-to-all-done.4 = bf16[16,8,1024]{2,1,0:T(8,128)(2,1)S(1)} async-done(((bf16[16,8,1024]{2,1,0:T(8,128)(2,1)}), bf16[16,8,1024]{2,1,0:T(8,128)(2,1)S(1)}, u32[]{:S(2)}, u32[]{:S(2)}) %all-to-all-start.4) | async-done | bytes 262176 | tf_op jit(solution)/shard_map/all_to_all | solution.py:435
  386.4 3.8 all-to-all-start.5
  391.5 1.9 fusion.66
  393.4 10.0 %all-to-all-done.5 = bf16[16,8,3200]{2,1,0:T(8,128)(2,1)S(1)} async-done(((bf16[16,8,3200]{2,1,0:T(8,128)(2,1)}), bf16[16,8,3200]{2,1,0:T(8,128)(2,1)S(1)}, u32[]{:S(2)}, u32[]{:S(2)}) %all-to-all-start.5) | async-done | bytes 819232 | tf_op jit(solution)/shard_map/all_to_all | solution.py:464
  411.3 5.9 %reduce-scatter.5.cloned.1.call-done = bf16[1,128,3072]{1,2,0:T(8,128)(2,1)} async-done(((bf16[8,128,3072]{1,2,0:T(8,128)(2,1)}), bf16[1,128,3072]{1,2,0:T(8,128)(2,1)}) %reduce-scatter.5.cloned.1.call-update) | async-done | bytes 786448 | tf_op jit(solution)/shard_map/reduce_scatter | solution.py:385
  (400 shorter events, 113.6 us)
Async XLA Ops:
  7.2 66.0 %all-gather.6.cloned.1.call-start = ((), (), s32[]{:S(2)}) async-start(), calls=%async_computation.8 | async-start | bytes 2359296 | tf_op jit(solution)/shard_map/all_gather | solution.py:319
  10.5 24.6 %collective-permute-start.12 = (bf16[72,1024]{1,0:T(8,128)(2,1)S(1)}, bf16[72,1024]{1,0:T(8,128)(2,1)S(1)}, u32[]{:S(2)}, u32[]{:S(2)}) collective-permute-start(bf16[72,1024]{1,0:T(8,128)(2,1)S(1)} %get-tuple-element.167), channel_id=1, source_target_pairs={{0,8},{8,16},{16,24},{24,0},{32,40},{40,48},{48,56},{56,32},{64,72... | collective-permute-start | bytes 442376 | tf_op jit(solution)/shard_map/ppermute | solution.py:34
  12.5 25.3 %collective-permute-start.13 = (bf16[72,1024]{1,0:T(8,128)(2,1)S(1)}, bf16[72,1024]{1,0:T(8,128)(2,1)S(1)}, u32[]{:S(2)}, u32[]{:S(2)}) collective-permute-start(bf16[72,1024]{1,0:T(8,128)(2,1)S(1)} %get-tuple-element.167), channel_id=1, source_target_pairs={{0,24},{8,0},{16,8},{24,16},{32,56},{40,32},{48,40},{56,48},{64,88... | collective-permute-start | bytes 442376 | tf_op jit(solution)/shard_map/ppermute | solution.py:34
  14.6 23.9 %collective-permute-start.14 = (bf16[72,1024]{1,0:T(8,128)(2,1)S(1)}, bf16[72,1024]{1,0:T(8,128)(2,1)S(1)}, u32[]{:S(2)}, u32[]{:S(2)}) collective-permute-start(bf16[72,1024]{1,0:T(8,128)(2,1)S(1)} %get-tuple-element.167), channel_id=1, source_target_pairs={{0,16},{8,24},{16,0},{24,8},{32,48},{40,56},{48,32},{56,40},{64,80... | collective-permute-start | bytes 442376 | tf_op jit(solution)/shard_map/ppermute | solution.py:34
  20.0 22.4 %collective-permute-start.18 = (bf16[72,1024]{1,0:T(8,128)(2,1)S(1)}, bf16[72,1024]{1,0:T(8,128)(2,1)S(1)}, u32[]{:S(2)}, u32[]{:S(2)}) collective-permute-start(bf16[72,1024]{1,0:T(8,128)(2,1)S(1)} %get-tuple-element.119), channel_id=1, source_target_pairs={{0,32},{8,40},{16,48},{24,56},{32,64},{40,72},{48,80},{56,88},{64,... | collective-permute-start | bytes 442376 | tf_op jit(solution)/shard_map/ppermute | solution.py:38
  21.6 21.8 %collective-permute-start.19 = (bf16[72,1024]{1,0:T(8,128)(2,1)S(1)}, bf16[72,1024]{1,0:T(8,128)(2,1)S(1)}, u32[]{:S(2)}, u32[]{:S(2)}) collective-permute-start(bf16[72,1024]{1,0:T(8,128)(2,1)S(1)} %get-tuple-element.119), channel_id=1, source_target_pairs={{0,96},{8,104},{16,112},{24,120},{32,0},{40,8},{48,16},{56,24},{64... | collective-permute-start | bytes 442376 | tf_op jit(solution)/shard_map/ppermute | solution.py:38
  25.5 27.5 %all-to-all-start = ((bf16[8,160,256]{2,1,0:T(8,128)(2,1)}), bf16[8,160,256]{2,1,0:T(8,128)(2,1)S(1)}, u32[]{:S(2)}, u32[]{:S(2)}) async-start(bf16[8,160,256]{2,1,0:T(8,128)(2,1)} %pad_maximum_fusion.3), calls=%async_computation | async-start | bytes 1310720 | tf_op jit(solution)/shard_map/all_to_all | solution.py:247
  29.9 65.8 %all-gather.12.cloned.1.call-start = ((), (), s32[]{:S(2)}) async-start(), calls=%async_computation.13 | async-start | bytes 2359296 | tf_op jit(solution)/shard_map/all_gather | solution.py:313
  30.7 138.5 %all-gather.8.cloned.1.call-start = ((), (), s32[]{:S(2)}) async-start(), calls=%async_computation.9 | async-start | bytes 7077888 | tf_op jit(solution)/shard_map/all_gather | solution.py:323
  35.1 9.0 %collective-permute-start.20 = (bf16[72,1024]{1,0:T(8,128)(2,1)S(1)}, bf16[72,1024]{1,0:T(8,128)(2,1)S(1)}, u32[]{:S(2)}, u32[]{:S(2)}) collective-permute-start(bf16[72,1024]{1,0:T(8,128)(2,1)S(1)} %get-tuple-element.119), channel_id=1, source_target_pairs={{0,64},{8,72},{16,80},{24,88},{32,96},{40,104},{48,112},{56,120},{... | collective-permute-start | bytes 442376 | tf_op jit(solution)/shard_map/ppermute | solution.py:38
  39.2 29.6 %collective-permute-start.15 = (bf16[4,72,1024]{2,1,0:T(8,128)(2,1)}, bf16[4,72,1024]{2,1,0:T(8,128)(2,1)}, u32[]{:S(2)}, u32[]{:S(2)}) collective-permute-start(bf16[4,72,1024]{2,1,0:T(8,128)(2,1)} %bitcast_dynamic-update-slice_fusion.20), channel_id=1, source_target_pairs={{0,32},{8,40},{16,48},{24,56},{32,64},{40,72},{48,80},{56,88},{64,... | collective-permute-start | bytes 1769480 | tf_op jit(solution)/shard_map/ppermute | solution.py:38
  39.8 32.3 %collective-permute-start.16 = (bf16[4,72,1024]{2,1,0:T(8,128)(2,1)}, bf16[4,72,1024]{2,1,0:T(8,128)(2,1)}, u32[]{:S(2)}, u32[]{:S(2)}) collective-permute-start(bf16[4,72,1024]{2,1,0:T(8,128)(2,1)} %bitcast_dynamic-update-slice_fusion.20), channel_id=1, source_target_pairs={{0,96},{8,104},{16,112},{24,120},{32,0},{40,8},{48,16},{56,24},{64... | collective-permute-start | bytes 1769480 | tf_op jit(solution)/shard_map/ppermute | solution.py:38
  42.4 30.9 %collective-permute-start.17 = (bf16[4,72,1024]{2,1,0:T(8,128)(2,1)}, bf16[4,72,1024]{2,1,0:T(8,128)(2,1)}, u32[]{:S(2)}, u32[]{:S(2)}) collective-permute-start(bf16[4,72,1024]{2,1,0:T(8,128)(2,1)} %bitcast_dynamic-update-slice_fusion.20), channel_id=1, source_target_pairs={{0,64},{8,72},{16,80},{24,88},{32,96},{40,104},{48,112},{56,120},{... | collective-permute-start | bytes 1769480 | tf_op jit(solution)/shard_map/ppermute | solution.py:38
  44.7 29.7 %collective-permute-start.21 = (bf16[4,72,1024]{2,1,0:T(8,128)(2,1)}, bf16[4,72,1024]{2,1,0:T(8,128)(2,1)}, u32[]{:S(2)}, u32[]{:S(2)}) collective-permute-start(bf16[4,72,1024]{2,1,0:T(8,128)(2,1)} %bitcast_dynamic-update-slice_fusion.16), channel_id=1, source_target_pairs={{0,8},{8,16},{16,24},{24,0},{32,40},{40,48},{48,56},{56,32},{64,72... | collective-permute-start | bytes 1769480 | tf_op jit(solution)/shard_map/ppermute | solution.py:34
  45.8 30.6 %collective-permute-start.22 = (bf16[4,72,1024]{2,1,0:T(8,128)(2,1)}, bf16[4,72,1024]{2,1,0:T(8,128)(2,1)}, u32[]{:S(2)}, u32[]{:S(2)}) collective-permute-start(bf16[4,72,1024]{2,1,0:T(8,128)(2,1)} %bitcast_dynamic-update-slice_fusion.16), channel_id=1, source_target_pairs={{0,24},{8,0},{16,8},{24,16},{32,56},{40,32},{48,40},{56,48},{64,88... | collective-permute-start | bytes 1769480 | tf_op jit(solution)/shard_map/ppermute | solution.py:34
  68.8 12.1 %collective-permute-start.23 = (bf16[4,72,1024]{2,1,0:T(8,128)(2,1)}, bf16[4,72,1024]{2,1,0:T(8,128)(2,1)S(1)}, u32[]{:S(2)}, u32[]{:S(2)}) collective-permute-start(bf16[4,72,1024]{2,1,0:T(8,128)(2,1)} %bitcast_dynamic-update-slice_fusion.16), channel_id=1, source_target_pairs={{0,16},{8,24},{16,0},{24,8},{32,48},{40,56},{48,32},{56,40},{64,80... | collective-permute-start | bytes 1769480 | tf_op jit(solution)/shard_map/ppermute | solution.py:34
  113.4 12.1 %all-to-all-start.1 = ((bf16[8,128,128]{1,2,0:T(8,128)(2,1)}), bf16[8,128,128]{1,2,0:T(8,128)(2,1)}, u32[]{:S(2)}, u32[]{:S(2)}) async-start(bf16[8,128,128]{1,2,0:T(8,128)(2,1)} %copy.302), calls=%async_computation.1 | async-start | bytes 524288 | tf_op jit(solution)/shard_map/all_to_all | solution.py:247
  127.7 8.2 %collective-permute-start = (bf16[64,1024]{1,0:T(8,128)(2,1)S(1)}, bf16[64,1024]{1,0:T(8,128)(2,1)S(1)}, u32[]{:S(2)}, u32[]{:S(2)}) collective-permute-start(bf16[64,1024]{1,0:T(8,128)(2,1)S(1)} %get-tuple-element.169), channel_id=1, source_target_pairs={{0,8},{8,16},{16,24},{24,0},{32,40},{40,48},{48,56},{56,32},{64,72... | collective-permute-start | bytes 393224 | tf_op jit(solution)/shard_map/ppermute | solution.py:34
  128.8 7.2 %collective-permute-start.1 = (bf16[64,1024]{1,0:T(8,128)(2,1)S(1)}, bf16[64,1024]{1,0:T(8,128)(2,1)S(1)}, u32[]{:S(2)}, u32[]{:S(2)}) collective-permute-start(bf16[64,1024]{1,0:T(8,128)(2,1)S(1)} %get-tuple-element.169), channel_id=1, source_target_pairs={{0,24},{8,0},{16,8},{24,16},{32,56},{40,32},{48,40},{56,48},{64,88... | collective-permute-start | bytes 393224 | tf_op jit(solution)/shard_map/ppermute | solution.py:34
  131.0 6.5 %collective-permute-start.2 = (bf16[64,1024]{1,0:T(8,128)(2,1)S(1)}, bf16[64,1024]{1,0:T(8,128)(2,1)S(1)}, u32[]{:S(2)}, u32[]{:S(2)}) collective-permute-start(bf16[64,1024]{1,0:T(8,128)(2,1)S(1)} %get-tuple-element.169), channel_id=1, source_target_pairs={{0,16},{8,24},{16,0},{24,8},{32,48},{40,56},{48,32},{56,40},{64,80... | collective-permute-start | bytes 393224 | tf_op jit(solution)/shard_map/ppermute | solution.py:34
  131.4 9.4 %collective-permute-start.6 = (bf16[64,1024]{1,0:T(8,128)(2,1)S(1)}, bf16[64,1024]{1,0:T(8,128)(2,1)S(1)}, u32[]{:S(2)}, u32[]{:S(2)}) collective-permute-start(bf16[64,1024]{1,0:T(8,128)(2,1)S(1)} %get-tuple-element.170), channel_id=1, source_target_pairs={{0,32},{8,40},{16,48},{24,56},{32,64},{40,72},{48,80},{56,88},{64,... | collective-permute-start | bytes 393224 | tf_op jit(solution)/shard_map/ppermute | solution.py:38
  131.4 10.4 %collective-permute-start.7 = (bf16[64,1024]{1,0:T(8,128)(2,1)S(1)}, bf16[64,1024]{1,0:T(8,128)(2,1)S(1)}, u32[]{:S(2)}, u32[]{:S(2)}) collective-permute-start(bf16[64,1024]{1,0:T(8,128)(2,1)S(1)} %get-tuple-element.170), channel_id=1, source_target_pairs={{0,96},{8,104},{16,112},{24,120},{32,0},{40,8},{48,16},{56,24},{64... | collective-permute-start | bytes 393224 | tf_op jit(solution)/shard_map/ppermute | solution.py:38
  135.9 7.9 %collective-permute-start.8 = (bf16[64,1024]{1,0:T(8,128)(2,1)S(1)}, bf16[64,1024]{1,0:T(8,128)(2,1)S(1)}, u32[]{:S(2)}, u32[]{:S(2)}) collective-permute-start(bf16[64,1024]{1,0:T(8,128)(2,1)S(1)} %get-tuple-element.170), channel_id=1, source_target_pairs={{0,64},{8,72},{16,80},{24,88},{32,96},{40,104},{48,112},{56,120},{... | collective-permute-start | bytes 393224 | tf_op jit(solution)/shard_map/ppermute | solution.py:38
  137.5 17.6 %collective-permute-start.3 = (bf16[4,64,1024]{2,1,0:T(8,128)(2,1)S(1)}, bf16[4,64,1024]{2,1,0:T(8,128)(2,1)S(1)}, u32[]{:S(2)}, u32[]{:S(2)}) collective-permute-start(bf16[4,64,1024]{2,1,0:T(8,128)(2,1)S(1)} %bitcast_dynamic-update-slice_fusion.33), channel_id=1, source_target_pairs={{0,32},{8,40},{16,48},{24,56},{32,64},{40,72},{48,80},{56,88},{64,... | collective-permute-start | bytes 1572872 | tf_op jit(solution)/shard_map/ppermute | solution.py:38
  137.6 24.3 %collective-permute-start.4 = (bf16[4,64,1024]{2,1,0:T(8,128)(2,1)S(1)}, bf16[4,64,1024]{2,1,0:T(8,128)(2,1)S(1)}, u32[]{:S(2)}, u32[]{:S(2)}) collective-permute-start(bf16[4,64,1024]{2,1,0:T(8,128)(2,1)S(1)} %bitcast_dynamic-update-slice_fusion.33), channel_id=1, source_target_pairs={{0,96},{8,104},{16,112},{24,120},{32,0},{40,8},{48,16},{56,24},{64... | collective-permute-start | bytes 1572872 | tf_op jit(solution)/shard_map/ppermute | solution.py:38
  140.8 22.6 %collective-permute-start.5 = (bf16[4,64,1024]{2,1,0:T(8,128)(2,1)S(1)}, bf16[4,64,1024]{2,1,0:T(8,128)(2,1)S(1)}, u32[]{:S(2)}, u32[]{:S(2)}) collective-permute-start(bf16[4,64,1024]{2,1,0:T(8,128)(2,1)S(1)} %bitcast_dynamic-update-slice_fusion.33), channel_id=1, source_target_pairs={{0,64},{8,72},{16,80},{24,88},{32,96},{40,104},{48,112},{56,120},{... | collective-permute-start | bytes 1572872 | tf_op jit(solution)/shard_map/ppermute | solution.py:38
  143.9 19.5 %collective-permute-start.9 = (bf16[4,64,1024]{2,1,0:T(8,128)(2,1)S(1)}, bf16[4,64,1024]{2,1,0:T(8,128)(2,1)S(1)}, u32[]{:S(2)}, u32[]{:S(2)}) collective-permute-start(bf16[4,64,1024]{2,1,0:T(8,128)(2,1)S(1)} %bitcast_dynamic-update-slice_fusion.29), channel_id=1, source_target_pairs={{0,8},{8,16},{16,24},{24,0},{32,40},{40,48},{48,56},{56,32},{64,72... | collective-permute-start | bytes 1572872 | tf_op jit(solution)/shard_map/ppermute | solution.py:34
  144.4 19.1 %collective-permute-start.10 = (bf16[4,64,1024]{2,1,0:T(8,128)(2,1)S(1)}, bf16[4,64,1024]{2,1,0:T(8,128)(2,1)S(1)}, u32[]{:S(2)}, u32[]{:S(2)}) collective-permute-start(bf16[4,64,1024]{2,1,0:T(8,128)(2,1)S(1)} %bitcast_dynamic-update-slice_fusion.29), channel_id=1, source_target_pairs={{0,24},{8,0},{16,8},{24,16},{32,56},{40,32},{48,40},{56,48},{64,88... | collective-permute-start | bytes 1572872 | tf_op jit(solution)/shard_map/ppermute | solution.py:34
  155.1 11.8 %collective-permute-start.11 = (bf16[4,64,1024]{2,1,0:T(8,128)(2,1)S(1)}, bf16[4,64,1024]{2,1,0:T(8,128)(2,1)S(1)}, u32[]{:S(2)}, u32[]{:S(2)}) collective-permute-start(bf16[4,64,1024]{2,1,0:T(8,128)(2,1)S(1)} %bitcast_dynamic-update-slice_fusion.29), channel_id=1, source_target_pairs={{0,16},{8,24},{16,0},{24,8},{32,48},{40,56},{48,32},{56,40},{64,80... | collective-permute-start | bytes 1572872 | tf_op jit(solution)/shard_map/ppermute | solution.py:34
  207.8 26.8 %collective-permute-start.36 = (bf16[4,64,1024]{2,1,0:T(8,128)(2,1)}, bf16[4,64,1024]{2,1,0:T(8,128)(2,1)}, u32[]{:S(2)}, u32[]{:S(2)}) collective-permute-start(bf16[4,64,1024]{2,1,0:T(8,128)(2,1)} %get-tuple-element.132), channel_id=1, source_target_pairs={{0,32},{8,40},{16,48},{24,56},{32,64},{40,72},{48,80},{56,88},{64,... | collective-permute-start | bytes 1572872 | tf_op jit(solution)/shard_map/ppermute | solution.py:38
  207.8 29.7 %collective-permute-start.37 = (bf16[4,64,1024]{2,1,0:T(8,128)(2,1)}, bf16[4,64,1024]{2,1,0:T(8,128)(2,1)}, u32[]{:S(2)}, u32[]{:S(2)}) collective-permute-start(bf16[4,64,1024]{2,1,0:T(8,128)(2,1)} %get-tuple-element.134), channel_id=1, source_target_pairs={{0,96},{8,104},{16,112},{24,120},{32,0},{40,8},{48,16},{56,24},{64... | collective-permute-start | bytes 1572872 | tf_op jit(solution)/shard_map/ppermute | solution.py:38
  211.0 26.6 %collective-permute-start.38 = (bf16[4,64,1024]{2,1,0:T(8,128)(2,1)}, bf16[4,64,1024]{2,1,0:T(8,128)(2,1)}, u32[]{:S(2)}, u32[]{:S(2)}) collective-permute-start(bf16[4,64,1024]{2,1,0:T(8,128)(2,1)} %get-tuple-element.133), channel_id=1, source_target_pairs={{0,64},{8,72},{16,80},{24,88},{32,96},{40,104},{48,112},{56,120},{... | collective-permute-start | bytes 1572872 | tf_op jit(solution)/shard_map/ppermute | solution.py:38
  218.6 22.2 %collective-permute-start.42 = (bf16[4,64,1024]{2,1,0:T(8,128)(2,1)}, bf16[4,64,1024]{2,1,0:T(8,128)(2,1)}, u32[]{:S(2)}, u32[]{:S(2)}) collective-permute-start(bf16[4,64,1024]{2,1,0:T(8,128)(2,1)} %get-tuple-element.135), channel_id=1, source_target_pairs={{0,8},{8,16},{16,24},{24,0},{32,40},{40,48},{48,56},{56,32},{64,72... | collective-permute-start | bytes 1572872 | tf_op jit(solution)/shard_map/ppermute | solution.py:34
  220.3 22.9 %collective-permute-start.43 = (bf16[4,64,1024]{2,1,0:T(8,128)(2,1)}, bf16[4,64,1024]{2,1,0:T(8,128)(2,1)}, u32[]{:S(2)}, u32[]{:S(2)}) collective-permute-start(bf16[4,64,1024]{2,1,0:T(8,128)(2,1)} %get-tuple-element.136), channel_id=1, source_target_pairs={{0,24},{8,0},{16,8},{24,16},{32,56},{40,32},{48,40},{56,48},{64,88... | collective-permute-start | bytes 1572872 | tf_op jit(solution)/shard_map/ppermute | solution.py:34
  235.4 16.5 %collective-permute-start.44 = (bf16[4,64,1024]{2,1,0:T(8,128)(2,1)S(1)}, bf16[4,64,1024]{2,1,0:T(8,128)(2,1)S(1)}, u32[]{:S(2)}, u32[]{:S(2)}) collective-permute-start(bf16[4,64,1024]{2,1,0:T(8,128)(2,1)S(1)} %copy-done.26), channel_id=1, source_target_pairs={{0,16},{8,24},{16,0},{24,8},{32,48},{40,56},{48,32},{56,40},{64,80... | collective-permute-start | bytes 1572872 | tf_op jit(solution)/shard_map/ppermute | solution.py:34
  237.5 23.6 %collective-permute-start.27 = (bf16[4,64,1152]{2,1,0:T(8,128)(2,1)S(1)}, bf16[4,64,1152]{2,1,0:T(8,128)(2,1)S(1)}, u32[]{:S(2)}, u32[]{:S(2)}) collective-permute-start(bf16[4,64,1152]{2,1,0:T(8,128)(2,1)S(1)} %get-tuple-element.126), channel_id=1, source_target_pairs={{0,8},{8,16},{16,24},{24,0},{32,40},{40,48},{48,56},{56,32},{64,72... | collective-permute-start | bytes 1769480 | tf_op jit(solution)/shard_map/ppermute | solution.py:34
  237.6 25.8 %collective-permute-start.28 = (bf16[4,64,1152]{2,1,0:T(8,128)(2,1)S(1)}, bf16[4,64,1152]{2,1,0:T(8,128)(2,1)S(1)}, u32[]{:S(2)}, u32[]{:S(2)}) collective-permute-start(bf16[4,64,1152]{2,1,0:T(8,128)(2,1)S(1)} %get-tuple-element.127), channel_id=1, source_target_pairs={{0,24},{8,0},{16,8},{24,16},{32,56},{40,32},{48,40},{56,48},{64,88... | collective-permute-start | bytes 1769480 | tf_op jit(solution)/shard_map/ppermute | solution.py:34
  240.8 28.2 %collective-permute-start.29 = (bf16[4,64,1152]{2,1,0:T(8,128)(2,1)S(1)}, bf16[4,64,1152]{2,1,0:T(8,128)(2,1)S(1)}, u32[]{:S(2)}, u32[]{:S(2)}) collective-permute-start(bf16[4,64,1152]{2,1,0:T(8,128)(2,1)S(1)} %get-tuple-element.128), channel_id=1, source_target_pairs={{0,16},{8,24},{16,0},{24,8},{32,48},{40,56},{48,32},{56,40},{64,80... | collective-permute-start | bytes 1769480 | tf_op jit(solution)/shard_map/ppermute | solution.py:34
  243.2 29.2 %collective-permute-start.24 = (bf16[4,64,1152]{2,1,0:T(8,128)(2,1)S(1)}, bf16[4,64,1152]{2,1,0:T(8,128)(2,1)S(1)}, u32[]{:S(2)}, u32[]{:S(2)}) collective-permute-start(bf16[4,64,1152]{2,1,0:T(8,128)(2,1)S(1)} %get-tuple-element.129), channel_id=1, source_target_pairs={{0,32},{8,40},{16,48},{24,56},{32,64},{40,72},{48,80},{56,88},{64,... | collective-permute-start | bytes 1769480 | tf_op jit(solution)/shard_map/ppermute | solution.py:38
  251.9 21.1 %collective-permute-start.25 = (bf16[4,64,1152]{2,1,0:T(8,128)(2,1)S(1)}, bf16[4,64,1152]{2,1,0:T(8,128)(2,1)S(1)}, u32[]{:S(2)}, u32[]{:S(2)}) collective-permute-start(bf16[4,64,1152]{2,1,0:T(8,128)(2,1)S(1)} %get-tuple-element.131), channel_id=1, source_target_pairs={{0,96},{8,104},{16,112},{24,120},{32,0},{40,8},{48,16},{56,24},{64... | collective-permute-start | bytes 1769480 | tf_op jit(solution)/shard_map/ppermute | solution.py:38
  261.1 14.0 %collective-permute-start.26 = (bf16[4,64,1152]{2,1,0:T(8,128)(2,1)S(1)}, bf16[4,64,1152]{2,1,0:T(8,128)(2,1)S(1)}, u32[]{:S(2)}, u32[]{:S(2)}) collective-permute-start(bf16[4,64,1152]{2,1,0:T(8,128)(2,1)S(1)} %get-tuple-element.130), channel_id=1, source_target_pairs={{0,64},{8,72},{16,80},{24,88},{32,96},{40,104},{48,112},{56,120},{... | collective-permute-start | bytes 1769480 | tf_op jit(solution)/shard_map/ppermute | solution.py:38
  263.4 13.3 %collective-permute-start.39 = (bf16[64,1024]{1,0:T(8,128)(2,1)S(1)}, bf16[64,1024]{1,0:T(8,128)(2,1)S(1)}, u32[]{:S(2)}, u32[]{:S(2)}) collective-permute-start(bf16[64,1024]{1,0:T(8,128)(2,1)S(1)} %get-tuple-element.159), channel_id=1, source_target_pairs={{0,8},{8,16},{16,24},{24,0},{32,40},{40,48},{48,56},{56,32},{64,72... | collective-permute-start | bytes 393224 | tf_op jit(solution)/shard_map/ppermute | solution.py:34
  269.0 9.8 %collective-permute-start.40 = (bf16[64,1024]{1,0:T(8,128)(2,1)S(1)}, bf16[64,1024]{1,0:T(8,128)(2,1)S(1)}, u32[]{:S(2)}, u32[]{:S(2)}) collective-permute-start(bf16[64,1024]{1,0:T(8,128)(2,1)S(1)} %get-tuple-element.161), channel_id=1, source_target_pairs={{0,24},{8,0},{16,8},{24,16},{32,56},{40,32},{48,40},{56,48},{64,88... | collective-permute-start | bytes 393224 | tf_op jit(solution)/shard_map/ppermute | solution.py:34
  272.4 7.8 %collective-permute-start.41 = (bf16[64,1024]{1,0:T(8,128)(2,1)S(1)}, bf16[64,1024]{1,0:T(8,128)(2,1)S(1)}, u32[]{:S(2)}, u32[]{:S(2)}) collective-permute-start(bf16[64,1024]{1,0:T(8,128)(2,1)S(1)} %get-tuple-element.160), channel_id=1, source_target_pairs={{0,16},{8,24},{16,0},{24,8},{32,48},{40,56},{48,32},{56,40},{64,80... | collective-permute-start | bytes 393224 | tf_op jit(solution)/shard_map/ppermute | solution.py:34
  273.0 9.5 %collective-permute-start.45 = (bf16[64,1024]{1,0:T(8,128)(2,1)S(1)}, bf16[64,1024]{1,0:T(8,128)(2,1)S(1)}, u32[]{:S(2)}, u32[]{:S(2)}) collective-permute-start(bf16[64,1024]{1,0:T(8,128)(2,1)S(1)} %get-tuple-element.162), channel_id=1, source_target_pairs={{0,32},{8,40},{16,48},{24,56},{32,64},{40,72},{48,80},{56,88},{64,... | collective-permute-start | bytes 393224 | tf_op jit(solution)/shard_map/ppermute | solution.py:38
  275.1 9.2 %collective-permute-start.46 = (bf16[64,1024]{1,0:T(8,128)(2,1)S(1)}, bf16[64,1024]{1,0:T(8,128)(2,1)S(1)}, u32[]{:S(2)}, u32[]{:S(2)}) collective-permute-start(bf16[64,1024]{1,0:T(8,128)(2,1)S(1)} %get-tuple-element.164), channel_id=1, source_target_pairs={{0,96},{8,104},{16,112},{24,120},{32,0},{40,8},{48,16},{56,24},{64... | collective-permute-start | bytes 393224 | tf_op jit(solution)/shard_map/ppermute | solution.py:38
  276.7 18.0 %copy-start.43 = (f32[8,1,128]{2,1,0:T(1,128)S(1)}, f32[8,1,128]{2,1,0:T(1,128)}, u32[]{:S(2)}) copy-start(f32[8,1,128]{2,1,0:T(1,128)} %get-tuple-element.150) | copy-start | bytes 12292
  276.8 8.1 %collective-permute-start.47 = (bf16[64,1024]{1,0:T(8,128)(2,1)S(1)}, bf16[64,1024]{1,0:T(8,128)(2,1)S(1)}, u32[]{:S(2)}, u32[]{:S(2)}) collective-permute-start(bf16[64,1024]{1,0:T(8,128)(2,1)S(1)} %get-tuple-element.163), channel_id=1, source_target_pairs={{0,64},{8,72},{16,80},{24,88},{32,96},{40,104},{48,112},{56,120},{... | collective-permute-start | bytes 393224 | tf_op jit(solution)/shard_map/ppermute | solution.py:38
  278.8 8.8 %collective-permute-start.30 = (bf16[64,1152]{1,0:T(8,128)(2,1)S(1)}, bf16[64,1152]{1,0:T(8,128)(2,1)S(1)}, u32[]{:S(2)}, u32[]{:S(2)}) collective-permute-start(bf16[64,1152]{1,0:T(8,128)(2,1)S(1)} %get-tuple-element.155), channel_id=1, source_target_pairs={{0,8},{8,16},{16,24},{24,0},{32,40},{40,48},{48,56},{56,32},{64,72... | collective-permute-start | bytes 442376 | tf_op jit(solution)/shard_map/ppermute | solution.py:34
  280.1 9.6 %collective-permute-start.31 = (bf16[64,1152]{1,0:T(8,128)(2,1)S(1)}, bf16[64,1152]{1,0:T(8,128)(2,1)S(1)}, u32[]{:S(2)}, u32[]{:S(2)}) collective-permute-start(bf16[64,1152]{1,0:T(8,128)(2,1)S(1)} %get-tuple-element.157), channel_id=1, source_target_pairs={{0,24},{8,0},{16,8},{24,16},{32,56},{40,32},{48,40},{56,48},{64,88... | collective-permute-start | bytes 442376 | tf_op jit(solution)/shard_map/ppermute | solution.py:34
  282.6 7.1 %collective-permute-start.32 = (bf16[64,1152]{1,0:T(8,128)(2,1)S(1)}, bf16[64,1152]{1,0:T(8,128)(2,1)S(1)}, u32[]{:S(2)}, u32[]{:S(2)}) collective-permute-start(bf16[64,1152]{1,0:T(8,128)(2,1)S(1)} %get-tuple-element.156), channel_id=1, source_target_pairs={{0,16},{8,24},{16,0},{24,8},{32,48},{40,56},{48,32},{56,40},{64,80... | collective-permute-start | bytes 442376 | tf_op jit(solution)/shard_map/ppermute | solution.py:34
  284.3 6.4 %collective-permute-start.33 = (bf16[64,1152]{1,0:T(8,128)(2,1)S(1)}, bf16[64,1152]{1,0:T(8,128)(2,1)S(1)}, u32[]{:S(2)}, u32[]{:S(2)}) collective-permute-start(bf16[64,1152]{1,0:T(8,128)(2,1)S(1)} %get-tuple-element.152), channel_id=1, source_target_pairs={{0,32},{8,40},{16,48},{24,56},{32,64},{40,72},{48,80},{56,88},{64,... | collective-permute-start | bytes 442376 | tf_op jit(solution)/shard_map/ppermute | solution.py:38
  284.8 7.0 %collective-permute-start.34 = (bf16[64,1152]{1,0:T(8,128)(2,1)S(1)}, bf16[64,1152]{1,0:T(8,128)(2,1)S(1)}, u32[]{:S(2)}, u32[]{:S(2)}) collective-permute-start(bf16[64,1152]{1,0:T(8,128)(2,1)S(1)} %get-tuple-element.154), channel_id=1, source_target_pairs={{0,96},{8,104},{16,112},{24,120},{32,0},{40,8},{48,16},{56,24},{64... | collective-permute-start | bytes 442376 | tf_op jit(solution)/shard_map/ppermute | solution.py:38
  287.6 6.7 %collective-permute-start.35 = (bf16[64,1152]{1,0:T(8,128)(2,1)S(1)}, bf16[64,1152]{1,0:T(8,128)(2,1)S(1)}, u32[]{:S(2)}, u32[]{:S(2)}) collective-permute-start(bf16[64,1152]{1,0:T(8,128)(2,1)S(1)} %get-tuple-element.153), channel_id=1, source_target_pairs={{0,64},{8,72},{16,80},{24,88},{32,96},{40,104},{48,112},{56,120},{... | collective-permute-start | bytes 442376 | tf_op jit(solution)/shard_map/ppermute | solution.py:38
  298.6 12.9 %all-to-all-start.2 = ((bf16[8,128,128]{2,1,0:T(8,128)(2,1)}), bf16[8,128,128]{2,1,0:T(8,128)(2,1)S(1)}, u32[]{:S(2)}, u32[]{:S(2)}) async-start(bf16[8,128,128]{2,1,0:T(8,128)(2,1)} %bitcast.381), calls=%async_computation.2 | async-start | bytes 524288 | tf_op jit(solution)/shard_map/all_to_all | solution.py:247
  303.9 49.2 %all-gather.10.cloned.1.call-start = ((), (), s32[]{:S(2)}) async-start(), calls=%async_computation.11 | async-start | bytes 2359296 | tf_op jit(solution)/shard_map/all_gather | solution.py:410
  304.5 85.8 %reduce-scatter.3.cloned.1.call-start = ((), (), s32[]{:S(2)}) async-start(), calls=%async_computation.10 | async-start | bytes 2359296 | tf_op jit(solution)/shard_map/reduce_scatter | solution.py:428
  329.1 88.2 %reduce-scatter.5.cloned.1.call-start = ((), (), s32[]{:S(2)}) async-start(), calls=%async_computation.12 | async-start | bytes 7077888 | tf_op jit(solution)/shard_map/reduce_scatter | solution.py:385
  346.0 27.3 %all-to-all-start.3 = ((bf16[128,8,384]{2,1,0:T(8,128)(2,1)}), bf16[128,8,384]{2,1,0:T(8,128)(2,1)S(1)}, u32[]{:S(2)}, u32[]{:S(2)}) async-start(bf16[128,8,384]{2,1,0:T(8,128)(2,1)} %bitcast.134), calls=%async_computation.4 | async-start | bytes 1572864 | tf_op jit(solution)/shard_map/all_to_all | solution.py:454
  355.8 34.4 %copy-start.9 = (bf16[1,128,1024]{2,1,0:T(8,128)(2,1)S(1)}, bf16[1,128,1024]{2,1,0:T(8,128)(2,1)}, u32[]{:S(2)}) copy-start(bf16[1,128,1024]{2,1,0:T(8,128)(2,1)} %param.14) | copy-start | bytes 786436
  355.8 34.4 %copy-start.45 = (f32[8,1,128]{2,1,0:T(1,128)S(1)}, f32[8,1,128]{2,1,0:T(1,128)}, u32[]{:S(2)}) copy-start(f32[8,1,128]{2,1,0:T(1,128)} %get-tuple-element.151) | copy-start | bytes 12292
  355.9 35.6 %copy-start.12 = (f32[128,1024]{1,0:T(8,128)S(1)}, f32[128,1024]{1,0:T(8,128)}, u32[]{:S(2)}) copy-start(f32[128,1024]{1,0:T(8,128)} %get-tuple-element.115) | copy-start | bytes 1572868
  373.4 12.0 %all-to-all-start.4 = ((bf16[16,8,1024]{2,1,0:T(8,128)(2,1)}), bf16[16,8,1024]{2,1,0:T(8,128)(2,1)S(1)}, u32[]{:S(2)}, u32[]{:S(2)}) async-start(bf16[16,8,1024]{2,1,0:T(8,128)(2,1)} %fusion.30), calls=%async_computation.5 | async-start | bytes 524288 | tf_op jit(solution)/shard_map/all_to_all | solution.py:435
  386.4 17.1 %all-to-all-start.5 = ((bf16[16,8,3200]{2,1,0:T(8,128)(2,1)}), bf16[16,8,3200]{2,1,0:T(8,128)(2,1)S(1)}, u32[]{:S(2)}, u32[]{:S(2)}) async-start(bf16[16,8,3200]{2,1,0:T(8,128)(2,1)} %broadcast_in_dim.231), calls=%async_computation.6 | async-start | bytes 1638400 | tf_op jit(solution)/shard_map/all_to_all | solution.py:464
  (68 other events, 467.7 us)
Sparse Core Ops, SparseCore 0:
  9.8 30.0 all-gather.5
  41.6 28.8 all-gather.11
  73.4 39.9 all-gather.7
  306.7 25.6 all-gather.9
  334.6 38.3 reduce-scatter.2
  375.3 41.9 reduce-scatter.4
